TPU v7x, 512 devices: a whole 4x8x8 slice. The times are simulated.
512 devices in a mesh: dp: 8 (over z), vocab: 64 (over y, x, core).
Axes of the slice: x: 4, y: 8, z: 8, core: 2. Of those that a mesh axis runs over, the one named last changes fastest.
Arguments:
- hidden: bfloat16 [1024, 4096], P('dp'), may hold values from -200 to 200
- head_weight: bfloat16 [4096, 81920], P('dp', 'vocab'), may hold values from -0.25 to 0.25
- teacher_logprobs: bfloat16 [1024, 81920], P(('dp', 'vocab')), may hold values from -16 to 16
- lengths: int32 [16], P('dp'), may hold values from 8 to 64
- seq_weights: float32 [16], P('dp'), may hold values from 0.5 to 2
Outputs:
- grad_hidden: bfloat16 [1024, 4096], P('dp')
- grad_head: bfloat16 [4096, 81920], P('dp', 'vocab')
All inputs are finite; a program needn't handle non-finite values.
Results may differ from a plain program's by a relative error of at most 0.0065.
Values may be sent and summed in bfloat16 or wider, within the bound.
No kernel may reach another device: no remote copies, remote signals or barrier semaphores. Data moves between devices by JAX's collectives and lax.ppermute only.
A program may use at most 64 MiB of HBM per device.

v0:
```python
import jax
import jax.numpy as jnp
from jax import lax
from jax.sharding import PartitionSpec as P

SEQ_LEN = 64


loss_scale = 32.0


def sum_terms(partial_terms):
    return lax.psum(partial_terms, "vocab").astype(jnp.bfloat16)


def body(hidden, head_weight, teacher_logprobs, lengths, seq_weights):
    teacher = lax.all_to_all(
        teacher_logprobs, "vocab", split_axis=1, concat_axis=0, tiled=True
    ).astype(jnp.float32)
    tok_rows = hidden.shape[0]
    full_head = lax.all_gather(head_weight, "dp", axis=0, tiled=True)
    logits = jnp.dot(hidden, full_head, preferred_element_type=jnp.float32)
    local_top = jnp.max(logits, axis=1, keepdims=True)
    top = lax.pmax(local_top, "vocab")
    shifted = logits - top
    expd = jnp.exp(shifted)
    total, weighted = lax.psum(
        (
            jnp.sum(expd, axis=1, keepdims=True),
            jnp.sum(expd * (shifted - teacher), axis=1, keepdims=True),
        ),
        "vocab",
    )
    log_total = jnp.log(total)
    log_probs = logits - top - log_total
    probs = jnp.exp(log_probs)
    gap = log_probs - teacher
    divergence = weighted / total - log_total
    rows = jnp.arange(tok_rows, dtype=jnp.int32)
    sequence = rows // SEQ_LEN
    position = rows % SEQ_LEN
    member = sequence[:, None] == jnp.arange(lengths.shape[0], dtype=jnp.int32)[None, :]
    row_length = jnp.sum(jnp.where(member, lengths[None, :], 0), axis=1)
    row_weight = jnp.sum(jnp.where(member, seq_weights[None, :], jnp.float32(0.0)), axis=1)
    weight = jnp.where(position < row_length, row_weight, jnp.float32(0.0))
    grad_logits = (loss_scale * weight[:, None] * probs * (gap - divergence)).astype(jnp.bfloat16)
    slices = lax.all_to_all(hidden, "dp", split_axis=1, concat_axis=0, tiled=True)
    grad_head = lax.dot_general(
        slices,
        lax.all_gather(grad_logits, "dp", axis=0, tiled=True),
        (((0,), (0,)), ((), ())),
        preferred_element_type=jnp.float32,
    )
    partial_terms = lax.dot_general(
        grad_logits, full_head, (((1,), (1,)), ((), ())), preferred_element_type=jnp.float32
    )
    grad_hidden = sum_terms(partial_terms)
    return (grad_hidden, grad_head.astype(jnp.bfloat16))


def solution(mesh):
    placed = (P("dp", None), P("dp", "vocab"), P(("dp", "vocab"), None), P("dp"), P("dp"))
    return jax.shard_map(
        body,
        mesh=mesh,
        in_specs=placed,
        out_specs=(P("dp", None), P("dp", "vocab")),
        check_vma=False,
    )
```

profile of v0, /device:TPU:1, one launch (start us, length us, event | category | flops | bytes accessed | tf_op | source)
XLA Modules:
  0.0 718.3 jit_solution(8647506242621483257)
XLA Ops:
  7.2 0.0 copy-start
  7.2 0.0 all-gather.3.cloned.1.call-start
  7.2 0.7 all-gather.3.cloned.1.call-update
  7.9 11.6 %all-to-all-start = ((bf16[2,64,1280]{2,0,1:T(2,128)(2,1)}), bf16[2,64,1280]{2,0,1:T(2,128)(2,1)S(1)}, u32[]{:S(2)}, u32[]{:S(2)}) async-start(bf16[2,64,1280]{2,0,1:T(2,128)(2,1)} %bitcast.23), calls=%async_computation | async-start | bytes 655360 | tf_op jit(solution)/shard_map/all_to_all | solution.py:17
  19.5 0.0 all-gather.5.cloned.1.call-start
  19.6 0.7 select_reduce_fusion
  20.3 0.7 select_reduce_fusion.1
  21.1 12.6 %all-to-all-done = bf16[2,64,1280]{2,0,1:T(2,128)(2,1)S(1)} async-done(((bf16[2,64,1280]{2,0,1:T(2,128)(2,1)}), bf16[2,64,1280]{2,0,1:T(2,128)(2,1)S(1)}, u32[]{:S(2)}, u32[]{:S(2)}) %all-to-all-start) | async-done | bytes 327712 | tf_op jit(solution)/shard_map/all_to_all | solution.py:17
  33.7 0.2 convert_bitcast_fusion
  34.0 0.5 reshape.45
  34.4 98.4 %all-gather.3.cloned.1.call-done = bf16[4096,1280]{1,0:T(8,128)(2,1)} async-done(((bf16[512,1280]{1,0:T(8,128)(2,1)}), bf16[4096,1280]{1,0:T(8,128)(2,1)}) %all-gather.3.cloned.1.call-update) | async-done | bytes 10485776 | tf_op jit(solution)/shard_map/all_gather | solution.py:21
  132.8 0.0 copy-done
  132.9 5.6 fusion.2
  138.4 124.1 %pmax.7 = f32[128]{0:T(128)S(1)} all-reduce(f32[128]{0:T(128)S(1)} %get-tuple-element.16), channel_id=1, replica_groups=mesh['dp'=8,'vocab'=64] {'vocab'}, use_global_device_ids=true, to_apply=%region_3.0 | all-reduce | flops 128 | bytes 1024 | tf_op jit(solution)/shard_map/pmax | solution.py:24
  262.5 0.3 exponential_reduce_fusion
  262.8 128.4 %all-reduce = (f32[128,1]{0,1:T(1,128)S(1)}, f32[128,1]{0,1:T(1,128)S(1)}) all-reduce(f32[128,1]{0,1:T(1,128)S(1)} %bitcast.25, f32[128,1]{0,1:T(1,128)S(1)} %bitcast.24), channel_id=1, replica_groups=mesh['dp'=8,'vocab'=64] {'vocab'}, use_global_device_ids=true, to_apply=%region_7.8 | all-reduce | flops 256 | bytes 2048 | tf_op jit(solution)/shard_map/psum | solution.py:27
  391.3 1.0 multiply_convert_fusion
  392.3 0.0 all-gather.5.cloned.1.call-update
  392.3 0.7 copy.16
  393.0 0.0 copy-start.1
  393.0 40.8 %all_to_all.32 = bf16[128,8,512]{0,2,1:T(8,128)(2,1)S(1)} all-to-all(bf16[128,8,512]{0,2,1:T(8,128)(2,1)S(1)} %bitcast.21), channel_id=1, replica_groups=mesh['dp'=8,'vocab'=64] {'dp'}, dimensions={1} | all-to-all | bytes 2097152 | tf_op jit(solution)/shard_map/all_to_all | solution.py:47
  433.8 0.5 copy.17
  434.3 0.0 copy-done.1
  434.3 7.5 %fusion.3 = f32[128,4096]{1,0:T(8,128)S(1)} fusion(bf16[128,1280]{1,0:T(8,128)(2,1)S(1)} %copy-done.1, bf16[4096,1280]{1,0:T(8,128)(2,1)} %all-gather.3.cloned.1.call-done), kind=kOutput, calls=%fused_computation.19 | convolution fusion | flops 1342177280 | bytes 12910592 | tf_op jit(solution)/shard_map/dot_general | solution.py:54
  441.8 264.9 %all-reduce.2 = bf16[128,4096]{1,0:T(8,128)(2,1)} all-reduce(f32[128,4096]{1,0:T(8,128)S(1)} %fusion.3), channel_id=1, replica_groups=mesh['dp'=8,'vocab'=64] {'vocab'}, use_global_device_ids=true, to_apply=%region_8.9 | all-reduce | flops 524288 | bytes 3145728 | tf_op jit(solution)/shard_map/psum | solution.py:13
  706.8 0.0 all-gather.5.cloned.1.call-done
  706.8 3.3 fusion
  710.1 1.4 copy.18
  (3 shorter events, 0.0 us)
Async XLA Ops:
  7.2 125.7 %copy-start = (bf16[128,4096]{1,0:T(8,128)(2,1)S(1)}, bf16[128,4096]{1,0:T(8,128)(2,1)}, u32[]{:S(2)}) copy-start(bf16[128,4096]{1,0:T(8,128)(2,1)} %param.5) | copy-start | bytes 3145732
  7.2 125.7 %all-gather.3.cloned.1.call-start = ((), (), s32[]{:S(2)}) async-start(), calls=%async_computation.2 | async-start | bytes 11796480 | tf_op jit(solution)/shard_map/all_gather | solution.py:21
  7.9 25.8 %all-to-all-start = ((bf16[2,64,1280]{2,0,1:T(2,128)(2,1)}), bf16[2,64,1280]{2,0,1:T(2,128)(2,1)S(1)}, u32[]{:S(2)}, u32[]{:S(2)}) async-start(bf16[2,64,1280]{2,0,1:T(2,128)(2,1)} %bitcast.23), calls=%async_computation | async-start | bytes 655360 | tf_op jit(solution)/shard_map/all_to_all | solution.py:17
  19.5 687.2 %all-gather.5.cloned.1.call-start = ((), (), s32[]{:S(2)}) async-start(), calls=%async_computation.3 | async-start | bytes 2949120 | tf_op jit(solution)/shard_map/all_gather | solution.py:50
  393.0 41.3 %copy-start.1 = (bf16[128,1280]{1,0:T(8,128)(2,1)S(1)}, bf16[128,1280]{1,0:T(8,128)(2,1)}, u32[]{:S(2)}) copy-start(bf16[128,1280]{1,0:T(8,128)(2,1)} %multiply_convert_fusion) | copy-start | bytes 983044
Sparse Core Ops, SparseCore 0:
  10.1 122.7 all-gather.2
  392.5 55.9 all-gather.4
where the time goes:
time: 721 us; the launch traced here: 718 us
  blocking collectives  558 us (77%)
  waiting for transfers between devices  112 us (16%)
  matrix products  16.4 us (2%)
  between operations  14.1 us (2%)
  starting transfers between devices  11.7 us (2%)
    psum x1, blocking collectives, sum_terms(): return lax.psum(partial_terms, 'vocab').astype(jnp.bfloat16)  265 us
    psum x1, blocking collectives, body(): lax.psum((jnp.sum(expd, axis=1, keepdims=True), jnp.sum(expd * (shifted -...  128 us
    pmax x1, blocking collectives, body(): top = lax.pmax(local_top, 'vocab')  124 us
    all_gather x1, waiting for transfers between devices, body(): full_head = lax.all_gather(head_weight, 'dp', axis=0, tiled=True)  98.4 us
    all_to_all x1, blocking collectives, body(): lax.all_to_all(hidden, 'dp', split_axis=1, concat_axis=0, tiled=True)  40.8 us
  transfers between devices with their start and end apart: 3, of which 2 were waited for; matrix products, arithmetic and copies ran while one was open for 2% of the time, Pallas kernels for 0%

commit v1 on v0

v1 whole, which is shorter than its diff:
```python
import jax
import jax.numpy as jnp
from jax import lax
from jax.sharding import PartitionSpec as P

SEQ_LEN = 64
LOSS_SCALE = 32.0


def pair_groups(n):
    return [[2 * i, 2 * i + 1] for i in range(n // 2)]


def core_groups(n):
    return [[2 * i + c for i in range(n // 2)] for c in range(2)]


def spread(block, groups=None, size=None):
    copies = jnp.broadcast_to(block[None], (size,) + block.shape)
    return lax.all_to_all(copies, "vocab", 0, 0, axis_index_groups=groups)


def hidden_slice(hidden, n_dp, n_v):
    rows, d = hidden.shape
    share = rows // n_v
    mine = lax.dynamic_slice_in_dim(hidden, lax.axis_index("vocab") * share, share, 0)
    mine = mine.reshape(share, n_dp, d // n_dp).transpose(1, 0, 2)
    got = lax.all_to_all(mine, "dp", 0, 0)
    everyone = spread(got, None, n_v)
    return everyone.transpose(1, 0, 2, 3).reshape(n_dp * rows, d // n_dp)


def sum_terms(partial_terms, n_v):
    rows, d = partial_terms.shape
    half, many = d // 2, n_v // 2
    swapped = lax.all_to_all(
        partial_terms.reshape(rows, 2, half).transpose(1, 0, 2), "vocab", 0, 0,
        axis_index_groups=pair_groups(n_v),
    )
    mine = (swapped[0] + swapped[1]).astype(jnp.bfloat16)
    terms = lax.all_to_all(
        mine.reshape(many, rows // many, half), "vocab", 0, 0, axis_index_groups=core_groups(n_v)
    )
    total = jnp.sum(terms.astype(jnp.float32), axis=0).astype(jnp.bfloat16)
    whole = spread(total, core_groups(n_v), many).reshape(rows, half)
    both = spread(whole, pair_groups(n_v), 2)
    return jnp.concatenate([both[0], both[1]], axis=1)


def body(hidden, head_weight, teacher_logprobs, lengths, seq_weights):
    n_dp, n_v = lax.axis_size("dp"), lax.axis_size("vocab")
    full_head = lax.all_gather(head_weight, "dp", axis=0, tiled=True)
    teacher = lax.all_to_all(
        teacher_logprobs, "vocab", split_axis=1, concat_axis=0, tiled=True
    ).astype(jnp.float32)
    slices = hidden_slice(hidden, n_dp, n_v)
    tok_rows = hidden.shape[0]

    rows = jnp.arange(tok_rows, dtype=jnp.int32)
    sequence = rows // SEQ_LEN
    position = rows % SEQ_LEN
    member = sequence[:, None] == jnp.arange(lengths.shape[0], dtype=jnp.int32)[None, :]
    row_length = jnp.sum(jnp.where(member, lengths[None, :], 0), axis=1)
    row_weight = jnp.sum(jnp.where(member, seq_weights[None, :], jnp.float32(0.0)), axis=1)
    weight = jnp.where(position < row_length, row_weight, jnp.float32(0.0))

    logits = jnp.dot(hidden, full_head, preferred_element_type=jnp.float32)
    local_top = jnp.max(logits, axis=1)
    shifted = logits - local_top[:, None]
    expd = jnp.exp(shifted)
    diff = shifted - teacher
    stats = jnp.stack([local_top, jnp.sum(expd, axis=1), jnp.sum(expd * diff, axis=1)])
    every = spread(stats, None, n_v)
    tops, sums, weighteds = every[:, 0], every[:, 1], every[:, 2]
    top = jnp.max(tops, axis=0)
    lower = tops - top[None]
    scale = jnp.exp(lower)
    total = jnp.sum(sums * scale, axis=0)
    weighted = jnp.sum(scale * (weighteds + lower * sums), axis=0)
    own = local_top - top
    factor = LOSS_SCALE * weight * jnp.exp(own) / total
    centre = own - weighted / total
    grad_logits = (factor[:, None] * expd * (diff + centre[:, None])).astype(jnp.bfloat16)

    all_grads = lax.all_gather(grad_logits, "dp", axis=0, tiled=True)
    partial_terms = lax.dot_general(
        grad_logits, full_head, (((1,), (1,)), ((), ())), preferred_element_type=jnp.float32
    )
    grad_hidden = sum_terms(partial_terms, n_v)
    grad_head = lax.dot_general(
        slices, all_grads, (((0,), (0,)), ((), ())), preferred_element_type=jnp.float32
    )
    return grad_hidden, grad_head.astype(jnp.bfloat16)


def solution(mesh):
    placed = (P("dp", None), P("dp", "vocab"), P(("dp", "vocab"), None), P("dp"), P("dp"))
    return jax.shard_map(
        body,
        mesh=mesh,
        in_specs=placed,
        out_specs=(P("dp", None), P("dp", "vocab")),
        check_vma=False,
    )
```

time: 721 us -> 286 us (0.40)
  blocking collectives: 558 us -> 12.9 us
  waiting for transfers between devices: 112 us -> 184 us
  starting transfers between devices: 11.7 us -> 43.6 us
    psum x2 -> x0, blocking collectives: 393 us -> none  [the longest x1 265 us: sum_terms(): return lax.psum(partial_terms, 'vocab').astype(jnp.bfloat16)]
    pmax x1 -> x0, blocking collectives: 124 us -> none  [body(): top = lax.pmax(local_top, 'vocab')]
    all_to_all x0 -> x5, waiting for transfers between devices: none -> 70.9 us  [the longest x3 53 us: spread(): return lax.all_to_all(copies, 'vocab', 0, 0, axis_index_groups=groups)]
    all_to_all x0 -> x5, starting transfers between devices: none -> 31.9 us  [the longest x3 24.1 us: spread(): return lax.all_to_all(copies, 'vocab', 0, 0, axis_index_groups=groups)]
    all_to_all x1 -> x2, blocking collectives: 40.8 us -> 12.9 us  [the longest x1 7.49 us: spread(): return lax.all_to_all(copies, 'vocab', 0, 0, axis_index_groups=groups)]
  transfers between devices with their start and end apart: 3 -> 8, of which waited for: 2 -> 7; matrix products, arithmetic and copies ran while one was open for 2% -> 4% of each run, Pallas kernels for 0% -> 0%
where the time goes in v1:
time: 286 us; the launch traced here: 285 us
  waiting for transfers between devices  184 us (64%)
  starting transfers between devices  43.6 us (15%)
  matrix products  17.5 us (6%)
  between operations  14.2 us (5%)
  blocking collectives  12.9 us (5%)
  local copies, waits for them, and re-layouts  9.62 us (3%)
  other arithmetic  3.27 us (1%)
    all_gather x1, waiting for transfers between devices, body(): full_head = lax.all_gather(head_weight, 'dp', axis=0, tiled=True)  98.4 us
    all_to_all x3, waiting for transfers between devices, spread(): return lax.all_to_all(copies, 'vocab', 0, 0, axis_index_groups=groups)  53 us
    all_to_all x3, starting transfers between devices, spread(): return lax.all_to_all(copies, 'vocab', 0, 0, axis_index_groups=groups)  24.1 us
    all_to_all x1, waiting for transfers between devices, sum_terms(): lax.all_to_all(mine.reshape(many, rows // many, half), 'vocab', 0, 0, axi...  14.3 us
    all_to_all x1, waiting for transfers between devices, body(): lax.all_to_all(teacher_logprobs, 'vocab', split_axis=1, concat_axis=0, ti...  13.5 us
    all_to_all x1, starting transfers between devices, body(): lax.all_to_all(teacher_logprobs, 'vocab', split_axis=1, concat_axis=0, ti...  11.6 us
    dot_general x1, matrix products, body(): lax.dot_general(grad_logits, full_head, (((1,), (1,)), ((), ())), preferr...  7.55 us
    all_to_all x1, blocking collectives, spread(): return lax.all_to_all(copies, 'vocab', 0, 0, axis_index_groups=groups)  7.49 us
  transfers between devices with their start and end apart: 8, of which 7 were waited for; matrix products, arithmetic and copies ran while one was open for 4% of the time, Pallas kernels for 0%

profile of v1, /device:TPU:1, one launch (start us, length us, event | category | flops | bytes accessed | tf_op | source)
XLA Modules:
  0.0 285.3 jit_solution(5706273965240571309)
XLA Ops:
  7.2 0.0 copy-start
  7.2 0.0 all-gather.3.cloned.1.call-start
  7.2 0.7 all-gather.3.cloned.1.call-update
  7.9 11.6 %all-to-all-start = ((bf16[2,64,1280]{2,0,1:T(2,128)(2,1)}), bf16[2,64,1280]{2,0,1:T(2,128)(2,1)S(1)}, u32[]{:S(2)}, u32[]{:S(2)}) async-start(bf16[2,64,1280]{2,0,1:T(2,128)(2,1)} %bitcast.37), calls=%async_computation | async-start | bytes 655360 | tf_op jit(solution)/shard_map/all_to_all | solution.py:53
  19.6 0.0 copy-done
  19.6 0.6 constant_dynamic-slice_fusion
  20.2 13.5 %all-to-all-done = bf16[2,64,1280]{2,0,1:T(2,128)(2,1)S(1)} async-done(((bf16[2,64,1280]{2,0,1:T(2,128)(2,1)}), bf16[2,64,1280]{2,0,1:T(2,128)(2,1)S(1)}, u32[]{:S(2)}, u32[]{:S(2)}) %all-to-all-start) | async-done | bytes 327712 | tf_op jit(solution)/shard_map/all_to_all | solution.py:53
  33.7 0.2 convert_bitcast_fusion
  34.0 0.5 reshape.83
  34.4 0.0 copy-start.2
  34.4 0.0 copy-start.3
  34.4 98.4 %all-gather.3.cloned.1.call-done = bf16[4096,1280]{1,0:T(8,128)(2,1)} async-done(((bf16[512,1280]{1,0:T(8,128)(2,1)}), bf16[4096,1280]{1,0:T(8,128)(2,1)}) %all-gather.3.cloned.1.call-update) | async-done | bytes 10485776 | tf_op jit(solution)/shard_map/all_gather | solution.py:52
  132.9 5.6 %fusion.3 = (f32[128]{0:T(128)S(1)}, f32[128,1280]{1,0:T(8,128)S(1)}) fusion(bf16[128,4096]{1,0:T(8,128)(2,1)S(1)} %copy-done, bf16[4096,1280]{1,0:T(8,128)(2,1)} %all-gather.3.cloned.1.call-done), kind=kOutput, calls=%fused_computation.29 | convolution fusion | flops 1342340992 | bytes 12190208 | tf_op jit(solution)/shard_map/dot_general | solution.py:67
  138.4 0.3 fusion.1
  138.8 0.7 broadcast_in_dim.66
  139.4 10.4 %all-to-all-start.1 = ((f32[64,3,128]{2,1,0:T(4,128)}), f32[64,3,128]{2,1,0:T(4,128)S(1)}, u32[]{:S(2)}, u32[]{:S(2)}) async-start(f32[64,3,128]{2,1,0:T(4,128)} %broadcast_in_dim.66), calls=%async_computation.1 | async-start | bytes 262144 | tf_op jit(solution)/shard_map/all_to_all | solution.py:20
  149.8 0.1 select_reduce_fusion
  149.9 0.1 select_reduce_fusion.1
  150.0 10.9 %all-to-all-done.1 = f32[64,3,128]{2,1,0:T(4,128)S(1)} async-done(((f32[64,3,128]{2,1,0:T(4,128)}), f32[64,3,128]{2,1,0:T(4,128)S(1)}, u32[]{:S(2)}, u32[]{:S(2)}) %all-to-all-start.1) | async-done | bytes 98336 | tf_op jit(solution)/shard_map/all_to_all | solution.py:20
  160.9 0.1 fusion.2
  161.1 0.3 multiply_convert_fusion
  161.4 0.0 copy-start.1
  161.4 7.6 %fusion.4 = f32[128,4096]{1,0:T(8,128)S(1)} fusion(bf16[128,1280]{1,0:T(8,128)(2,1)S(1)} %multiply_convert_fusion, bf16[4096,1280]{1,0:T(8,128)(2,1)} %all-gather.3.cloned.1.call-done), kind=kOutput, calls=%fused_computation.30 | convolution fusion | flops 1342177280 | bytes 12910592 | tf_op jit(solution)/shard_map/dot_general | solution.py:86
  169.0 0.2 copy.31
  169.2 5.4 %all_to_all.48 = f32[2,128,2048]{2,1,0:T(8,128)S(1)} all-to-all(f32[2,128,2048]{2,1,0:T(8,128)S(1)} %bitcast.35), channel_id=1, replica_groups={{0,1},{2,3},{4,5},{6,7},{8,9},{10,11},{12,13},{14,15},{16,17},{18,19},{..., dimensions={0} | all-to-all | bytes 4194304 | tf_op jit(solution)/shard_map/all_to_all | solution.py:36
  174.6 3.8 %all-to-all-start.6 = ((bf16[8,2,512]{2,1,0:T(2,128)(2,1)}), bf16[8,2,512]{2,1,0:T(2,128)(2,1)S(1)}, u32[]{:S(2)}, u32[]{:S(2)}) async-start(bf16[8,2,512]{2,1,0:T(2,128)(2,1)} %bitcast.12), calls=%async_computation.6 | async-start | bytes 32768 | tf_op jit(solution)/shard_map/all_to_all | solution.py:28
  178.5 0.9 fusion
  179.4 2.0 convert_element_type.29
  181.4 3.7 %all-to-all-done.6 = bf16[8,2,512]{2,1,0:T(2,128)(2,1)S(1)} async-done(((bf16[8,2,512]{2,1,0:T(2,128)(2,1)}), bf16[8,2,512]{2,1,0:T(2,128)(2,1)S(1)}, u32[]{:S(2)}, u32[]{:S(2)}) %all-to-all-start.6) | async-done | bytes 16416 | tf_op jit(solution)/shard_map/all_to_all | solution.py:28
  185.1 3.9 %all-to-all-start.3 = ((bf16[32,4,2048]{2,1,0:T(4,128)(2,1)}), bf16[32,4,2048]{2,1,0:T(4,128)(2,1)S(1)}, u32[]{:S(2)}, u32[]{:S(2)}) async-start(bf16[32,4,2048]{2,1,0:T(4,128)(2,1)} %convert_element_type.29), calls=%async_computation.3 | async-start | bytes 1048576 | tf_op jit(solution)/shard_map/all_to_all | solution.py:41
  189.0 0.0 all-gather.5.cloned.1.call-start
  189.0 0.7 all-gather.5.cloned.1.call-update
  189.7 14.3 %all-to-all-done.3 = bf16[32,4,2048]{2,1,0:T(4,128)(2,1)S(1)} async-done(((bf16[32,4,2048]{2,1,0:T(4,128)(2,1)}), bf16[32,4,2048]{2,1,0:T(4,128)(2,1)S(1)}, u32[]{:S(2)}, u32[]{:S(2)}) %all-to-all-start.3) | async-done | bytes 524320 | tf_op jit(solution)/shard_map/all_to_all | solution.py:41
  204.0 2.0 broadcast_in_dim.70
  206.0 8.5 %all-to-all-start.7 = ((bf16[64,8,2,512]{3,2,1,0:T(2,128)(2,1)}), bf16[64,8,2,512]{3,2,1,0:T(2,128)(2,1)S(1)}, u32[]{:S(2)}, u32[]{:S(2)}) async-start(bf16[64,8,2,512]{3,2,1,0:T(2,128)(2,1)} %broadcast_in_dim.70), calls=%async_computation.7 | async-start | bytes 2097152 | tf_op jit(solution)/shard_map/all_to_all | solution.py:20
  214.5 0.2 reduce_sum.72
  214.7 27.8 %all-to-all-done.7 = bf16[64,8,2,512]{3,2,1,0:T(2,128)(2,1)S(1)} async-done(((bf16[64,8,2,512]{3,2,1,0:T(2,128)(2,1)}), bf16[64,8,2,512]{3,2,1,0:T(2,128)(2,1)S(1)}, u32[]{:S(2)}, u32[]{:S(2)}) %all-to-all-start.7) | async-done | bytes 1048608 | tf_op jit(solution)/shard_map/all_to_all | solution.py:20
  242.5 1.0 broadcast_in_dim.67
  243.5 5.3 %all-to-all-start.4 = ((bf16[32,4,2048]{2,1,0:T(4,128)(2,1)}), bf16[32,4,2048]{2,1,0:T(4,128)(2,1)}, u32[]{:S(2)}, u32[]{:S(2)}) async-start(bf16[32,4,2048]{2,1,0:T(4,128)(2,1)} %broadcast_in_dim.67), calls=%async_computation.4 | async-start | bytes 1048576 | tf_op jit(solution)/shard_map/all_to_all | solution.py:20
  248.8 0.7 copy.26
  249.5 0.4 reshape.82
  250.0 14.3 %all-to-all-done.4 = bf16[32,4,2048]{2,1,0:T(4,128)(2,1)} async-done(((bf16[32,4,2048]{2,1,0:T(4,128)(2,1)}), bf16[32,4,2048]{2,1,0:T(4,128)(2,1)}, u32[]{:S(2)}, u32[]{:S(2)}) %all-to-all-start.4) | async-done | bytes 524320 | tf_op jit(solution)/shard_map/all_to_all | solution.py:20
  264.2 1.2 broadcast_in_dim.68
  265.4 0.1 broadcast_in_dim.69
  265.5 7.5 %all_to_all.49 = bf16[2,128,2048]{2,1,0:T(8,128)(2,1)S(1)} all-to-all(bf16[2,128,2048]{2,1,0:T(8,128)(2,1)S(1)} %broadcast_in_dim.69), channel_id=1, replica_groups={{0,1},{2,3},{4,5},{6,7},{8,9},{10,11},{12,13},{14,15},{16,17},{18,19},{..., dimensions={0} | all-to-all | bytes 2097152 | tf_op jit(solution)/shard_map/all_to_all | solution.py:20
  273.0 0.1 slice_bitcast_fusion.1
  273.1 1.1 pad_maximum_fusion
  274.1 4.4 %convolution_convert_fusion = bf16[512,1280]{1,0:T(8,128)(2,1)} fusion(bf16[1024,512]{1,0:T(8,128)(2,1)S(1)} %reshape.82, bf16[1024,1280]{1,0:T(8,128)(2,1)} %all-gather.5.cloned.1.call-done), kind=kOutput, calls=%fused_computation | convolution fusion | flops 1342832640 | bytes 4980736 | tf_op jit(solution)/shard_map/dot_general | solution.py:90
  (9 shorter events, 0.1 us)
Async XLA Ops:
  7.2 12.4 %copy-start = (bf16[128,4096]{1,0:T(8,128)(2,1)S(1)}, bf16[128,4096]{1,0:T(8,128)(2,1)}, u32[]{:S(2)}) copy-start(bf16[128,4096]{1,0:T(8,128)(2,1)} %param.5) | copy-start | bytes 3145732
  7.2 125.7 %all-gather.3.cloned.1.call-start = ((), (), s32[]{:S(2)}) async-start(), calls=%async_computation.8 | async-start | bytes 11796480 | tf_op jit(solution)/shard_map/all_gather | solution.py:52
  7.9 25.8 %all-to-all-start = ((bf16[2,64,1280]{2,0,1:T(2,128)(2,1)}), bf16[2,64,1280]{2,0,1:T(2,128)(2,1)S(1)}, u32[]{:S(2)}, u32[]{:S(2)}) async-start(bf16[2,64,1280]{2,0,1:T(2,128)(2,1)} %bitcast.37), calls=%async_computation | async-start | bytes 655360 | tf_op jit(solution)/shard_map/all_to_all | solution.py:53
  34.4 115.4 %copy-start.2 = (f32[2]{0:T(128)S(1)}, f32[2]{0:T(128)}, u32[]{:S(2)}) copy-start(f32[2]{0:T(128)} %param.9) | copy-start | bytes 28
  34.4 115.5 %copy-start.3 = (s32[2]{0:T(128)S(1)}, s32[2]{0:T(128)}, u32[]{:S(2)}) copy-start(s32[2]{0:T(128)} %param.8) | copy-start | bytes 28
  139.4 21.5 %all-to-all-start.1 = ((f32[64,3,128]{2,1,0:T(4,128)}), f32[64,3,128]{2,1,0:T(4,128)S(1)}, u32[]{:S(2)}, u32[]{:S(2)}) async-start(f32[64,3,128]{2,1,0:T(4,128)} %broadcast_in_dim.66), calls=%async_computation.1 | async-start | bytes 262144 | tf_op jit(solution)/shard_map/all_to_all | solution.py:20
  161.4 7.6 %copy-start.1 = (bf16[128,1280]{1,0:T(8,128)(2,1)}, bf16[128,1280]{1,0:T(8,128)(2,1)S(1)}, u32[]{:S(2)}) copy-start(bf16[128,1280]{1,0:T(8,128)(2,1)S(1)} %multiply_convert_fusion) | copy-start | bytes 983044
  174.6 10.5 %all-to-all-start.6 = ((bf16[8,2,512]{2,1,0:T(2,128)(2,1)}), bf16[8,2,512]{2,1,0:T(2,128)(2,1)S(1)}, u32[]{:S(2)}, u32[]{:S(2)}) async-start(bf16[8,2,512]{2,1,0:T(2,128)(2,1)} %bitcast.12), calls=%async_computation.6 | async-start | bytes 32768 | tf_op jit(solution)/shard_map/all_to_all | solution.py:28
  185.1 18.9 %all-to-all-start.3 = ((bf16[32,4,2048]{2,1,0:T(4,128)(2,1)}), bf16[32,4,2048]{2,1,0:T(4,128)(2,1)S(1)}, u32[]{:S(2)}, u32[]{:S(2)}) async-start(bf16[32,4,2048]{2,1,0:T(4,128)(2,1)} %convert_element_type.29), calls=%async_computation.3 | async-start | bytes 1048576 | tf_op jit(solution)/shard_map/all_to_all | solution.py:41
  189.0 85.2 %all-gather.5.cloned.1.call-start = ((), (), s32[]{:S(2)}) async-start(), calls=%async_computation.9 | async-start | bytes 2949120 | tf_op jit(solution)/shard_map/all_gather | solution.py:85
  206.0 36.5 %all-to-all-start.7 = ((bf16[64,8,2,512]{3,2,1,0:T(2,128)(2,1)}), bf16[64,8,2,512]{3,2,1,0:T(2,128)(2,1)S(1)}, u32[]{:S(2)}, u32[]{:S(2)}) async-start(bf16[64,8,2,512]{3,2,1,0:T(2,128)(2,1)} %broadcast_in_dim.70), calls=%async_computation.7 | async-start | bytes 2097152 | tf_op jit(solution)/shard_map/all_to_all | solution.py:20
  243.5 20.7 %all-to-all-start.4 = ((bf16[32,4,2048]{2,1,0:T(4,128)(2,1)}), bf16[32,4,2048]{2,1,0:T(4,128)(2,1)}, u32[]{:S(2)}, u32[]{:S(2)}) async-start(bf16[32,4,2048]{2,1,0:T(4,128)(2,1)} %broadcast_in_dim.67), calls=%async_computation.4 | async-start | bytes 1048576 | tf_op jit(solution)/shard_map/all_to_all | solution.py:20
Sparse Core Ops, SparseCore 0:
  10.1 122.7 all-gather.2
  191.9 40.1 all-gather.4

commit v2 on v1

--- a/solution.py
+++ b/solution.py
@@ -30,7 +30,27 @@
     return everyone.transpose(1, 0, 2, 3).reshape(n_dp * rows, d // n_dp)
 
 
-def sum_terms(partial_terms, n_v):
+def ring_blocks(block, n):
+    right = [(i, (i + 1) % n) for i in range(n)]
+    left = [(i, (i - 1) % n) for i in range(n)]
+    half = block.shape[0] // 2
+    parts = [block[:half], block[half:]]
+    got = {0: list(parts)}
+    up, down = list(parts), list(parts)
+    for step in range(1, n // 2 + 1):
+        last = step == n // 2
+        down[0] = lax.ppermute(down[0], "dp", left)
+        up[1] = lax.ppermute(up[1], "dp", right)
+        if not last:
+            down[1] = lax.ppermute(down[1], "dp", left)
+            up[0] = lax.ppermute(up[0], "dp", right)
+            got[step], got[n - step] = list(down), list(up)
+        else:
+            got[step] = [down[0], up[1]]
+    return [got[k] for k in range(n)]
+
+
+def sum_terms(partial_terms, n_v, other):
     rows, d = partial_terms.shape
     half, many = d // 2, n_v // 2
     swapped = lax.all_to_all(
@@ -43,13 +63,14 @@
     )
     total = jnp.sum(terms.astype(jnp.float32), axis=0).astype(jnp.bfloat16)
     whole = spread(total, core_groups(n_v), many).reshape(rows, half)
+    whole, other = lax.optimization_barrier((whole, other))
     both = spread(whole, pair_groups(n_v), 2)
-    return jnp.concatenate([both[0], both[1]], axis=1)
+    return jnp.concatenate([both[0], both[1]], axis=1), other
 
 
 def body(hidden, head_weight, teacher_logprobs, lengths, seq_weights):
     n_dp, n_v = lax.axis_size("dp"), lax.axis_size("vocab")
-    full_head = lax.all_gather(head_weight, "dp", axis=0, tiled=True)
+    blocks = ring_blocks(head_weight, n_dp)
     teacher = lax.all_to_all(
         teacher_logprobs, "vocab", split_axis=1, concat_axis=0, tiled=True
     ).astype(jnp.float32)
@@ -64,7 +85,21 @@
     row_weight = jnp.sum(jnp.where(member, seq_weights[None, :], jnp.float32(0.0)), axis=1)
     weight = jnp.where(position < row_length, row_weight, jnp.float32(0.0))
 
-    logits = jnp.dot(hidden, full_head, preferred_element_type=jnp.float32)
+    me = lax.axis_index("dp")
+    depth = head_weight.shape[0]
+    part = depth // 2
+    logits = None
+    order = [0]
+    for k in range(1, n_dp // 2 + 1):
+        order += [k] if k == n_dp - k else [k, n_dp - k]
+    for k in order:
+        if k == n_dp // 2:
+            blocks[k][0], slices = lax.optimization_barrier((blocks[k][0], slices))
+        place = lax.rem(me + k, n_dp) * depth
+        for i in range(2):
+            feats = lax.dynamic_slice_in_dim(hidden, place + i * part, part, 1)
+            term = jnp.dot(feats, blocks[k][i], preferred_element_type=jnp.float32)
+            logits = term if logits is None else logits + term
     local_top = jnp.max(logits, axis=1)
     shifted = logits - local_top[:, None]
     expd = jnp.exp(shifted)
@@ -83,10 +118,18 @@
     grad_logits = (factor[:, None] * expd * (diff + centre[:, None])).astype(jnp.bfloat16)
 
     all_grads = lax.all_gather(grad_logits, "dp", axis=0, tiled=True)
-    partial_terms = lax.dot_general(
-        grad_logits, full_head, (((1,), (1,)), ((), ())), preferred_element_type=jnp.float32
+    partial_terms = jnp.concatenate(
+        [
+            lax.dot_general(
+                grad_logits, piece, (((1,), (1,)), ((), ())), preferred_element_type=jnp.float32
+            )
+            for pieces in blocks
+            for piece in pieces
+        ],
+        axis=1,
     )
-    grad_hidden = sum_terms(partial_terms, n_v)
+    turned, all_grads = sum_terms(partial_terms, n_v, all_grads)
+    grad_hidden = jnp.roll(turned, me * depth, axis=1)
     grad_head = lax.dot_general(
         slices, all_grads, (((0,), (0,)), ((), ())), preferred_element_type=jnp.float32
     )

time: 286 us -> 280 us (0.979)
  waiting for transfers between devices: 184 us -> 72.8 us
  starting transfers between devices: 43.6 us -> 98.8 us
  matrix products: 17.5 us -> 44.2 us
  blocking collectives: 12.9 us -> 25 us
  local copies, waits for them, and re-layouts: 9.62 us -> 17.5 us
    all_gather x1 -> x0, waiting for transfers between devices: 98.4 us -> none  [body(): full_head = lax.all_gather(head_weight, 'dp', axis=0, tiled=True)]
    ppermute x0 -> x14, starting transfers between devices: none -> 45.7 us  [the longest x4 16.9 us: ring_blocks(): down[0] = lax.ppermute(down[0], 'dp', left)]
    ppermute x0 -> x14, waiting for transfers between devices: none -> 33.3 us  [the longest x4 26.5 us: ring_blocks(): down[0] = lax.ppermute(down[0], 'dp', left)]
    all_to_all x3 -> x4, waiting for transfers between devices: 53 us -> 25.9 us  [spread(): return lax.all_to_all(copies, 'vocab', 0, 0, axis_index_groups=groups)]
    dot_general x2 -> x32, matrix products: 13.1 us -> 39.9 us  [the longest x16 27 us: body(): lax.dot_general(grad_logits, piece, (((1,), (1,)), ((), ())), preferred_e...]
    all_to_all x1 -> x0, waiting for transfers between devices: 14.3 us -> none  [sum_terms(): lax.all_to_all(mine.reshape(many, rows // many, half), 'vocab', 0, 0, axi...]
    all_to_all x1, blocking collectives: 7.49 us -> 19.6 us  [sum_terms(): lax.all_to_all(mine.reshape(many, rows // many, half), 'vocab', 0, 0, axi...]
    all_to_all x1, starting transfers between devices: 3.85 us -> 10.9 us  [hidden_slice(): got = lax.all_to_all(mine, 'dp', 0, 0)]
  transfers between devices with their start and end apart: 8 -> 21, of which waited for: 7 -> 8; matrix products, arithmetic and copies ran while one was open for 4% -> 20% of each run, Pallas kernels for 0% -> 0%
where the time goes in v2:
time: 280 us; the launch traced here: 278 us
  starting transfers between devices  98.8 us (35%)
  waiting for transfers between devices  72.8 us (26%)
  matrix products  44.2 us (16%)
  blocking collectives  25 us (9%)
  local copies, waits for them, and re-layouts  17.5 us (6%)
  between operations  14.7 us (5%)
  other arithmetic  5.17 us (2%)
    all_to_all x4, starting transfers between devices, spread(): return lax.all_to_all(copies, 'vocab', 0, 0, axis_index_groups=groups)  29.8 us
    dot_general x16, matrix products, body(): lax.dot_general(grad_logits, piece, (((1,), (1,)), ((), ())), preferred_e...  27 us
    ppermute x4, waiting for transfers between devices, ring_blocks(): down[0] = lax.ppermute(down[0], 'dp', left)  26.5 us
    all_to_all x4, waiting for transfers between devices, spread(): return lax.all_to_all(copies, 'vocab', 0, 0, axis_index_groups=groups)  25.9 us
    all_to_all x1, blocking collectives, sum_terms(): lax.all_to_all(mine.reshape(many, rows // many, half), 'vocab', 0, 0, axi...  19.6 us
    ppermute x4, starting transfers between devices, ring_blocks(): down[0] = lax.ppermute(down[0], 'dp', left)  16.9 us
    all_to_all x1, waiting for transfers between devices, body(): lax.all_to_all(teacher_logprobs, 'vocab', split_axis=1, concat_axis=0, ti...  13.6 us
    dot_general x16, matrix products, body(): term = jnp.dot(feats, blocks[k][i], preferred_element_type=jnp.float32)  12.9 us
  transfers between devices with their start and end apart: 21, of which 8 were waited for; matrix products, arithmetic and copies ran while one was open for 20% of the time, Pallas kernels for 0%

profile of v2, /device:TPU:1, one launch (start us, length us, event | category | flops | bytes accessed | tf_op | source)
XLA Modules:
  0.0 278.2 jit_solution(8628159323151332897)
XLA Ops:
  9.0 10.9 %all-to-all-start = ((bf16[8,2,512]{2,1,0:T(2,128)(2,1)}), bf16[8,2,512]{2,1,0:T(2,128)(2,1)S(1)}, u32[]{:S(2)}, u32[]{:S(2)}) async-start(bf16[8,2,512]{2,1,0:T(2,128)(2,1)} %bitcast.1), calls=%async_computation | async-start | bytes 32768 | tf_op jit(solution)/shard_map/all_to_all | solution.py:28
  19.9 2.4 fusion.62
  22.3 3.4 %collective-permute-start.3 = (bf16[256,1280]{1,0:T(8,128)(2,1)}, bf16[256,1280]{1,0:T(8,128)(2,1)}, u32[]{:S(2)}, u32[]{:S(2)}) collective-permute-start(bf16[256,1280]{1,0:T(8,128)(2,1)} %get-tuple-element.15), channel_id=1, source_target_pairs={{0,64},{64,128},{128,192},{192,256},{256,320},{320,384},{384,448},... | collective-permute-start | bytes 1966088 | tf_op jit(solution)/shard_map/ppermute | solution.py:43
  25.7 3.1 %collective-permute-start.1 = (bf16[256,1280]{1,0:T(8,128)(2,1)}, bf16[256,1280]{1,0:T(8,128)(2,1)}, u32[]{:S(2)}, u32[]{:S(2)}) collective-permute-start(bf16[256,1280]{1,0:T(8,128)(2,1)} %get-tuple-element.15), channel_id=1, source_target_pairs={{0,448},{64,0},{128,64},{192,128},{256,192},{320,256},{384,320},{4... | collective-permute-start | bytes 1966088 | tf_op jit(solution)/shard_map/ppermute | solution.py:45
  28.8 2.1 collective-permute-start.2
  31.0 4.3 %collective-permute-start = (bf16[256,1280]{1,0:T(8,128)(2,1)}, bf16[256,1280]{1,0:T(8,128)(2,1)}, u32[]{:S(2)}, u32[]{:S(2)}) collective-permute-start(bf16[256,1280]{1,0:T(8,128)(2,1)} %get-tuple-element.14), channel_id=1, source_target_pairs={{0,448},{64,0},{128,64},{192,128},{256,192},{320,256},{384,320},{4... | collective-permute-start | bytes 1966088 | tf_op jit(solution)/shard_map/ppermute | solution.py:42
  35.4 12.2 %all-to-all-start.2 = ((bf16[2,64,1280]{2,0,1:T(2,128)(2,1)}), bf16[2,64,1280]{2,0,1:T(2,128)(2,1)S(1)}, u32[]{:S(2)}, u32[]{:S(2)}) async-start(bf16[2,64,1280]{2,0,1:T(2,128)(2,1)} %bitcast.5), calls=%async_computation.2 | async-start | bytes 655360 | tf_op jit(solution)/shard_map/all_to_all | solution.py:74
  48.2 13.6 %all-to-all-done.2 = bf16[2,64,1280]{2,0,1:T(2,128)(2,1)S(1)} async-done(((bf16[2,64,1280]{2,0,1:T(2,128)(2,1)}), bf16[2,64,1280]{2,0,1:T(2,128)(2,1)S(1)}, u32[]{:S(2)}, u32[]{:S(2)}) %all-to-all-start.2) | async-done | bytes 327712 | tf_op jit(solution)/shard_map/all_to_all | solution.py:74
  61.8 2.0 broadcast_in_dim.41
  63.8 5.1 %all-to-all-start.1 = ((bf16[64,8,2,512]{3,2,1,0:T(2,128)(2,1)}), bf16[64,8,2,512]{3,2,1,0:T(2,128)(2,1)S(1)}, u32[]{:S(2)}, u32[]{:S(2)}) async-start(bf16[64,8,2,512]{3,2,1,0:T(2,128)(2,1)} %broadcast_in_dim.41), calls=%async_computation.1 | async-start | bytes 2097152 | tf_op jit(solution)/shard_map/all_to_all | solution.py:20
  68.8 2.0 convert_bitcast_fusion
  72.4 1.9 collective-permute-start.7
  74.4 4.6 %collective-permute-start.5 = (bf16[256,1280]{1,0:T(8,128)(2,1)}, bf16[256,1280]{1,0:T(8,128)(2,1)S(1)}, u32[]{:S(2)}, u32[]{:S(2)}) collective-permute-start(bf16[256,1280]{1,0:T(8,128)(2,1)} %collective-permute-done.1), channel_id=1, source_target_pairs={{0,448},{64,0},{128,64},{192,128},{256,192},{320,256},{384,320},{4... | collective-permute-start | bytes 1966088 | tf_op jit(solution)/shard_map/ppermute | solution.py:45
  79.0 1.9 collective-permute-start.4
  83.6 3.4 %collective-permute-start.6 = (bf16[256,1280]{1,0:T(8,128)(2,1)}, bf16[256,1280]{1,0:T(8,128)(2,1)S(1)}, u32[]{:S(2)}, u32[]{:S(2)}) collective-permute-start(bf16[256,1280]{1,0:T(8,128)(2,1)} %collective-permute-done.2), channel_id=1, source_target_pairs={{0,64},{64,128},{128,192},{192,256},{256,320},{320,384},{384,448},... | collective-permute-start | bytes 1966088 | tf_op jit(solution)/shard_map/ppermute | solution.py:46
  89.7 1.9 collective-permute-done.7
  91.6 1.9 collective-permute-start.11
  93.5 4.6 %collective-permute-start.9 = (bf16[256,1280]{1,0:T(8,128)(2,1)S(1)}, bf16[256,1280]{1,0:T(8,128)(2,1)S(1)}, u32[]{:S(2)}, u32[]{:S(2)}) collective-permute-start(bf16[256,1280]{1,0:T(8,128)(2,1)S(1)} %collective-permute-done.5), channel_id=1, source_target_pairs={{0,448},{64,0},{128,64},{192,128},{256,192},{320,256},{384,320},{4... | collective-permute-start | bytes 1966088 | tf_op jit(solution)/shard_map/ppermute | solution.py:45
  98.1 8.5 %collective-permute-done.4 = bf16[256,1280]{1,0:T(8,128)(2,1)S(1)} collective-permute-done((bf16[256,1280]{1,0:T(8,128)(2,1)}, bf16[256,1280]{1,0:T(8,128)(2,1)S(1)}, u32[]{:S(2)}, u32[]{:S(2)}) %collective-permute-start.4) | collective-permute-done | bytes 655392 | tf_op jit(solution)/shard_map/ppermute | solution.py:42
  106.6 5.2 %collective-permute-start.8 = (bf16[256,1280]{1,0:T(8,128)(2,1)S(1)}, bf16[256,1280]{1,0:T(8,128)(2,1)}, u32[]{:S(2)}, u32[]{:S(2)}) collective-permute-start(bf16[256,1280]{1,0:T(8,128)(2,1)S(1)} %collective-permute-done.4), channel_id=1, source_target_pairs={{0,448},{64,0},{128,64},{192,128},{256,192},{320,256},{384,320},{4... | collective-permute-start | bytes 1966088 | tf_op jit(solution)/shard_map/ppermute | solution.py:42
  112.4 1.9 collective-permute-start.10
  114.9 4.8 %collective-permute-done.11 = bf16[256,1280]{1,0:T(8,128)(2,1)S(1)} collective-permute-done((bf16[256,1280]{1,0:T(8,128)(2,1)S(1)}, bf16[256,1280]{1,0:T(8,128)(2,1)S(1)}, u32[]{:S(2)}, u32[]{:S(2)}) %collective-permute-start.11) | collective-permute-done | bytes 655392 | tf_op jit(solution)/shard_map/ppermute | solution.py:43
  119.7 1.9 collective-permute-start.13
  121.6 13.0 %collective-permute-done.8 = bf16[256,1280]{1,0:T(8,128)(2,1)} collective-permute-done((bf16[256,1280]{1,0:T(8,128)(2,1)S(1)}, bf16[256,1280]{1,0:T(8,128)(2,1)}, u32[]{:S(2)}, u32[]{:S(2)}) %collective-permute-start.8) | collective-permute-done | bytes 655392 | tf_op jit(solution)/shard_map/ppermute | solution.py:42
  134.6 5.4 %collective-permute-start.12 = (bf16[256,1280]{1,0:T(8,128)(2,1)}, bf16[256,1280]{1,0:T(8,128)(2,1)}, u32[]{:S(2)}, u32[]{:S(2)}) collective-permute-start(bf16[256,1280]{1,0:T(8,128)(2,1)} %collective-permute-done.8), channel_id=1, source_target_pairs={{0,448},{64,0},{128,64},{192,128},{256,192},{320,256},{384,320},{4... | collective-permute-start | bytes 1966088 | tf_op jit(solution)/shard_map/ppermute | solution.py:42
  141.5 2.2 fusion.3
  143.7 1.8 copy.22
  145.4 2.2 reshape.84
  147.7 5.0 %collective-permute-done.12 = bf16[256,1280]{1,0:T(8,128)(2,1)} collective-permute-done((bf16[256,1280]{1,0:T(8,128)(2,1)}, bf16[256,1280]{1,0:T(8,128)(2,1)}, u32[]{:S(2)}, u32[]{:S(2)}) %collective-permute-start.12) | collective-permute-done | bytes 655392 | tf_op jit(solution)/shard_map/ppermute | solution.py:42
  156.8 12.6 %all-to-all-start.3 = ((f32[64,3,128]{2,1,0:T(4,128)}), f32[64,3,128]{2,1,0:T(4,128)S(1)}, u32[]{:S(2)}, u32[]{:S(2)}) async-start(f32[64,3,128]{2,1,0:T(4,128)} %broadcast_in_dim.66), calls=%async_computation.3 | async-start | bytes 262144 | tf_op jit(solution)/shard_map/all_to_all | solution.py:20
  169.8 10.7 %all-to-all-done.3 = f32[64,3,128]{2,1,0:T(4,128)S(1)} async-done(((f32[64,3,128]{2,1,0:T(4,128)}), f32[64,3,128]{2,1,0:T(4,128)S(1)}, u32[]{:S(2)}, u32[]{:S(2)}) %all-to-all-start.3) | async-done | bytes 98336 | tf_op jit(solution)/shard_map/all_to_all | solution.py:20
  180.9 2.2 convolution_dynamic-update-slice_fusion.15
  183.2 2.3 convolution_dynamic-update-slice_fusion.14
  185.5 2.2 convolution_dynamic-update-slice_fusion.13
  187.7 2.2 convolution_dynamic-update-slice_fusion.12
  192.0 2.2 convolution_dynamic-update-slice_fusion.9
  195.2 2.2 convolution_dynamic-update-slice_fusion.7
  197.4 2.2 convolution_dynamic-update-slice_fusion.6
  203.7 2.1 convolution_dynamic-update-slice_fusion.1
  205.8 2.1 convolution_dynamic-update-slice_fusion
  208.0 1.8 copy.31
  209.7 5.4 %all_to_all.48 = f32[2,128,2048]{2,1,0:T(8,128)S(1)} all-to-all(f32[2,128,2048]{2,1,0:T(8,128)S(1)} %bitcast.74), channel_id=1, replica_groups={{0,1},{2,3},{4,5},{6,7},{8,9},{10,11},{12,13},{14,15},{16,17},{18,19},{..., dimensions={0} | all-to-all | bytes 4194304 | tf_op jit(solution)/shard_map/all_to_all | solution.py:56
  215.5 19.6 %all_to_all.49 = bf16[32,4,2048]{2,1,0:T(4,128)(2,1)S(1)} all-to-all(bf16[32,4,2048]{2,1,0:T(4,128)(2,1)S(1)} %convert_element_type.29), channel_id=1, replica_groups={{0,2,4,6,8,10,12,14,16,18,20,22,24,26,28,30,32,34,36,38,40,42,44,46,48,..., dimensions={0} | all-to-all | bytes 1048576 | tf_op jit(solution)/shard_map/all_to_all | solution.py:61
  236.3 5.0 %all-to-all-start.6 = ((bf16[32,4,2048]{2,1,0:T(4,128)(2,1)}), bf16[32,4,2048]{2,1,0:T(4,128)(2,1)S(1)}, u32[]{:S(2)}, u32[]{:S(2)}) async-start(bf16[32,4,2048]{2,1,0:T(4,128)(2,1)} %broadcast_in_dim.67), calls=%async_computation.6 | async-start | bytes 1048576 | tf_op jit(solution)/shard_map/all_to_all | solution.py:20
  241.3 15.2 %all-to-all-done.6 = bf16[32,4,2048]{2,1,0:T(4,128)(2,1)S(1)} async-done(((bf16[32,4,2048]{2,1,0:T(4,128)(2,1)}), bf16[32,4,2048]{2,1,0:T(4,128)(2,1)S(1)}, u32[]{:S(2)}, u32[]{:S(2)}) %all-to-all-start.6) | async-done | bytes 524320 | tf_op jit(solution)/shard_map/all_to_all | solution.py:20
  257.8 7.2 %all-to-all-start.7 = ((bf16[2,128,2048]{2,1,0:T(8,128)(2,1)}), bf16[2,128,2048]{2,1,0:T(8,128)(2,1)S(1)}, u32[]{:S(2)}, u32[]{:S(2)}) async-start(bf16[2,128,2048]{2,1,0:T(8,128)(2,1)} %broadcast_in_dim.68), calls=%async_computation.7 | async-start | bytes 2097152 | tf_op jit(solution)/shard_map/all_to_all | solution.py:20
  264.9 4.4 %convolution_convert_fusion = bf16[512,1280]{1,0:T(8,128)(2,1)} fusion(bf16[1024,512]{1,0:T(8,128)(2,1)S(1)} %copy-done.4, bf16[1024,1280]{1,0:T(8,128)(2,1)} %all-gather.2.cloned.1.call-done), kind=kOutput, calls=%fused_computation | convolution fusion | flops 1342832640 | bytes 4980736 | tf_op jit(solution)/shard_map/dot_general | solution.py:133
  269.4 1.9 fusion.12
  (97 shorter events, 26.7 us)
Async XLA Ops:
  7.2 1.2 copy-start
  7.2 40.4 %copy-start.3 = (bf16[512,1280]{1,0:T(8,128)(2,1)S(1)}, bf16[512,1280]{1,0:T(8,128)(2,1)}, u32[]{:S(2)}) copy-start(bf16[512,1280]{1,0:T(8,128)(2,1)} %param.6) | copy-start | bytes 3932164
  9.0 26.4 %all-to-all-start = ((bf16[8,2,512]{2,1,0:T(2,128)(2,1)}), bf16[8,2,512]{2,1,0:T(2,128)(2,1)S(1)}, u32[]{:S(2)}, u32[]{:S(2)}) async-start(bf16[8,2,512]{2,1,0:T(2,128)(2,1)} %bitcast.1), calls=%async_computation | async-start | bytes 32768 | tf_op jit(solution)/shard_map/all_to_all | solution.py:28
  22.3 50.1 %collective-permute-start.3 = (bf16[256,1280]{1,0:T(8,128)(2,1)}, bf16[256,1280]{1,0:T(8,128)(2,1)}, u32[]{:S(2)}, u32[]{:S(2)}) collective-permute-start(bf16[256,1280]{1,0:T(8,128)(2,1)} %get-tuple-element.15), channel_id=1, source_target_pairs={{0,64},{64,128},{128,192},{192,256},{256,320},{320,384},{384,448},... | collective-permute-start | bytes 1966088 | tf_op jit(solution)/shard_map/ppermute | solution.py:43
  25.7 48.7 %collective-permute-start.1 = (bf16[256,1280]{1,0:T(8,128)(2,1)}, bf16[256,1280]{1,0:T(8,128)(2,1)}, u32[]{:S(2)}, u32[]{:S(2)}) collective-permute-start(bf16[256,1280]{1,0:T(8,128)(2,1)} %get-tuple-element.15), channel_id=1, source_target_pairs={{0,448},{64,0},{128,64},{192,128},{256,192},{320,256},{384,320},{4... | collective-permute-start | bytes 1966088 | tf_op jit(solution)/shard_map/ppermute | solution.py:45
  28.8 54.8 %collective-permute-start.2 = (bf16[256,1280]{1,0:T(8,128)(2,1)}, bf16[256,1280]{1,0:T(8,128)(2,1)}, u32[]{:S(2)}, u32[]{:S(2)}) collective-permute-start(bf16[256,1280]{1,0:T(8,128)(2,1)} %get-tuple-element.14), channel_id=1, source_target_pairs={{0,64},{64,128},{128,192},{192,256},{256,320},{320,384},{384,448},... | collective-permute-start | bytes 1966088 | tf_op jit(solution)/shard_map/ppermute | solution.py:46
  31.0 48.0 %collective-permute-start = (bf16[256,1280]{1,0:T(8,128)(2,1)}, bf16[256,1280]{1,0:T(8,128)(2,1)}, u32[]{:S(2)}, u32[]{:S(2)}) collective-permute-start(bf16[256,1280]{1,0:T(8,128)(2,1)} %get-tuple-element.14), channel_id=1, source_target_pairs={{0,448},{64,0},{128,64},{192,128},{256,192},{320,256},{384,320},{4... | collective-permute-start | bytes 1966088 | tf_op jit(solution)/shard_map/ppermute | solution.py:42
  35.4 26.4 %all-to-all-start.2 = ((bf16[2,64,1280]{2,0,1:T(2,128)(2,1)}), bf16[2,64,1280]{2,0,1:T(2,128)(2,1)S(1)}, u32[]{:S(2)}, u32[]{:S(2)}) async-start(bf16[2,64,1280]{2,0,1:T(2,128)(2,1)} %bitcast.5), calls=%async_computation.2 | async-start | bytes 655360 | tf_op jit(solution)/shard_map/all_to_all | solution.py:74
  61.8 2.0 copy-start.17
  63.8 79.9 %all-to-all-start.1 = ((bf16[64,8,2,512]{3,2,1,0:T(2,128)(2,1)}), bf16[64,8,2,512]{3,2,1,0:T(2,128)(2,1)S(1)}, u32[]{:S(2)}, u32[]{:S(2)}) async-start(bf16[64,8,2,512]{3,2,1,0:T(2,128)(2,1)} %broadcast_in_dim.41), calls=%async_computation.1 | async-start | bytes 2097152 | tf_op jit(solution)/shard_map/all_to_all | solution.py:20
  72.4 19.2 %collective-permute-start.7 = (bf16[256,1280]{1,0:T(8,128)(2,1)}, bf16[256,1280]{1,0:T(8,128)(2,1)S(1)}, u32[]{:S(2)}, u32[]{:S(2)}) collective-permute-start(bf16[256,1280]{1,0:T(8,128)(2,1)} %collective-permute-done.3), channel_id=1, source_target_pairs={{0,64},{64,128},{128,192},{192,256},{256,320},{320,384},{384,448},... | collective-permute-start | bytes 1966088 | tf_op jit(solution)/shard_map/ppermute | solution.py:43
  74.4 19.2 %collective-permute-start.5 = (bf16[256,1280]{1,0:T(8,128)(2,1)}, bf16[256,1280]{1,0:T(8,128)(2,1)S(1)}, u32[]{:S(2)}, u32[]{:S(2)}) collective-permute-start(bf16[256,1280]{1,0:T(8,128)(2,1)} %collective-permute-done.1), channel_id=1, source_target_pairs={{0,448},{64,0},{128,64},{192,128},{256,192},{320,256},{384,320},{4... | collective-permute-start | bytes 1966088 | tf_op jit(solution)/shard_map/ppermute | solution.py:45
  79.0 27.7 %collective-permute-start.4 = (bf16[256,1280]{1,0:T(8,128)(2,1)}, bf16[256,1280]{1,0:T(8,128)(2,1)S(1)}, u32[]{:S(2)}, u32[]{:S(2)}) collective-permute-start(bf16[256,1280]{1,0:T(8,128)(2,1)} %collective-permute-done), channel_id=1, source_target_pairs={{0,448},{64,0},{128,64},{192,128},{256,192},{320,256},{384,320},{4... | collective-permute-start | bytes 1966088 | tf_op jit(solution)/shard_map/ppermute | solution.py:42
  83.6 28.8 %collective-permute-start.6 = (bf16[256,1280]{1,0:T(8,128)(2,1)}, bf16[256,1280]{1,0:T(8,128)(2,1)S(1)}, u32[]{:S(2)}, u32[]{:S(2)}) collective-permute-start(bf16[256,1280]{1,0:T(8,128)(2,1)} %collective-permute-done.2), channel_id=1, source_target_pairs={{0,64},{64,128},{128,192},{192,256},{256,320},{320,384},{384,448},... | collective-permute-start | bytes 1966088 | tf_op jit(solution)/shard_map/ppermute | solution.py:46
  91.6 23.2 %copy-start.5 = (bf16[256,1280]{1,0:T(8,128)(2,1)}, bf16[256,1280]{1,0:T(8,128)(2,1)S(1)}, u32[]{:S(2)}) copy-start(bf16[256,1280]{1,0:T(8,128)(2,1)S(1)} %collective-permute-done.7) | copy-start | bytes 1966084
  91.6 28.1 %collective-permute-start.11 = (bf16[256,1280]{1,0:T(8,128)(2,1)S(1)}, bf16[256,1280]{1,0:T(8,128)(2,1)S(1)}, u32[]{:S(2)}, u32[]{:S(2)}) collective-permute-start(bf16[256,1280]{1,0:T(8,128)(2,1)S(1)} %collective-permute-done.7), channel_id=1, source_target_pairs={{0,64},{64,128},{128,192},{192,256},{256,320},{320,384},{384,448},... | collective-permute-start | bytes 1966088 | tf_op jit(solution)/shard_map/ppermute | solution.py:43
  93.5 21.3 %copy-start.9 = (bf16[256,1280]{1,0:T(8,128)(2,1)}, bf16[256,1280]{1,0:T(8,128)(2,1)S(1)}, u32[]{:S(2)}) copy-start(bf16[256,1280]{1,0:T(8,128)(2,1)S(1)} %collective-permute-done.5) | copy-start | bytes 1966084
  93.5 46.7 %collective-permute-start.9 = (bf16[256,1280]{1,0:T(8,128)(2,1)S(1)}, bf16[256,1280]{1,0:T(8,128)(2,1)S(1)}, u32[]{:S(2)}, u32[]{:S(2)}) collective-permute-start(bf16[256,1280]{1,0:T(8,128)(2,1)S(1)} %collective-permute-done.5), channel_id=1, source_target_pairs={{0,448},{64,0},{128,64},{192,128},{256,192},{320,256},{384,320},{4... | collective-permute-start | bytes 1966088 | tf_op jit(solution)/shard_map/ppermute | solution.py:45
  106.6 8.2 %copy-start.11 = (bf16[256,1280]{1,0:T(8,128)(2,1)}, bf16[256,1280]{1,0:T(8,128)(2,1)S(1)}, u32[]{:S(2)}) copy-start(bf16[256,1280]{1,0:T(8,128)(2,1)S(1)} %collective-permute-done.4) | copy-start | bytes 1966084
  106.6 28.0 %collective-permute-start.8 = (bf16[256,1280]{1,0:T(8,128)(2,1)S(1)}, bf16[256,1280]{1,0:T(8,128)(2,1)}, u32[]{:S(2)}, u32[]{:S(2)}) collective-permute-start(bf16[256,1280]{1,0:T(8,128)(2,1)S(1)} %collective-permute-done.4), channel_id=1, source_target_pairs={{0,448},{64,0},{128,64},{192,128},{256,192},{320,256},{384,320},{4... | collective-permute-start | bytes 1966088 | tf_op jit(solution)/shard_map/ppermute | solution.py:42
  112.4 2.5 copy-start.7
  112.4 28.2 %collective-permute-start.10 = (bf16[256,1280]{1,0:T(8,128)(2,1)S(1)}, bf16[256,1280]{1,0:T(8,128)(2,1)S(1)}, u32[]{:S(2)}, u32[]{:S(2)}) collective-permute-start(bf16[256,1280]{1,0:T(8,128)(2,1)S(1)} %collective-permute-done.6), channel_id=1, source_target_pairs={{0,64},{64,128},{128,192},{192,256},{256,320},{320,384},{384,448},... | collective-permute-start | bytes 1966088 | tf_op jit(solution)/shard_map/ppermute | solution.py:46
  119.7 33.0 %collective-permute-start.13 = (bf16[256,1280]{1,0:T(8,128)(2,1)S(1)}, bf16[256,1280]{1,0:T(8,128)(2,1)}, u32[]{:S(2)}, u32[]{:S(2)}) collective-permute-start(bf16[256,1280]{1,0:T(8,128)(2,1)S(1)} %collective-permute-done.11), channel_id=1, source_target_pairs={{0,64},{64,128},{128,192},{192,256},{256,320},{320,384},{384,448},... | collective-permute-start | bytes 1966088 | tf_op jit(solution)/shard_map/ppermute | solution.py:43
  134.6 18.1 %collective-permute-start.12 = (bf16[256,1280]{1,0:T(8,128)(2,1)}, bf16[256,1280]{1,0:T(8,128)(2,1)}, u32[]{:S(2)}, u32[]{:S(2)}) collective-permute-start(bf16[256,1280]{1,0:T(8,128)(2,1)} %collective-permute-done.8), channel_id=1, source_target_pairs={{0,448},{64,0},{128,64},{192,128},{256,192},{320,256},{384,320},{4... | collective-permute-start | bytes 1966088 | tf_op jit(solution)/shard_map/ppermute | solution.py:42
  140.3 0.8 copy-start.13
  140.6 0.9 copy-start.15
  154.1 15.5 %copy-start.18 = (f32[2]{0:T(128)S(1)}, f32[2]{0:T(128)}, u32[]{:S(2)}) copy-start(f32[2]{0:T(128)} %param.9) | copy-start | bytes 28
  154.1 15.6 %copy-start.19 = (s32[2]{0:T(128)S(1)}, s32[2]{0:T(128)}, u32[]{:S(2)}) copy-start(s32[2]{0:T(128)} %param.8) | copy-start | bytes 28
  156.8 23.7 %all-to-all-start.3 = ((f32[64,3,128]{2,1,0:T(4,128)}), f32[64,3,128]{2,1,0:T(4,128)S(1)}, u32[]{:S(2)}, u32[]{:S(2)}) async-start(f32[64,3,128]{2,1,0:T(4,128)} %broadcast_in_dim.66), calls=%async_computation.3 | async-start | bytes 262144 | tf_op jit(solution)/shard_map/all_to_all | solution.py:20
  169.3 87.3 %all-gather.2.cloned.1.call-start = ((), (), s32[]{:S(2)}) async-start(), calls=%async_computation.8 | async-start | bytes 2949120 | tf_op jit(solution)/shard_map/all_gather | solution.py:120
  180.9 2.2 copy-start.1
  183.1 6.8 %copy-start.12 = (bf16[256,1280]{1,0:T(8,128)(2,1)S(1)}, bf16[256,1280]{1,0:T(8,128)(2,1)}, u32[]{:S(2)}) copy-start(bf16[256,1280]{1,0:T(8,128)(2,1)} %copy-done.11) | copy-start | bytes 1966084
  183.2 4.6 %copy-start.2 = (bf16[128,1280]{1,0:T(8,128)(2,1)S(1)}, bf16[128,1280]{1,0:T(8,128)(2,1)}, u32[]{:S(2)}) copy-start(bf16[128,1280]{1,0:T(8,128)(2,1)} %copy-done.1) | copy-start | bytes 983044
  183.2 7.8 %copy-start.10 = (bf16[256,1280]{1,0:T(8,128)(2,1)S(1)}, bf16[256,1280]{1,0:T(8,128)(2,1)}, u32[]{:S(2)}) copy-start(bf16[256,1280]{1,0:T(8,128)(2,1)} %copy-done.9) | copy-start | bytes 1966084
  187.7 6.4 %copy-start.14 = (bf16[256,1280]{1,0:T(8,128)(2,1)S(1)}, bf16[256,1280]{1,0:T(8,128)(2,1)}, u32[]{:S(2)}) copy-start(bf16[256,1280]{1,0:T(8,128)(2,1)} %copy-done.13) | copy-start | bytes 1966084
  192.0 7.6 %copy-start.16 = (bf16[256,1280]{1,0:T(8,128)(2,1)S(1)}, bf16[256,1280]{1,0:T(8,128)(2,1)}, u32[]{:S(2)}) copy-start(bf16[256,1280]{1,0:T(8,128)(2,1)} %copy-done.15) | copy-start | bytes 1966084
  195.2 6.4 %copy-start.8 = (bf16[256,1280]{1,0:T(8,128)(2,1)S(1)}, bf16[256,1280]{1,0:T(8,128)(2,1)}, u32[]{:S(2)}) copy-start(bf16[256,1280]{1,0:T(8,128)(2,1)} %copy-done.7) | copy-start | bytes 1966084
  197.4 5.3 %copy-start.6 = (bf16[256,1280]{1,0:T(8,128)(2,1)S(1)}, bf16[256,1280]{1,0:T(8,128)(2,1)}, u32[]{:S(2)}) copy-start(bf16[256,1280]{1,0:T(8,128)(2,1)} %copy-done.5) | copy-start | bytes 1966084
  236.3 20.2 %all-to-all-start.6 = ((bf16[32,4,2048]{2,1,0:T(4,128)(2,1)}), bf16[32,4,2048]{2,1,0:T(4,128)(2,1)S(1)}, u32[]{:S(2)}, u32[]{:S(2)}) async-start(bf16[32,4,2048]{2,1,0:T(4,128)(2,1)} %broadcast_in_dim.67), calls=%async_computation.6 | async-start | bytes 1048576 | tf_op jit(solution)/shard_map/all_to_all | solution.py:20
  256.6 8.3 %copy-start.4 = (bf16[1024,512]{1,0:T(8,128)(2,1)S(1)}, bf16[1024,512]{1,0:T(8,128)(2,1)}, u32[]{:S(2)}) copy-start(bf16[1024,512]{1,0:T(8,128)(2,1)} %reshape.84) | copy-start | bytes 3145732
  257.8 11.5 %all-to-all-start.7 = ((bf16[2,128,2048]{2,1,0:T(8,128)(2,1)}), bf16[2,128,2048]{2,1,0:T(8,128)(2,1)S(1)}, u32[]{:S(2)}, u32[]{:S(2)}) async-start(bf16[2,128,2048]{2,1,0:T(8,128)(2,1)} %broadcast_in_dim.68), calls=%async_computation.7 | async-start | bytes 2097152 | tf_op jit(solution)/shard_map/all_to_all | solution.py:20
Sparse Core Ops, SparseCore 0:
  183.3 38.4 all-gather.1

commit v3 on v2

--- a/solution.py
+++ b/solution.py
@@ -1,6 +1,8 @@
 import jax
 import jax.numpy as jnp
 from jax import lax
+from jax.experimental import pallas as pl
+from jax.experimental.pallas import tpu as pltpu
 from jax.sharding import PartitionSpec as P
 
 SEQ_LEN = 64
@@ -20,14 +22,10 @@
     return lax.all_to_all(copies, "vocab", 0, 0, axis_index_groups=groups)
 
 
-def hidden_slice(hidden, n_dp, n_v):
-    rows, d = hidden.shape
-    share = rows // n_v
+def hidden_share(hidden, n_v):
+    share = hidden.shape[0] // n_v
     mine = lax.dynamic_slice_in_dim(hidden, lax.axis_index("vocab") * share, share, 0)
-    mine = mine.reshape(share, n_dp, d // n_dp).transpose(1, 0, 2)
-    got = lax.all_to_all(mine, "dp", 0, 0)
-    everyone = spread(got, None, n_v)
-    return everyone.transpose(1, 0, 2, 3).reshape(n_dp * rows, d // n_dp)
+    return lax.all_gather(mine, "dp", axis=0)
 
 
 def ring_blocks(block, n):
@@ -50,22 +48,49 @@
     return [got[k] for k in range(n)]
 
 
-def sum_terms(partial_terms, n_v, other):
-    rows, d = partial_terms.shape
-    half, many = d // 2, n_v // 2
+def terms_kernel(me_ref, grads_ref, *refs):
+    pieces, out_ref = refs[:-1], refs[-1]
+    blocks, _, depth = out_ref.shape
+    per = len(pieces) // blocks
+    part = depth // per
+    grads = grads_ref[...]
+    for j, piece in enumerate(pieces):
+        place = lax.rem(me_ref[0] + j // per, blocks)
+        out_ref[place, :, pl.ds(j % per * part, part)] = lax.dot_general(
+            grads, piece[...], (((1,), (1,)), ((), ())), preferred_element_type=jnp.float32
+        )
+
+
+def hidden_terms(me, grads, pieces, blocks):
+    rows, width = grads.shape
+    d = sum(piece.shape[0] for piece in pieces)
+    vmem = pl.BlockSpec(memory_space=pltpu.VMEM)
+    return pl.pallas_call(
+        terms_kernel,
+        out_shape=jax.ShapeDtypeStruct((blocks, rows, d // blocks), jnp.float32),
+        in_specs=[pl.BlockSpec(memory_space=pltpu.SMEM)] + [vmem] * (1 + len(pieces)),
+        out_specs=vmem,
+        compiler_params=pltpu.CompilerParams(vmem_limit_bytes=24 * 2**20),
+        cost_estimate=pl.CostEstimate(
+            flops=2 * rows * d * width, bytes_accessed=2 * d * width + 4 * rows * d, transcendentals=0
+        ),
+    )(me.reshape(1), grads, *pieces)
+
+
+def sum_terms(terms, n_v, other):
+    blocks, rows, d = terms.shape
+    many = n_v // 2
     swapped = lax.all_to_all(
-        partial_terms.reshape(rows, 2, half).transpose(1, 0, 2), "vocab", 0, 0,
-        axis_index_groups=pair_groups(n_v),
+        terms.reshape(2, blocks // 2, rows, d), "vocab", 0, 0, axis_index_groups=pair_groups(n_v)
     )
     mine = (swapped[0] + swapped[1]).astype(jnp.bfloat16)
-    terms = lax.all_to_all(
-        mine.reshape(many, rows // many, half), "vocab", 0, 0, axis_index_groups=core_groups(n_v)
-    )
-    total = jnp.sum(terms.astype(jnp.float32), axis=0).astype(jnp.bfloat16)
-    whole = spread(total, core_groups(n_v), many).reshape(rows, half)
+    mine = mine.reshape(many, blocks // 2 * rows // many, d)
+    parts = lax.all_to_all(mine, "vocab", 0, 0, axis_index_groups=core_groups(n_v))
+    total = jnp.sum(parts.astype(jnp.float32), axis=0).astype(jnp.bfloat16)
+    whole = spread(total, core_groups(n_v), many)
     whole, other = lax.optimization_barrier((whole, other))
     both = spread(whole, pair_groups(n_v), 2)
-    return jnp.concatenate([both[0], both[1]], axis=1), other
+    return both.reshape(blocks, rows, d), other
 
 
 def body(hidden, head_weight, teacher_logprobs, lengths, seq_weights):
@@ -74,7 +99,7 @@
     teacher = lax.all_to_all(
         teacher_logprobs, "vocab", split_axis=1, concat_axis=0, tiled=True
     ).astype(jnp.float32)
-    slices = hidden_slice(hidden, n_dp, n_v)
+    share = hidden_share(hidden, n_v)
     tok_rows = hidden.shape[0]
 
     rows = jnp.arange(tok_rows, dtype=jnp.int32)
@@ -93,8 +118,10 @@
     for k in range(1, n_dp // 2 + 1):
         order += [k] if k == n_dp - k else [k, n_dp - k]
     for k in order:
-        if k == n_dp // 2:
-            blocks[k][0], slices = lax.optimization_barrier((blocks[k][0], slices))
+        if k == 1:
+            blocks[k][0], share = lax.optimization_barrier((blocks[k][0], share))
+            share = lax.dynamic_slice_in_dim(share, me * depth, depth, 2)
+            slices = lax.all_gather(share, "vocab", axis=0)
         place = lax.rem(me + k, n_dp) * depth
         for i in range(2):
             feats = lax.dynamic_slice_in_dim(hidden, place + i * part, part, 1)
@@ -117,19 +144,12 @@
     centre = own - weighted / total
     grad_logits = (factor[:, None] * expd * (diff + centre[:, None])).astype(jnp.bfloat16)
 
+    slices, grad_logits = lax.optimization_barrier((slices, grad_logits))
+    slices = slices.transpose(1, 0, 2, 3).reshape(n_dp * tok_rows, depth)
     all_grads = lax.all_gather(grad_logits, "dp", axis=0, tiled=True)
-    partial_terms = jnp.concatenate(
-        [
-            lax.dot_general(
-                grad_logits, piece, (((1,), (1,)), ((), ())), preferred_element_type=jnp.float32
-            )
-            for pieces in blocks
-            for piece in pieces
-        ],
-        axis=1,
-    )
-    turned, all_grads = sum_terms(partial_terms, n_v, all_grads)
-    grad_hidden = jnp.roll(turned, me * depth, axis=1)
+    terms = hidden_terms(me, grad_logits, [p for pieces in blocks for p in pieces], n_dp)
+    summed, all_grads = sum_terms(terms, n_v, all_grads)
+    grad_hidden = jnp.concatenate([summed[k] for k in range(n_dp)], axis=1)
     grad_head = lax.dot_general(
         slices, all_grads, (((0,), (0,)), ((), ())), preferred_element_type=jnp.float32
     )

time: 280 us -> 259 us (0.925)
  matrix products: 44.2 us -> 13.1 us
  blocking collectives: 25 us -> 53.9 us
  waiting for transfers between devices: 72.8 us -> 56.9 us
  starting transfers between devices: 98.8 us -> 85 us
  local copies, waits for them, and re-layouts: 17.5 us -> 24.9 us
  Pallas kernels: 0 us -> 4.91 us
    dot_general x16 -> x0, matrix products: 27 us -> none  [body(): lax.dot_general(grad_logits, piece, (((1,), (1,)), ((), ())), preferred_e...]
    ppermute x4, waiting for transfers between devices: 26.5 us -> 3.52 us  [ring_blocks(): down[0] = lax.ppermute(down[0], 'dp', left)]
    all_gather x0 -> x1, blocking collectives: none -> 20.6 us  [hidden_share(): return lax.all_gather(mine, 'dp', axis=0)]
    ppermute x4, waiting for transfers between devices: 6.71 us -> 23.2 us  [ring_blocks(): up[1] = lax.ppermute(up[1], 'dp', right)]
    all_to_all x1, waiting for transfers between devices: 13.6 us -> 0.01 us  [body(): lax.all_to_all(teacher_logprobs, 'vocab', split_axis=1, concat_axis=0, ti...]
    unnamed x40 -> x68, local copies, waits for them, and re-layouts: 1.89 us -> 12.9 us
    all_to_all x1 -> x0, starting transfers between devices: 10.9 us -> none  [hidden_slice(): got = lax.all_to_all(mine, 'dp', 0, 0)]
    all_to_all x4 -> x2, starting transfers between devices: 29.8 us -> 20.4 us  [spread(): return lax.all_to_all(copies, 'vocab', 0, 0, axis_index_groups=groups)]
  transfers between devices with their start and end apart: 21 -> 19, of which waited for: 8 -> 7; matrix products, arithmetic and copies ran while one was open for 20% -> 9% of each run, Pallas kernels for 0% -> 2%
where the time goes in v3:
time: 259 us; the launch traced here: 258 us
  starting transfers between devices  85 us (33%)
  waiting for transfers between devices  56.9 us (22%)
  blocking collectives  53.9 us (21%)
  local copies, waits for them, and re-layouts  24.9 us (10%)
  between operations  14.7 us (6%)
  matrix products  13.1 us (5%)
  Pallas kernels  4.91 us (2%)
  other arithmetic  4.14 us (2%)
    ppermute x4, waiting for transfers between devices, ring_blocks(): up[1] = lax.ppermute(up[1], 'dp', right)  23.2 us
    all_gather x1, blocking collectives, hidden_share(): return lax.all_gather(mine, 'dp', axis=0)  20.6 us
    all_to_all x2, starting transfers between devices, spread(): return lax.all_to_all(copies, 'vocab', 0, 0, axis_index_groups=groups)  20.4 us
    all_to_all x2, waiting for transfers between devices, spread(): return lax.all_to_all(copies, 'vocab', 0, 0, axis_index_groups=groups)  20.4 us
    all_to_all x1, blocking collectives, sum_terms(): lax.all_to_all(mine, 'vocab', 0, 0, axis_index_groups=core_groups(n_v))  20 us
    ppermute x3, starting transfers between devices, ring_blocks(): down[1] = lax.ppermute(down[1], 'dp', left)  18.4 us
    ppermute x4, starting transfers between devices, ring_blocks(): down[0] = lax.ppermute(down[0], 'dp', left)  16.7 us
    unnamed x68, local copies, waits for them, and re-layouts  12.9 us
  transfers between devices with their start and end apart: 19, of which 7 were waited for; matrix products, arithmetic and copies ran while one was open for 9% of the time, Pallas kernels for 2%

profile of v3, /device:TPU:1, one launch (start us, length us, event | category | flops | bytes accessed | tf_op | source)
XLA Modules:
  0.0 257.7 jit_solution(16111982389538363807)
XLA Ops:
  7.2 1.5 fusion.65
  8.6 4.8 %collective-permute-start.3 = (bf16[256,1280]{1,0:T(8,128)(2,1)S(1)}, bf16[256,1280]{1,0:T(8,128)(2,1)}, u32[]{:S(2)}, u32[]{:S(2)}) collective-permute-start(bf16[256,1280]{1,0:T(8,128)(2,1)S(1)} %get-tuple-element.18.refs_1_), channel_id=1, source_target_pairs={{0,64},{64,128},{128,192},{192,256},{256,320},{320,384},{384,448},... | collective-permute-start | bytes 1966088 | tf_op jit(solution)/shard_map/ppermute | solution.py:41
  13.5 8.6 %collective-permute-start.1 = (bf16[256,1280]{1,0:T(8,128)(2,1)S(1)}, bf16[256,1280]{1,0:T(8,128)(2,1)}, u32[]{:S(2)}, u32[]{:S(2)}) collective-permute-start(bf16[256,1280]{1,0:T(8,128)(2,1)S(1)} %get-tuple-element.18.refs_1_), channel_id=1, source_target_pairs={{0,448},{64,0},{128,64},{192,128},{256,192},{320,256},{384,320},{4... | collective-permute-start | bytes 1966088 | tf_op jit(solution)/shard_map/ppermute | solution.py:43
  22.1 1.9 collective-permute-start.2
  24.0 4.6 %collective-permute-start = (bf16[256,1280]{1,0:T(8,128)(2,1)S(1)}, bf16[256,1280]{1,0:T(8,128)(2,1)S(1)}, u32[]{:S(2)}, u32[]{:S(2)}) collective-permute-start(bf16[256,1280]{1,0:T(8,128)(2,1)S(1)} %get-tuple-element.19.refs_0_), channel_id=1, source_target_pairs={{0,448},{64,0},{128,64},{192,128},{256,192},{320,256},{384,320},{4... | collective-permute-start | bytes 1966088 | tf_op jit(solution)/shard_map/ppermute | solution.py:40
  28.6 11.6 %all-to-all-start = ((bf16[2,64,1280]{2,0,1:T(2,128)(2,1)}), bf16[2,64,1280]{2,0,1:T(2,128)(2,1)S(1)}, u32[]{:S(2)}, u32[]{:S(2)}) async-start(bf16[2,64,1280]{2,0,1:T(2,128)(2,1)} %bitcast.82), calls=%async_computation | async-start | bytes 655360 | tf_op jit(solution)/shard_map/all_to_all | solution.py:99
  40.3 1.3 fusion.45
  41.7 2.2 convolution_add_fusion.4
  43.9 20.6 %all-gather.2 = bf16[8,2,4096]{2,1,0:T(2,128)(2,1)S(1)} all-gather(bf16[1,2,4096]{2,1,0:T(2,128)(2,1)S(1)} %dynamic-slice_bitcast_fusion), channel_id=2, replica_groups=mesh['dp'=8,'vocab'=64] {'dp'}, dimensions={0}, use_global_device_ids=true | all-gather | bytes 147456 | tf_op jit(solution)/shard_map/all_gather | solution.py:28
  65.6 2.4 reshape.86
  68.6 4.9 %collective-permute-start.4 = (bf16[256,1280]{1,0:T(8,128)(2,1)S(1)}, bf16[256,1280]{1,0:T(8,128)(2,1)S(1)}, u32[]{:S(2)}, u32[]{:S(2)}) collective-permute-start(bf16[256,1280]{1,0:T(8,128)(2,1)S(1)} %collective-permute-done.refs_2_), channel_id=1, source_target_pairs={{0,448},{64,0},{128,64},{192,128},{256,192},{320,256},{384,320},{4... | collective-permute-start | bytes 1966088 | tf_op jit(solution)/shard_map/ppermute | solution.py:40
  73.5 1.9 collective-permute-start.7
  75.5 4.6 %collective-permute-start.5 = (bf16[256,1280]{1,0:T(8,128)(2,1)}, bf16[256,1280]{1,0:T(8,128)(2,1)S(1)}, u32[]{:S(2)}, u32[]{:S(2)}) collective-permute-start(bf16[256,1280]{1,0:T(8,128)(2,1)} %collective-permute-done.1.refs_3_), channel_id=1, source_target_pairs={{0,448},{64,0},{128,64},{192,128},{256,192},{320,256},{384,320},{4... | collective-permute-start | bytes 1966088 | tf_op jit(solution)/shard_map/ppermute | solution.py:43
  80.0 1.3 fusion.37
  81.4 1.3 fusion.41
  82.8 1.9 collective-permute-start.6
  84.7 1.4 fusion.39
  86.4 1.9 collective-permute-start.11
  88.3 6.9 %collective-permute-done.5.refs_5_ = bf16[256,1280]{1,0:T(8,128)(2,1)S(1)} collective-permute-done((bf16[256,1280]{1,0:T(8,128)(2,1)}, bf16[256,1280]{1,0:T(8,128)(2,1)S(1)}, u32[]{:S(2)}, u32[]{:S(2)}) %collective-permute-start.5) | collective-permute-done | bytes 655392 | tf_op jit(solution)/shard_map/ppermute | solution.py:43
  95.2 5.2 %collective-permute-start.9 = (bf16[256,1280]{1,0:T(8,128)(2,1)S(1)}, bf16[256,1280]{1,0:T(8,128)(2,1)S(1)}, u32[]{:S(2)}, u32[]{:S(2)}) collective-permute-start(bf16[256,1280]{1,0:T(8,128)(2,1)S(1)} %collective-permute-done.5.refs_5_), channel_id=1, source_target_pairs={{0,448},{64,0},{128,64},{192,128},{256,192},{320,256},{384,320},{4... | collective-permute-start | bytes 1966088 | tf_op jit(solution)/shard_map/ppermute | solution.py:43
  100.5 1.9 collective-permute-start.8
  102.9 3.4 %collective-permute-start.10 = (bf16[256,1280]{1,0:T(8,128)(2,1)S(1)}, bf16[256,1280]{1,0:T(8,128)(2,1)S(1)}, u32[]{:S(2)}, u32[]{:S(2)}) collective-permute-start(bf16[256,1280]{1,0:T(8,128)(2,1)S(1)} %collective-permute-done.6.refs_12_), channel_id=1, source_target_pairs={{0,64},{64,128},{128,192},{192,256},{256,320},{320,384},{384,448},... | collective-permute-start | bytes 1966088 | tf_op jit(solution)/shard_map/ppermute | solution.py:44
  106.9 10.0 %collective-permute-done.11.refs_11_ = bf16[256,1280]{1,0:T(8,128)(2,1)S(1)} collective-permute-done((bf16[256,1280]{1,0:T(8,128)(2,1)S(1)}, bf16[256,1280]{1,0:T(8,128)(2,1)S(1)}, u32[]{:S(2)}, u32[]{:S(2)}) %collective-permute-start.11) | collective-permute-done | bytes 655392 | tf_op jit(solution)/shard_map/ppermute | solution.py:41
  116.9 1.9 collective-permute-start.13
  118.8 3.5 %collective-permute-done.8.refs_6_ = bf16[256,1280]{1,0:T(8,128)(2,1)S(1)} collective-permute-done((bf16[256,1280]{1,0:T(8,128)(2,1)S(1)}, bf16[256,1280]{1,0:T(8,128)(2,1)S(1)}, u32[]{:S(2)}, u32[]{:S(2)}) %collective-permute-start.8) | collective-permute-done | bytes 655392 | tf_op jit(solution)/shard_map/ppermute | solution.py:40
  122.4 5.3 %collective-permute-start.12 = (bf16[256,1280]{1,0:T(8,128)(2,1)S(1)}, bf16[256,1280]{1,0:T(8,128)(2,1)S(1)}, u32[]{:S(2)}, u32[]{:S(2)}) collective-permute-start(bf16[256,1280]{1,0:T(8,128)(2,1)S(1)} %collective-permute-done.8.refs_6_), channel_id=1, source_target_pairs={{0,448},{64,0},{128,64},{192,128},{256,192},{320,256},{384,320},{4... | collective-permute-start | bytes 1966088 | tf_op jit(solution)/shard_map/ppermute | solution.py:40
  128.2 2.8 %collective-permute-done.10.refs_10_ = bf16[256,1280]{1,0:T(8,128)(2,1)S(1)} collective-permute-done((bf16[256,1280]{1,0:T(8,128)(2,1)S(1)}, bf16[256,1280]{1,0:T(8,128)(2,1)S(1)}, u32[]{:S(2)}, u32[]{:S(2)}) %collective-permute-start.10) | collective-permute-done | bytes 655392 | tf_op jit(solution)/shard_map/ppermute | solution.py:44
  131.8 13.2 %collective-permute-done.13.refs_9_ = bf16[256,1280]{1,0:T(8,128)(2,1)S(1)} collective-permute-done((bf16[256,1280]{1,0:T(8,128)(2,1)S(1)}, bf16[256,1280]{1,0:T(8,128)(2,1)S(1)}, u32[]{:S(2)}, u32[]{:S(2)}) %collective-permute-start.13) | collective-permute-done | bytes 655392 | tf_op jit(solution)/shard_map/ppermute | solution.py:41
  147.2 15.4 %all-to-all-start.1 = ((f32[64,3,128]{2,1,0:T(4,128)}), f32[64,3,128]{2,1,0:T(4,128)S(1)}, u32[]{:S(2)}, u32[]{:S(2)}) async-start(f32[64,3,128]{2,1,0:T(4,128)} %broadcast_in_dim.59), calls=%async_computation.1 | async-start | bytes 262144 | tf_op jit(solution)/shard_map/all_to_all | solution.py:22
  162.8 2.4 copy.38
  165.2 8.5 %all-to-all-done.1 = f32[64,3,128]{2,1,0:T(4,128)S(1)} async-done(((f32[64,3,128]{2,1,0:T(4,128)}), f32[64,3,128]{2,1,0:T(4,128)S(1)}, u32[]{:S(2)}, u32[]{:S(2)}) %all-to-all-start.1) | async-done | bytes 98336 | tf_op jit(solution)/shard_map/all_to_all | solution.py:22
  173.9 2.3 multiply_convert_fusion.grads_ref
  177.2 1.1 copy-done.3
  178.2 1.1 copy-done.5
  179.3 1.1 copy-done.7
  180.4 1.1 copy-done.9
  181.5 1.1 copy-done.11
  182.6 1.1 copy-done.13
  187.0 1.1 copy-done.21
  188.1 4.9 %shard_map.68 = f32[8,128,512]{2,1,0:T(8,128)S(1)} custom-call(s32[1]{0:T(128)} %bitcast.me_ref, bf16[128,1280]{1,0:T(8,128)(2,1)S(1)} %copy-done.1, bf16[256,1280]{1,0:T(8,128)(2,1)S(1)} %get-tuple-element.19.refs_0_, bf16[256,1280]{1,0:T(8,128)(2,1)S(1)} %get-tuple-element.18.refs_1_, bf16[256,1280]{1,0:T(8,128)(2,1)S(1)} %collective-permute-done.refs_2_, ...), custom_call_target="tpu_custom_call" | custom-call | flops 1342177280 | bytes 12582912 | tf_op jit(solution)/shard_map/pallas_call | solution.py:68
  193.0 5.4 %all_to_all.38 = f32[2,4,128,512]{3,2,1,0:T(8,128)S(1)} all-to-all(f32[2,4,128,512]{3,2,1,0:T(8,128)S(1)} %bitcast.71), channel_id=1, replica_groups={{0,1},{2,3},{4,5},{6,7},{8,9},{10,11},{12,13},{14,15},{16,17},{18,19},{..., dimensions={0} | all-to-all | bytes 4194304 | tf_op jit(solution)/shard_map/all_to_all | solution.py:83
  198.6 20.0 %all_to_all.39 = bf16[32,16,512]{2,1,0:T(8,128)(2,1)S(1)} all-to-all(bf16[32,16,512]{2,1,0:T(8,128)(2,1)S(1)} %bitcast.81), channel_id=1, replica_groups={{0,2,4,6,8,10,12,14,16,18,20,22,24,26,28,30,32,34,36,38,40,42,44,46,48,..., dimensions={0} | all-to-all | bytes 1048576 | tf_op jit(solution)/shard_map/all_to_all | solution.py:88
  219.6 5.0 %all-to-all-start.4 = ((bf16[32,16,512]{2,1,0:T(8,128)(2,1)}), bf16[32,16,512]{2,1,0:T(8,128)(2,1)S(1)}, u32[]{:S(2)}, u32[]{:S(2)}) async-start(bf16[32,16,512]{2,1,0:T(8,128)(2,1)} %broadcast_in_dim.60), calls=%async_computation.4 | async-start | bytes 1048576 | tf_op jit(solution)/shard_map/all_to_all | solution.py:22
  224.6 2.0 copy.34
  226.7 1.5 reshape.85
  228.2 11.9 %all-to-all-done.4 = bf16[32,16,512]{2,1,0:T(8,128)(2,1)S(1)} async-done(((bf16[32,16,512]{2,1,0:T(8,128)(2,1)}), bf16[32,16,512]{2,1,0:T(8,128)(2,1)S(1)}, u32[]{:S(2)}, u32[]{:S(2)}) %all-to-all-start.4) | async-done | bytes 524320 | tf_op jit(solution)/shard_map/all_to_all | solution.py:22
  240.2 7.8 %all_to_all.40 = bf16[2,32,16,512]{3,2,1,0:T(8,128)(2,1)S(1)} all-to-all(bf16[2,32,16,512]{3,2,1,0:T(8,128)(2,1)S(1)} %broadcast_in_dim.61), channel_id=1, replica_groups={{0,1},{2,3},{4,5},{6,7},{8,9},{10,11},{12,13},{14,15},{16,17},{18,19},{..., dimensions={0} | all-to-all | bytes 2097152 | tf_op jit(solution)/shard_map/all_to_all | solution.py:22
  248.2 2.6 %convolution_convert_fusion = bf16[512,1280]{1,0:T(8,128)(2,1)} fusion(bf16[1024,512]{1,0:T(8,128)(2,1)S(1)} %reshape.85, bf16[1024,1280]{1,0:T(8,128)(2,1)S(1)} %copy-done.26), kind=kOutput, calls=%fused_computation | convolution fusion | flops 1342832640 | bytes 4980736 | tf_op jit(solution)/shard_map/dot_general | solution.py:153
  (105 shorter events, 12.5 us)
Async XLA Ops:
  7.2 33.1 %copy-start = (bf16[128,4096]{1,0:T(8,128)(2,1)S(1)}, bf16[128,4096]{1,0:T(8,128)(2,1)}, u32[]{:S(2)}) copy-start(bf16[128,4096]{1,0:T(8,128)(2,1)} %param.5) | copy-start | bytes 3145732
  8.6 64.9 %collective-permute-start.3 = (bf16[256,1280]{1,0:T(8,128)(2,1)S(1)}, bf16[256,1280]{1,0:T(8,128)(2,1)}, u32[]{:S(2)}, u32[]{:S(2)}) collective-permute-start(bf16[256,1280]{1,0:T(8,128)(2,1)S(1)} %get-tuple-element.18.refs_1_), channel_id=1, source_target_pairs={{0,64},{64,128},{128,192},{192,256},{256,320},{320,384},{384,448},... | collective-permute-start | bytes 1966088 | tf_op jit(solution)/shard_map/ppermute | solution.py:41
  13.5 62.0 %collective-permute-start.1 = (bf16[256,1280]{1,0:T(8,128)(2,1)S(1)}, bf16[256,1280]{1,0:T(8,128)(2,1)}, u32[]{:S(2)}, u32[]{:S(2)}) collective-permute-start(bf16[256,1280]{1,0:T(8,128)(2,1)S(1)} %get-tuple-element.18.refs_1_), channel_id=1, source_target_pairs={{0,448},{64,0},{128,64},{192,128},{256,192},{320,256},{384,320},{4... | collective-permute-start | bytes 1966088 | tf_op jit(solution)/shard_map/ppermute | solution.py:43
  22.1 60.7 %collective-permute-start.2 = (bf16[256,1280]{1,0:T(8,128)(2,1)S(1)}, bf16[256,1280]{1,0:T(8,128)(2,1)}, u32[]{:S(2)}, u32[]{:S(2)}) collective-permute-start(bf16[256,1280]{1,0:T(8,128)(2,1)S(1)} %get-tuple-element.19.refs_0_), channel_id=1, source_target_pairs={{0,64},{64,128},{128,192},{192,256},{256,320},{320,384},{384,448},... | collective-permute-start | bytes 1966088 | tf_op jit(solution)/shard_map/ppermute | solution.py:44
  24.0 44.0 %collective-permute-start = (bf16[256,1280]{1,0:T(8,128)(2,1)S(1)}, bf16[256,1280]{1,0:T(8,128)(2,1)S(1)}, u32[]{:S(2)}, u32[]{:S(2)}) collective-permute-start(bf16[256,1280]{1,0:T(8,128)(2,1)S(1)} %get-tuple-element.19.refs_0_), channel_id=1, source_target_pairs={{0,448},{64,0},{128,64},{192,128},{256,192},{320,256},{384,320},{4... | collective-permute-start | bytes 1966088 | tf_op jit(solution)/shard_map/ppermute | solution.py:40
  28.6 35.9 %all-to-all-start = ((bf16[2,64,1280]{2,0,1:T(2,128)(2,1)}), bf16[2,64,1280]{2,0,1:T(2,128)(2,1)S(1)}, u32[]{:S(2)}, u32[]{:S(2)}) async-start(bf16[2,64,1280]{2,0,1:T(2,128)(2,1)} %bitcast.82), calls=%async_computation | async-start | bytes 655360 | tf_op jit(solution)/shard_map/all_to_all | solution.py:99
  40.2 122.6 %all-gather.8.cloned.1.call-start = ((), (), s32[]{:S(2)}) async-start(), calls=%async_computation.7 | async-start | bytes 1064960 | tf_op jit(solution)/shard_map/all_gather | solution.py:124
  68.6 17.4 %copy-start.25 = (f32[128,1280]{1,0:T(8,128)S(1)}, f32[128,1280]{1,0:T(8,128)}, u32[]{:S(2)}) copy-start(f32[128,1280]{1,0:T(8,128)} %convolution_add_fusion.4) | copy-start | bytes 1966084
  68.6 31.8 %collective-permute-start.4 = (bf16[256,1280]{1,0:T(8,128)(2,1)S(1)}, bf16[256,1280]{1,0:T(8,128)(2,1)S(1)}, u32[]{:S(2)}, u32[]{:S(2)}) collective-permute-start(bf16[256,1280]{1,0:T(8,128)(2,1)S(1)} %collective-permute-done.refs_2_), channel_id=1, source_target_pairs={{0,448},{64,0},{128,64},{192,128},{256,192},{320,256},{384,320},{4... | collective-permute-start | bytes 1966088 | tf_op jit(solution)/shard_map/ppermute | solution.py:40
  73.5 12.8 %collective-permute-start.7 = (bf16[256,1280]{1,0:T(8,128)(2,1)}, bf16[256,1280]{1,0:T(8,128)(2,1)S(1)}, u32[]{:S(2)}, u32[]{:S(2)}) collective-permute-start(bf16[256,1280]{1,0:T(8,128)(2,1)} %collective-permute-done.3.refs_15_), channel_id=1, source_target_pairs={{0,64},{64,128},{128,192},{192,256},{256,320},{320,384},{384,448},... | collective-permute-start | bytes 1966088 | tf_op jit(solution)/shard_map/ppermute | solution.py:41
  75.5 19.8 %collective-permute-start.5 = (bf16[256,1280]{1,0:T(8,128)(2,1)}, bf16[256,1280]{1,0:T(8,128)(2,1)S(1)}, u32[]{:S(2)}, u32[]{:S(2)}) collective-permute-start(bf16[256,1280]{1,0:T(8,128)(2,1)} %collective-permute-done.1.refs_3_), channel_id=1, source_target_pairs={{0,448},{64,0},{128,64},{192,128},{256,192},{320,256},{384,320},{4... | collective-permute-start | bytes 1966088 | tf_op jit(solution)/shard_map/ppermute | solution.py:43
  82.8 20.2 %collective-permute-start.6 = (bf16[256,1280]{1,0:T(8,128)(2,1)}, bf16[256,1280]{1,0:T(8,128)(2,1)S(1)}, u32[]{:S(2)}, u32[]{:S(2)}) collective-permute-start(bf16[256,1280]{1,0:T(8,128)(2,1)} %collective-permute-done.2.refs_14_), channel_id=1, source_target_pairs={{0,64},{64,128},{128,192},{192,256},{256,320},{320,384},{384,448},... | collective-permute-start | bytes 1966088 | tf_op jit(solution)/shard_map/ppermute | solution.py:44
  86.3 20.5 %copy-start.6 = (bf16[256,1280]{1,0:T(8,128)(2,1)}, bf16[256,1280]{1,0:T(8,128)(2,1)S(1)}, u32[]{:S(2)}) copy-start(bf16[256,1280]{1,0:T(8,128)(2,1)S(1)} %collective-permute-done.7.refs_13_) | copy-start | bytes 1966084
  86.4 30.6 %collective-permute-start.11 = (bf16[256,1280]{1,0:T(8,128)(2,1)S(1)}, bf16[256,1280]{1,0:T(8,128)(2,1)S(1)}, u32[]{:S(2)}, u32[]{:S(2)}) collective-permute-start(bf16[256,1280]{1,0:T(8,128)(2,1)S(1)} %collective-permute-done.7.refs_13_), channel_id=1, source_target_pairs={{0,64},{64,128},{128,192},{192,256},{256,320},{320,384},{384,448},... | collective-permute-start | bytes 1966088 | tf_op jit(solution)/shard_map/ppermute | solution.py:41
  95.2 11.6 %copy-start.8 = (bf16[256,1280]{1,0:T(8,128)(2,1)}, bf16[256,1280]{1,0:T(8,128)(2,1)S(1)}, u32[]{:S(2)}) copy-start(bf16[256,1280]{1,0:T(8,128)(2,1)S(1)} %collective-permute-done.5.refs_5_) | copy-start | bytes 1966084
  95.2 32.7 %collective-permute-start.9 = (bf16[256,1280]{1,0:T(8,128)(2,1)S(1)}, bf16[256,1280]{1,0:T(8,128)(2,1)S(1)}, u32[]{:S(2)}, u32[]{:S(2)}) collective-permute-start(bf16[256,1280]{1,0:T(8,128)(2,1)S(1)} %collective-permute-done.5.refs_5_), channel_id=1, source_target_pairs={{0,448},{64,0},{128,64},{192,128},{256,192},{320,256},{384,320},{4... | collective-permute-start | bytes 1966088 | tf_op jit(solution)/shard_map/ppermute | solution.py:43
  100.5 6.4 %copy-start.2 = (bf16[256,1280]{1,0:T(8,128)(2,1)}, bf16[256,1280]{1,0:T(8,128)(2,1)S(1)}, u32[]{:S(2)}) copy-start(bf16[256,1280]{1,0:T(8,128)(2,1)S(1)} %collective-permute-done.4.refs_4_) | copy-start | bytes 1966084
  100.5 21.9 %collective-permute-start.8 = (bf16[256,1280]{1,0:T(8,128)(2,1)S(1)}, bf16[256,1280]{1,0:T(8,128)(2,1)S(1)}, u32[]{:S(2)}, u32[]{:S(2)}) collective-permute-start(bf16[256,1280]{1,0:T(8,128)(2,1)S(1)} %collective-permute-done.4.refs_4_), channel_id=1, source_target_pairs={{0,448},{64,0},{128,64},{192,128},{256,192},{320,256},{384,320},{4... | collective-permute-start | bytes 1966088 | tf_op jit(solution)/shard_map/ppermute | solution.py:40
  102.9 3.9 %copy-start.10 = (bf16[256,1280]{1,0:T(8,128)(2,1)}, bf16[256,1280]{1,0:T(8,128)(2,1)S(1)}, u32[]{:S(2)}) copy-start(bf16[256,1280]{1,0:T(8,128)(2,1)S(1)} %collective-permute-done.6.refs_12_) | copy-start | bytes 1966084
  102.9 28.0 %collective-permute-start.10 = (bf16[256,1280]{1,0:T(8,128)(2,1)S(1)}, bf16[256,1280]{1,0:T(8,128)(2,1)S(1)}, u32[]{:S(2)}, u32[]{:S(2)}) collective-permute-start(bf16[256,1280]{1,0:T(8,128)(2,1)S(1)} %collective-permute-done.6.refs_12_), channel_id=1, source_target_pairs={{0,64},{64,128},{128,192},{192,256},{256,320},{320,384},{384,448},... | collective-permute-start | bytes 1966088 | tf_op jit(solution)/shard_map/ppermute | solution.py:44
  116.9 14.6 %copy-start.12 = (bf16[256,1280]{1,0:T(8,128)(2,1)}, bf16[256,1280]{1,0:T(8,128)(2,1)S(1)}, u32[]{:S(2)}) copy-start(bf16[256,1280]{1,0:T(8,128)(2,1)S(1)} %collective-permute-done.11.refs_11_) | copy-start | bytes 1966084
  116.9 28.1 %collective-permute-start.13 = (bf16[256,1280]{1,0:T(8,128)(2,1)S(1)}, bf16[256,1280]{1,0:T(8,128)(2,1)S(1)}, u32[]{:S(2)}, u32[]{:S(2)}) collective-permute-start(bf16[256,1280]{1,0:T(8,128)(2,1)S(1)} %collective-permute-done.11.refs_11_), channel_id=1, source_target_pairs={{0,64},{64,128},{128,192},{192,256},{256,320},{320,384},{384,448},... | collective-permute-start | bytes 1966088 | tf_op jit(solution)/shard_map/ppermute | solution.py:41
  122.4 9.2 %copy-start.4 = (bf16[256,1280]{1,0:T(8,128)(2,1)}, bf16[256,1280]{1,0:T(8,128)(2,1)S(1)}, u32[]{:S(2)}) copy-start(bf16[256,1280]{1,0:T(8,128)(2,1)S(1)} %collective-permute-done.8.refs_6_) | copy-start | bytes 1966084
  122.4 22.9 %collective-permute-start.12 = (bf16[256,1280]{1,0:T(8,128)(2,1)S(1)}, bf16[256,1280]{1,0:T(8,128)(2,1)S(1)}, u32[]{:S(2)}, u32[]{:S(2)}) collective-permute-start(bf16[256,1280]{1,0:T(8,128)(2,1)S(1)} %collective-permute-done.8.refs_6_), channel_id=1, source_target_pairs={{0,448},{64,0},{128,64},{192,128},{256,192},{320,256},{384,320},{4... | collective-permute-start | bytes 1966088 | tf_op jit(solution)/shard_map/ppermute | solution.py:40
  127.9 3.6 %copy-start.14 = (bf16[256,1280]{1,0:T(8,128)(2,1)}, bf16[256,1280]{1,0:T(8,128)(2,1)S(1)}, u32[]{:S(2)}) copy-start(bf16[256,1280]{1,0:T(8,128)(2,1)S(1)} %collective-permute-done.9.refs_7_) | copy-start | bytes 1966084
  131.0 0.8 copy-start.16
  131.8 13.9 %copy-start.22 = (f32[128,1280]{1,0:T(8,128)S(1)}, f32[128,1280]{1,0:T(8,128)}, u32[]{:S(2)}) copy-start(f32[128,1280]{1,0:T(8,128)} %reshape.86) | copy-start | bytes 1966084
  145.0 1.0 copy-start.18
  145.3 17.4 %copy-start.28 = (f32[2]{0:T(128)S(1)}, f32[2]{0:T(128)}, u32[]{:S(2)}) copy-start(f32[2]{0:T(128)} %param.9) | copy-start | bytes 28
  145.3 17.5 %copy-start.29 = (s32[2]{0:T(128)S(1)}, s32[2]{0:T(128)}, u32[]{:S(2)}) copy-start(s32[2]{0:T(128)} %param.8) | copy-start | bytes 28
  145.3 0.9 copy-start.20
  147.2 26.5 %all-to-all-start.1 = ((f32[64,3,128]{2,1,0:T(4,128)}), f32[64,3,128]{2,1,0:T(4,128)S(1)}, u32[]{:S(2)}, u32[]{:S(2)}) async-start(f32[64,3,128]{2,1,0:T(4,128)} %broadcast_in_dim.59), calls=%async_computation.1 | async-start | bytes 262144 | tf_op jit(solution)/shard_map/all_to_all | solution.py:22
  162.6 77.4 %all-gather.6.cloned.1.call-start = ((), (), s32[]{:S(2)}) async-start(), calls=%async_computation.6 | async-start | bytes 2949120 | tf_op jit(solution)/shard_map/all_gather | solution.py:149
  176.2 1.0 copy-start.1
  177.2 1.1 copy-start.3
  178.2 1.1 copy-start.5
  179.3 1.1 copy-start.7
  180.4 1.1 copy-start.9
  181.5 1.1 copy-start.11
  182.6 1.1 copy-start.13
  183.7 1.1 copy-start.15
  184.8 1.1 copy-start.17
  185.9 1.1 copy-start.19
  187.0 1.1 copy-start.21
  198.6 26.0 %copy-start.24 = (bf16[512,2,512]{2,0,1:T(8,128)(2,1)S(1)}, bf16[512,2,512]{2,0,1:T(8,128)(2,1)}, u32[]{:S(2)}) copy-start(bf16[512,2,512]{2,0,1:T(8,128)(2,1)} %copy.38) | copy-start | bytes 3145732
  219.6 20.5 %all-to-all-start.4 = ((bf16[32,16,512]{2,1,0:T(8,128)(2,1)}), bf16[32,16,512]{2,1,0:T(8,128)(2,1)S(1)}, u32[]{:S(2)}, u32[]{:S(2)}) async-start(bf16[32,16,512]{2,1,0:T(8,128)(2,1)} %broadcast_in_dim.60), calls=%async_computation.4 | async-start | bytes 1048576 | tf_op jit(solution)/shard_map/all_to_all | solution.py:22
  240.2 8.0 %copy-start.26 = (bf16[1024,1280]{1,0:T(8,128)(2,1)S(1)}, bf16[1024,1280]{1,0:T(8,128)(2,1)}, u32[]{:S(2)}) copy-start(bf16[1024,1280]{1,0:T(8,128)(2,1)} %all-gather.6.cloned.1.call-done) | copy-start | bytes 7864324
  248.2 2.6 %copy-start.27 = (bf16[128,4096]{1,0:T(8,128)(2,1)}, bf16[128,4096]{1,0:T(8,128)(2,1)S(1)}, u32[]{:S(2)}) copy-start(bf16[128,4096]{1,0:T(8,128)(2,1)S(1)} %fusion.12) | copy-start | bytes 3145732
  (1 other events, 0.8 us)
Sparse Core Ops, SparseCore 0:
  68.7 86.6 all-gather.7
  176.3 34.2 all-gather.5

commit v4 on v1

v4 whole, which is shorter than its diff:
```python
import jax
import jax.numpy as jnp
from jax import lax
from jax.experimental import pallas as pl
from jax.experimental.pallas import tpu as pltpu
from jax.sharding import PartitionSpec as P

SEQ_LEN = 64
LOSS_SCALE = 32.0
GATHERED = 10
LANES = 128
VMEM = pl.BlockSpec(memory_space=pltpu.VMEM)
HBM = pl.BlockSpec(memory_space=pl.ANY)


def pair_groups(n):
    return [[2 * i, 2 * i + 1] for i in range(n // 2)]


def core_groups(n):
    return [[2 * i + c for i in range(n // 2)] for c in range(2)]


def spread(block, size, groups=None, axis="vocab"):
    copies = jnp.broadcast_to(block[None], (size,) + block.shape)
    return lax.all_to_all(copies, axis, 0, 0, axis_index_groups=groups)


def hidden_share(hidden, n_dp, n_v):
    rows, d = hidden.shape
    share = rows // n_v
    mine = lax.dynamic_slice_in_dim(hidden, lax.axis_index("vocab") * share, share, 0)
    return mine.reshape(share, n_dp, d // n_dp).transpose(1, 0, 2)


def ring_blocks(block, n):
    right = [(i, (i + 1) % n) for i in range(n)]
    left = [(i, (i - 1) % n) for i in range(n)]
    half = block.shape[0] // 2
    got = {0: block}
    up = down = block
    for step in range(1, n // 2):
        down, up = lax.ppermute(down, "dp", left), lax.ppermute(up, "dp", right)
        got[step], got[n - step] = down, up
    got[n // 2] = jnp.concatenate(
        [lax.ppermute(down[:half], "dp", left), lax.ppermute(up[half:], "dp", right)]
    )
    return [got[k] for k in range(n)]


def along_lanes(column, rows):
    return jnp.transpose(jnp.broadcast_to(column, (rows, LANES)))[:1]


def stats_kernel(teacher_ref, logits_ref, out_ref):
    rows = logits_ref.shape[0]
    logits = logits_ref[...]
    top = jnp.max(logits, axis=1, keepdims=True)
    shifted = logits - top
    expd = jnp.exp(shifted)
    total = jnp.sum(expd, axis=1, keepdims=True)
    gaps = expd * (shifted - teacher_ref[...].astype(jnp.float32))
    weighted = jnp.sum(gaps, axis=1, keepdims=True)
    stats = jnp.concatenate([along_lanes(v, rows) for v in (top, total, weighted)], axis=0)
    out_ref[...] = jnp.broadcast_to(stats[None], out_ref.shape)


def grads_kernel(every_ref, weight_ref, teacher_ref, logits_ref, out_ref):
    rows, width = logits_ref.shape
    tops, sums, weighteds = (every_ref[:, i, :] for i in range(3))
    top = jnp.max(tops, axis=0, keepdims=True)
    lower = tops - top
    scale = jnp.exp(lower)
    total = jnp.sum(sums * scale, axis=0, keepdims=True)
    weighted = jnp.sum(scale * (weighteds + lower * sums), axis=0, keepdims=True)
    factor = LOSS_SCALE * weight_ref[...] / total
    top, factor, centre = (
        jnp.transpose(jnp.broadcast_to(v, (LANES, rows))) for v in (top, factor, weighted / total)
    )
    for c in range(width // LANES):
        cols = pl.ds(c * LANES, LANES)
        shifted = logits_ref[:, cols] - top
        gap = shifted - teacher_ref[:, cols].astype(jnp.float32) - centre
        out_ref[:, cols] = (factor * jnp.exp(shifted) * gap).astype(jnp.bfloat16)


def terms_kernel(me_ref, grads_ref, gathered_ref, *refs):
    pieces, (out_ref, held, kept, sems, piece_sems) = refs[:-5], refs[-5:]
    blocks = len(pieces)
    deep = held.shape[1]
    copies = [
        pltpu.make_async_copy(gathered_ref.at[pl.ds(j * deep, deep)], held.at[j], sems.at[j])
        for j in range(blocks)
    ]
    piece_copies = [
        pltpu.make_async_copy(piece, kept.at[j], piece_sems.at[j]) for j, piece in enumerate(pieces)
    ]
    for j in range(blocks):
        copies[j].start()
        piece_copies[j].start()
    grads = grads_ref[...]
    contract = (((1,), (1,)), ((), ()))
    for j in range(blocks):
        copies[j].wait()
        out_ref[j, :, :deep] = lax.dot_general(
            grads, held[j], contract, preferred_element_type=jnp.float32
        )
        piece_copies[j].wait()
        out_ref[lax.rem(me_ref[0] + j, blocks), :, deep:] = lax.dot_general(
            grads, kept[j], contract, preferred_element_type=jnp.float32
        )


def hidden_terms(me, grads, gathered, pieces):
    rows, width = grads.shape
    blocks = len(pieces)
    deep, rest = gathered.shape[0] // blocks, pieces[0].shape[0]
    d = blocks * (deep + rest)
    return pl.pallas_call(
        terms_kernel,
        out_shape=jax.ShapeDtypeStruct((blocks, rows, deep + rest), jnp.float32),
        in_specs=[pl.BlockSpec(memory_space=pltpu.SMEM), VMEM, HBM] + [HBM] * blocks,
        out_specs=VMEM,
        scratch_shapes=[
            pltpu.VMEM((blocks, deep, width), gathered.dtype),
            pltpu.VMEM((blocks, rest, width), gathered.dtype),
            pltpu.SemaphoreType.DMA((blocks,)),
            pltpu.SemaphoreType.DMA((blocks,)),
        ],
        compiler_params=pltpu.CompilerParams(vmem_limit_bytes=56 * 2**20),
        cost_estimate=pl.CostEstimate(
            flops=2 * rows * d * width, bytes_accessed=2 * d * width + 4 * rows * d, transcendentals=0
        ),
    )(me.reshape(1), grads, gathered, *pieces)


def row_kernel(kernel, shape, dtype, *args):
    size = args[-1].size
    return pl.pallas_call(
        kernel,
        out_shape=jax.ShapeDtypeStruct(shape, dtype),
        in_specs=[VMEM] * len(args),
        out_specs=VMEM,
        compiler_params=pltpu.CompilerParams(vmem_limit_bytes=16 * 2**20),
        cost_estimate=pl.CostEstimate(flops=8 * size, bytes_accessed=8 * size, transcendentals=size),
    )(*args)


def sum_terms(terms, n_v):
    blocks, rows, d = terms.shape
    many = n_v // 2
    swapped = lax.all_to_all(
        terms.reshape(2, blocks // 2, rows, d), "vocab", 0, 0, axis_index_groups=pair_groups(n_v)
    )
    mine = (swapped[0] + swapped[1]).astype(jnp.bfloat16)
    mine = mine.reshape(many, blocks // 2 * rows // many, d)
    parts = lax.all_to_all(mine, "vocab", 0, 0, axis_index_groups=core_groups(n_v))
    total = jnp.sum(parts.astype(jnp.float32), axis=0).astype(jnp.bfloat16)
    whole = spread(total, many, core_groups(n_v))
    both = spread(whole, 2, pair_groups(n_v))
    return both.reshape(blocks, rows, d)


def body(hidden, head_weight, teacher_logprobs, lengths, seq_weights):
    n_dp, n_v = lax.axis_size("dp"), lax.axis_size("vocab")
    me = lax.axis_index("dp")
    depth, width = head_weight.shape
    tok_rows = hidden.shape[0]
    deep = depth * GATHERED // 16
    gathered = lax.all_gather(head_weight[:deep], "dp", axis=0, tiled=True)
    pieces = ring_blocks(head_weight[deep:], n_dp)
    teacher = lax.all_to_all(teacher_logprobs, "vocab", split_axis=1, concat_axis=0, tiled=True)
    share = lax.all_to_all(hidden_share(hidden, n_dp, n_v), "dp", 0, 0)
    everyone = spread(share, n_v)

    rows = jnp.arange(tok_rows, dtype=jnp.int32)
    sequence = rows // SEQ_LEN
    position = rows % SEQ_LEN
    member = sequence[:, None] == jnp.arange(lengths.shape[0], dtype=jnp.int32)[None, :]
    row_length = jnp.sum(jnp.where(member, lengths[None, :], 0), axis=1)
    row_weight = jnp.sum(jnp.where(member, seq_weights[None, :], jnp.float32(0.0)), axis=1)
    weight = jnp.where(position < row_length, row_weight, jnp.float32(0.0)).reshape(1, tok_rows)

    features = hidden.reshape(tok_rows, n_dp, depth)
    first = features[:, :, :deep].reshape(tok_rows, n_dp * deep)
    logits = None
    for k in range(n_dp):
        feats = lax.dynamic_slice_in_dim(
            hidden, lax.rem(me + k, n_dp) * depth + deep, depth - deep, 1
        )
        term = jnp.dot(feats, pieces[k], preferred_element_type=jnp.float32)
        logits = term if logits is None else logits + term
    gathered, everyone, teacher, logits, weight, first = lax.optimization_barrier(
        (gathered, everyone, teacher, logits, weight, first)
    )
    logits = logits + jnp.dot(first, gathered, preferred_element_type=jnp.float32)
    stats = row_kernel(stats_kernel, (n_v, 3, tok_rows), jnp.float32, teacher, logits)
    every = lax.all_to_all(stats, "vocab", 0, 0)
    grad_logits = row_kernel(
        grads_kernel, logits.shape, jnp.bfloat16, every, weight, teacher, logits
    )

    everyone, grad_logits = lax.optimization_barrier((everyone, grad_logits))
    slices = everyone.transpose(1, 0, 2, 3).reshape(n_dp * tok_rows, depth)
    all_grads = lax.all_gather(grad_logits, "dp", axis=0, tiled=True)
    summed = sum_terms(hidden_terms(me, grad_logits, gathered, pieces), n_v)
    grad_hidden = jnp.concatenate([summed[k] for k in range(n_dp)], axis=1)
    grad_head = lax.dot_general(
        slices, all_grads, (((0,), (0,)), ((), ())), preferred_element_type=jnp.float32
    )
    return grad_hidden, grad_head.astype(jnp.bfloat16)


def solution(mesh):
    placed = (P("dp", None), P("dp", "vocab"), P(("dp", "vocab"), None), P("dp"), P("dp"))
    return jax.shard_map(
        body,
        mesh=mesh,
        in_specs=placed,
        out_specs=(P("dp", None), P("dp", "vocab")),
        check_vma=False,
    )
```

time: 286 us -> 233 us (0.81)
  waiting for transfers between devices: 184 us -> 52.3 us
  blocking collectives: 12.9 us -> 54.1 us
  starting transfers between devices: 43.6 us -> 68.7 us
  Pallas kernels: 0 us -> 12.8 us
    all_gather x1, waiting for transfers between devices: 98.4 us -> 0.01 us  [body(): gathered = lax.all_gather(head_weight[:deep], 'dp', axis=0, tiled=True)]
    all_to_all x5 -> x3, waiting for transfers between devices: 70.9 us -> 23.6 us  [the longest x2 15.9 us: spread(): return lax.all_to_all(copies, axis, 0, 0, axis_index_groups=groups)]
    all_to_all x2 -> x4, blocking collectives: 12.9 us -> 54.1 us  [the longest x1 19.9 us: body(): every = lax.all_to_all(stats, 'vocab', 0, 0)]
    ppermute x0 -> x8, starting transfers between devices: none -> 33.5 us  [the longest x6 27 us: ring_blocks(): down, up = (lax.ppermute(down, 'dp', left), lax.ppermute(up, 'dp', right))]
    ppermute x0 -> x8, waiting for transfers between devices: none -> 28.6 us  [the longest x6 21.1 us: ring_blocks(): down, up = (lax.ppermute(down, 'dp', left), lax.ppermute(up, 'dp', right))]
    all_to_all x1, waiting for transfers between devices: 13.5 us -> 0.01 us  [body(): lax.all_to_all(teacher_logprobs, 'vocab', split_axis=1, concat_axis=0, ti...]
    pallas_call x0 -> x3, Pallas kernels: none -> 12.8 us  [the longest x1 11.3 us: hidden_terms(): pl.pallas_call(terms_kernel, out_shape=jax.ShapeDtypeStruct((blocks, rows...]
    all_to_all x5 -> x3, starting transfers between devices: 31.9 us -> 20.4 us  [the longest x2 16.5 us: spread(): return lax.all_to_all(copies, axis, 0, 0, axis_index_groups=groups)]
  transfers between devices with their start and end apart: 8 -> 14, of which waited for: 7 -> 7; matrix products, arithmetic and copies ran while one was open for 4% -> 7% of each run, Pallas kernels for 0% -> 5%
where the time goes in v4:
time: 233 us; the launch traced here: 232 us
  starting transfers between devices  68.7 us (29%)
  blocking collectives  54.1 us (23%)
  waiting for transfers between devices  52.3 us (22%)
  matrix products  19.1 us (8%)
  between operations  14.6 us (6%)
  Pallas kernels  12.8 us (5%)
  local copies, waits for them, and re-layouts  9.87 us (4%)
    ppermute x6, starting transfers between devices, ring_blocks(): down, up = (lax.ppermute(down, 'dp', left), lax.ppermute(up, 'dp', right))  27 us
    ppermute x6, waiting for transfers between devices, ring_blocks(): down, up = (lax.ppermute(down, 'dp', left), lax.ppermute(up, 'dp', right))  21.1 us
    all_to_all x1, blocking collectives, body(): every = lax.all_to_all(stats, 'vocab', 0, 0)  19.9 us
    all_to_all x1, blocking collectives, sum_terms(): lax.all_to_all(mine, 'vocab', 0, 0, axis_index_groups=core_groups(n_v))  19.5 us
    all_to_all x2, starting transfers between devices, spread(): return lax.all_to_all(copies, axis, 0, 0, axis_index_groups=groups)  16.5 us
    all_to_all x2, waiting for transfers between devices, spread(): return lax.all_to_all(copies, axis, 0, 0, axis_index_groups=groups)  15.9 us
    all_to_all x1, starting transfers between devices, body(): lax.all_to_all(teacher_logprobs, 'vocab', split_axis=1, concat_axis=0, ti...  14.8 us
    pallas_call x1, Pallas kernels, hidden_terms(): pl.pallas_call(terms_kernel, out_shape=jax.ShapeDtypeStruct((blocks, rows...  11.3 us
  transfers between devices with their start and end apart: 14, of which 7 were waited for; matrix products, arithmetic and copies ran while one was open for 7% of the time, Pallas kernels for 5%

profile of v4, /device:TPU:1, one launch (start us, length us, event | category | flops | bytes accessed | tf_op | source)
XLA Modules:
  0.0 231.9 jit_solution(11204608231872981048)
XLA Ops:
  7.2 2.2 slice.45
  9.6 4.8 %collective-permute-start.4 = (bf16[192,1280]{1,0:T(8,128)(2,1)S(1)}, bf16[192,1280]{1,0:T(8,128)(2,1)}, u32[]{:S(2)}, u32[]{:S(2)}) collective-permute-start(bf16[192,1280]{1,0:T(8,128)(2,1)S(1)} %slice.46.refs_0_), channel_id=1, source_target_pairs={{0,64},{64,128},{128,192},{192,256},{256,320},{320,384},{384,448},... | collective-permute-start | bytes 1474568 | tf_op jit(solution)/shard_map/ppermute | solution.py:43
  14.4 8.6 %collective-permute-start = (bf16[192,1280]{1,0:T(8,128)(2,1)S(1)}, bf16[192,1280]{1,0:T(8,128)(2,1)}, u32[]{:S(2)}, u32[]{:S(2)}) collective-permute-start(bf16[192,1280]{1,0:T(8,128)(2,1)S(1)} %slice.46.refs_0_), channel_id=1, source_target_pairs={{0,448},{64,0},{128,64},{192,128},{256,192},{320,256},{384,320},{4... | collective-permute-start | bytes 1474568 | tf_op jit(solution)/shard_map/ppermute | solution.py:43
  23.0 0.6 constant_dynamic-slice_fusion
  23.6 3.9 %all-to-all-start = ((bf16[8,2,512]{2,1,0:T(2,128)(2,1)}), bf16[8,2,512]{2,1,0:T(2,128)(2,1)S(1)}, u32[]{:S(2)}, u32[]{:S(2)}) async-start(bf16[8,2,512]{2,1,0:T(2,128)(2,1)} %bitcast.2), calls=%async_computation | async-start | bytes 32768 | tf_op jit(solution)/shard_map/all_to_all | solution.py:173
  27.6 0.3 fusion.22
  27.9 7.7 %all-to-all-done = bf16[8,2,512]{2,1,0:T(2,128)(2,1)S(1)} async-done(((bf16[8,2,512]{2,1,0:T(2,128)(2,1)}), bf16[8,2,512]{2,1,0:T(2,128)(2,1)S(1)}, u32[]{:S(2)}, u32[]{:S(2)}) %all-to-all-start) | async-done | bytes 16416 | tf_op jit(solution)/shard_map/all_to_all | solution.py:173
  35.5 14.8 %all-to-all-start.2 = ((bf16[2,64,1280]{2,0,1:T(2,128)(2,1)}), bf16[2,64,1280]{2,0,1:T(2,128)(2,1)}, u32[]{:S(2)}, u32[]{:S(2)}) async-start(bf16[2,64,1280]{2,0,1:T(2,128)(2,1)} %bitcast.72), calls=%async_computation.2 | async-start | bytes 655360 | tf_op jit(solution)/shard_map/all_to_all | solution.py:172
  50.4 0.7 copy.14
  51.1 0.9 slice.62
  52.1 2.2 collective-permute-start.5
  54.3 4.9 %collective-permute-start.1 = (bf16[192,1280]{1,0:T(8,128)(2,1)}, bf16[192,1280]{1,0:T(8,128)(2,1)S(1)}, u32[]{:S(2)}, u32[]{:S(2)}) collective-permute-start(bf16[192,1280]{1,0:T(8,128)(2,1)} %collective-permute-done.refs_1_), channel_id=1, source_target_pairs={{0,448},{64,0},{128,64},{192,128},{256,192},{320,256},{384,320},{4... | collective-permute-start | bytes 1474568 | tf_op jit(solution)/shard_map/ppermute | solution.py:43
  59.3 1.4 convolution_add_fusion.3
  60.7 19.0 %collective-permute-done.5.refs_6_ = bf16[192,1280]{1,0:T(8,128)(2,1)} collective-permute-done((bf16[192,1280]{1,0:T(8,128)(2,1)}, bf16[192,1280]{1,0:T(8,128)(2,1)}, u32[]{:S(2)}, u32[]{:S(2)}) %collective-permute-start.5) | collective-permute-done | bytes 491552 | tf_op jit(solution)/shard_map/ppermute | solution.py:43
  79.7 1.9 collective-permute-start.6
  81.6 4.6 %collective-permute-start.2 = (bf16[192,1280]{1,0:T(8,128)(2,1)S(1)}, bf16[192,1280]{1,0:T(8,128)(2,1)S(1)}, u32[]{:S(2)}, u32[]{:S(2)}) collective-permute-start(bf16[192,1280]{1,0:T(8,128)(2,1)S(1)} %collective-permute-done.1.refs_2_), channel_id=1, source_target_pairs={{0,448},{64,0},{128,64},{192,128},{256,192},{320,256},{384,320},{4... | collective-permute-start | bytes 1474568 | tf_op jit(solution)/shard_map/ppermute | solution.py:43
  86.2 2.0 broadcast_in_dim.50
  88.2 11.5 %all-to-all-start.1 = ((bf16[64,8,2,512]{3,2,1,0:T(2,128)(2,1)}), bf16[64,8,2,512]{3,2,1,0:T(2,128)(2,1)S(1)}, u32[]{:S(2)}, u32[]{:S(2)}) async-start(bf16[64,8,2,512]{3,2,1,0:T(2,128)(2,1)} %broadcast_in_dim.50), calls=%async_computation.1 | async-start | bytes 2097152 | tf_op jit(solution)/shard_map/all_to_all | solution.py:26
  99.7 2.2 fusion.12
  101.9 1.1 all_to_all.40.teacher_ref
  103.0 1.2 convolution_add_fusion.2
  104.2 2.1 collective-permute-done.6.refs_5_
  106.3 1.9 collective-permute-start.7
  108.3 4.6 %collective-permute-start.3 = (bf16[96,1280]{1,0:T(8,128)(2,1)S(1)}, bf16[96,1280]{1,0:T(8,128)(2,1)S(1)}, u32[]{:S(2)}, u32[]{:S(2)}) collective-permute-start(bf16[96,1280]{1,0:T(8,128)(2,1)S(1)} %slice.60), channel_id=1, source_target_pairs={{0,448},{64,0},{128,64},{192,128},{256,192},{320,256},{384,320},{4... | collective-permute-start | bytes 737288 | tf_op jit(solution)/shard_map/ppermute | solution.py:46
  112.9 1.4 fusion.14
  114.3 7.0 %collective-permute-done.3 = bf16[96,1280]{1,0:T(8,128)(2,1)S(1)} collective-permute-done((bf16[96,1280]{1,0:T(8,128)(2,1)S(1)}, bf16[96,1280]{1,0:T(8,128)(2,1)S(1)}, u32[]{:S(2)}, u32[]{:S(2)}) %collective-permute-start.3) | collective-permute-done | bytes 245792 | tf_op jit(solution)/shard_map/ppermute | solution.py:46
  121.3 0.5 collective-permute-done.7
  121.9 1.3 fusion.17
  123.2 1.2 fusion.2
  124.4 1.2 fusion.1
  125.7 2.0 all-to-all-done.1
  127.6 4.1 %fusion.33 = f32[128,1280]{1,0:T(8,128)S(1)} fusion(bf16[128,2560]{0,1:T(8,128)(2,1)} %bitcast.70, bf16[2560,1280]{1,0:T(8,128)(2,1)} %all-gather.3.cloned.1.call-done.gathered_ref), kind=kOutput, calls=%fused_computation.59 | convolution fusion | flops 838860800 | bytes 7864320 | tf_op jit(solution)/shard_map/dot_general | solution.py:196
  131.8 0.1 add.167.logits_ref
  131.9 0.4 shard_map.68
  132.3 19.9 %all_to_all.54.every_ref = f32[64,3,128]{2,1,0:T(4,128)S(1)} all-to-all(f32[64,3,128]{2,1,0:T(4,128)S(1)} %shard_map.68), channel_id=1, replica_groups=mesh['dp'=8,'vocab'=64] {'vocab'}, dimensions={0} | all-to-all | bytes 196608 | tf_op jit(solution)/shard_map/all_to_all | solution.py:198
  152.2 1.0 shard_map.69.grads_ref
  153.3 11.3 %shard_map.70 = f32[8,128,512]{2,1,0:T(8,128)} custom-call(s32[1]{0:T(128)} %bitcast.me_ref, bf16[128,1280]{1,0:T(8,128)(2,1)} %shard_map.69.grads_ref, bf16[2560,1280]{1,0:T(8,128)(2,1)} %all-gather.3.cloned.1.call-done.gathered_ref, bf16[192,1280]{1,0:T(8,128)(2,1)} %copy-done.6, bf16[192,1280]{1,0:T(8,128)(2,1)} %collective-permute-done.refs_1_, ...), custom_call_target="tpu_custom_call" | custom-call | flops 1342177280 | bytes 12582912 | tf_op jit(solution)/shard_map/pallas_call | solution.py:119
  164.6 6.7 %all_to_all.55 = f32[2,4,128,512]{3,2,1,0:T(8,128)S(1)} all-to-all(f32[2,4,128,512]{3,2,1,0:T(8,128)} %bitcast.59), channel_id=1, replica_groups={{0,1},{2,3},{4,5},{6,7},{8,9},{10,11},{12,13},{14,15},{16,17},{18,19},{..., dimensions={0} | all-to-all | bytes 4194304 | tf_op jit(solution)/shard_map/all_to_all | solution.py:152
  171.4 0.2 fusion.3
  171.5 19.5 %all_to_all.56 = bf16[32,16,512]{2,1,0:T(8,128)(2,1)S(1)} all-to-all(bf16[32,16,512]{2,1,0:T(8,128)(2,1)S(1)} %bitcast.71), channel_id=1, replica_groups={{0,2,4,6,8,10,12,14,16,18,20,22,24,26,28,30,32,34,36,38,40,42,44,46,48,..., dimensions={0} | all-to-all | bytes 1048576 | tf_op jit(solution)/shard_map/all_to_all | solution.py:157
  191.1 0.9 broadcast_in_dim.56
  192.0 5.0 %all-to-all-start.6 = ((bf16[32,16,512]{2,1,0:T(8,128)(2,1)}), bf16[32,16,512]{2,1,0:T(8,128)(2,1)S(1)}, u32[]{:S(2)}, u32[]{:S(2)}) async-start(bf16[32,16,512]{2,1,0:T(8,128)(2,1)} %broadcast_in_dim.56), calls=%async_computation.6 | async-start | bytes 1048576 | tf_op jit(solution)/shard_map/all_to_all | solution.py:26
  197.0 0.7 copy.15
  197.7 0.4 reshape.94
  198.2 14.0 %all-to-all-done.6 = bf16[32,16,512]{2,1,0:T(8,128)(2,1)S(1)} async-done(((bf16[32,16,512]{2,1,0:T(8,128)(2,1)}), bf16[32,16,512]{2,1,0:T(8,128)(2,1)S(1)}, u32[]{:S(2)}, u32[]{:S(2)}) %all-to-all-start.6) | async-done | bytes 524320 | tf_op jit(solution)/shard_map/all_to_all | solution.py:26
  212.1 0.1 broadcast_in_dim.57
  212.2 7.9 %all_to_all.57 = bf16[2,32,16,512]{3,2,1,0:T(8,128)(2,1)S(1)} all-to-all(bf16[2,32,16,512]{3,2,1,0:T(8,128)(2,1)S(1)} %broadcast_in_dim.57), channel_id=1, replica_groups={{0,1},{2,3},{4,5},{6,7},{8,9},{10,11},{12,13},{14,15},{16,17},{18,19},{..., dimensions={0} | all-to-all | bytes 2097152 | tf_op jit(solution)/shard_map/all_to_all | solution.py:26
  220.3 4.7 %convolution_convert_fusion = bf16[512,1280]{1,0:T(8,128)(2,1)} fusion(bf16[1024,512]{1,0:T(8,128)(2,1)S(1)} %reshape.94, bf16[1024,1280]{1,0:T(8,128)(2,1)} %all-gather.5.cloned.1.call-done), kind=kOutput, calls=%fused_computation | convolution fusion | flops 1342832640 | bytes 4980736 | tf_op jit(solution)/shard_map/dot_general | solution.py:208
  (51 shorter events, 0.7 us)
Async XLA Ops:
  7.2 2.3 %copy-start.4 = (bf16[512,1280]{1,0:T(8,128)(2,1)S(1)}, bf16[512,1280]{1,0:T(8,128)(2,1)}, u32[]{:S(2)}) copy-start(bf16[512,1280]{1,0:T(8,128)(2,1)} %param.6) | copy-start | bytes 3932164
  7.2 15.8 %copy-start.5 = (bf16[128,4096]{1,0:T(8,128)(2,1)S(1)}, bf16[128,4096]{1,0:T(8,128)(2,1)}, u32[]{:S(2)}) copy-start(bf16[128,4096]{1,0:T(8,128)(2,1)} %param.5) | copy-start | bytes 3145732
  7.2 43.1 %copy-start.9 = (f32[2]{0:T(128)S(1)}, f32[2]{0:T(128)}, u32[]{:S(2)}) copy-start(f32[2]{0:T(128)} %param.9) | copy-start | bytes 28
  7.2 120.4 %all-gather.3.cloned.1.call-start = ((), (), s32[]{:S(2)}) async-start(), calls=%async_computation.8 | async-start | bytes 7372800 | tf_op jit(solution)/shard_map/all_gather | solution.py:170
  9.6 42.4 %copy-start.6 = (bf16[192,1280]{1,0:T(8,128)(2,1)}, bf16[192,1280]{1,0:T(8,128)(2,1)S(1)}, u32[]{:S(2)}) copy-start(bf16[192,1280]{1,0:T(8,128)(2,1)S(1)} %slice.46.refs_0_) | copy-start | bytes 1474564
  9.6 42.5 %collective-permute-start.4 = (bf16[192,1280]{1,0:T(8,128)(2,1)S(1)}, bf16[192,1280]{1,0:T(8,128)(2,1)}, u32[]{:S(2)}, u32[]{:S(2)}) collective-permute-start(bf16[192,1280]{1,0:T(8,128)(2,1)S(1)} %slice.46.refs_0_), channel_id=1, source_target_pairs={{0,64},{64,128},{128,192},{192,256},{256,320},{320,384},{384,448},... | collective-permute-start | bytes 1474568 | tf_op jit(solution)/shard_map/ppermute | solution.py:43
  14.4 39.9 %collective-permute-start = (bf16[192,1280]{1,0:T(8,128)(2,1)S(1)}, bf16[192,1280]{1,0:T(8,128)(2,1)}, u32[]{:S(2)}, u32[]{:S(2)}) collective-permute-start(bf16[192,1280]{1,0:T(8,128)(2,1)S(1)} %slice.46.refs_0_), channel_id=1, source_target_pairs={{0,448},{64,0},{128,64},{192,128},{256,192},{320,256},{384,320},{4... | collective-permute-start | bytes 1474568 | tf_op jit(solution)/shard_map/ppermute | solution.py:43
  23.6 11.9 %all-to-all-start = ((bf16[8,2,512]{2,1,0:T(2,128)(2,1)}), bf16[8,2,512]{2,1,0:T(2,128)(2,1)S(1)}, u32[]{:S(2)}, u32[]{:S(2)}) async-start(bf16[8,2,512]{2,1,0:T(2,128)(2,1)} %bitcast.2), calls=%async_computation | async-start | bytes 32768 | tf_op jit(solution)/shard_map/all_to_all | solution.py:173
  27.6 24.4 %copy-start.10 = (s32[2]{0:T(128)S(1)}, s32[2]{0:T(128)}, u32[]{:S(2)}) copy-start(s32[2]{0:T(128)} %param.8) | copy-start | bytes 28
  35.5 50.6 %all-to-all-start.2 = ((bf16[2,64,1280]{2,0,1:T(2,128)(2,1)}), bf16[2,64,1280]{2,0,1:T(2,128)(2,1)}, u32[]{:S(2)}, u32[]{:S(2)}) async-start(bf16[2,64,1280]{2,0,1:T(2,128)(2,1)} %bitcast.72), calls=%async_computation.2 | async-start | bytes 655360 | tf_op jit(solution)/shard_map/all_to_all | solution.py:172
  52.1 27.6 %collective-permute-start.5 = (bf16[192,1280]{1,0:T(8,128)(2,1)}, bf16[192,1280]{1,0:T(8,128)(2,1)}, u32[]{:S(2)}, u32[]{:S(2)}) collective-permute-start(bf16[192,1280]{1,0:T(8,128)(2,1)} %collective-permute-done.4.refs_7_), channel_id=1, source_target_pairs={{0,64},{64,128},{128,192},{192,256},{256,320},{320,384},{384,448},... | collective-permute-start | bytes 1474568 | tf_op jit(solution)/shard_map/ppermute | solution.py:43
  54.3 27.2 %collective-permute-start.1 = (bf16[192,1280]{1,0:T(8,128)(2,1)}, bf16[192,1280]{1,0:T(8,128)(2,1)S(1)}, u32[]{:S(2)}, u32[]{:S(2)}) collective-permute-start(bf16[192,1280]{1,0:T(8,128)(2,1)} %collective-permute-done.refs_1_), channel_id=1, source_target_pairs={{0,448},{64,0},{128,64},{192,128},{256,192},{320,256},{384,320},{4... | collective-permute-start | bytes 1474568 | tf_op jit(solution)/shard_map/ppermute | solution.py:43
  79.7 26.6 %collective-permute-start.6 = (bf16[192,1280]{1,0:T(8,128)(2,1)}, bf16[192,1280]{1,0:T(8,128)(2,1)S(1)}, u32[]{:S(2)}, u32[]{:S(2)}) collective-permute-start(bf16[192,1280]{1,0:T(8,128)(2,1)} %collective-permute-done.5.refs_6_), channel_id=1, source_target_pairs={{0,64},{64,128},{128,192},{192,256},{256,320},{320,384},{384,448},... | collective-permute-start | bytes 1474568 | tf_op jit(solution)/shard_map/ppermute | solution.py:43
  81.6 22.6 %copy-start.7 = (bf16[192,1280]{1,0:T(8,128)(2,1)}, bf16[192,1280]{1,0:T(8,128)(2,1)S(1)}, u32[]{:S(2)}) copy-start(bf16[192,1280]{1,0:T(8,128)(2,1)S(1)} %collective-permute-done.1.refs_2_) | copy-start | bytes 1474564
  81.6 26.7 %collective-permute-start.2 = (bf16[192,1280]{1,0:T(8,128)(2,1)S(1)}, bf16[192,1280]{1,0:T(8,128)(2,1)S(1)}, u32[]{:S(2)}, u32[]{:S(2)}) collective-permute-start(bf16[192,1280]{1,0:T(8,128)(2,1)S(1)} %collective-permute-done.1.refs_2_), channel_id=1, source_target_pairs={{0,448},{64,0},{128,64},{192,128},{256,192},{320,256},{384,320},{4... | collective-permute-start | bytes 1474568 | tf_op jit(solution)/shard_map/ppermute | solution.py:43
  88.2 39.5 %all-to-all-start.1 = ((bf16[64,8,2,512]{3,2,1,0:T(2,128)(2,1)}), bf16[64,8,2,512]{3,2,1,0:T(2,128)(2,1)S(1)}, u32[]{:S(2)}, u32[]{:S(2)}) async-start(bf16[64,8,2,512]{3,2,1,0:T(2,128)(2,1)} %broadcast_in_dim.50), calls=%async_computation.1 | async-start | bytes 2097152 | tf_op jit(solution)/shard_map/all_to_all | solution.py:26
  99.6 120.7 %all-gather.5.cloned.1.call-start = ((), (), s32[]{:S(2)}) async-start(), calls=%async_computation.9 | async-start | bytes 2949120 | tf_op jit(solution)/shard_map/all_gather | solution.py:205
  106.3 18.1 %copy-start = (bf16[192,1280]{1,0:T(8,128)(2,1)}, bf16[192,1280]{1,0:T(8,128)(2,1)S(1)}, u32[]{:S(2)}) copy-start(bf16[192,1280]{1,0:T(8,128)(2,1)S(1)} %collective-permute-done.6.refs_5_) | copy-start | bytes 1474564
  106.3 15.5 %collective-permute-start.7 = (bf16[96,1280]{1,0:T(8,128)(2,1)S(1)}, bf16[96,1280]{1,0:T(8,128)(2,1)S(1)}, u32[]{:S(2)}, u32[]{:S(2)}) collective-permute-start(bf16[96,1280]{1,0:T(8,128)(2,1)S(1)} %slice.61), channel_id=1, source_target_pairs={{0,64},{64,128},{128,192},{192,256},{256,320},{320,384},{384,448},... | collective-permute-start | bytes 737288 | tf_op jit(solution)/shard_map/ppermute | solution.py:46
  108.3 16.2 %copy-start.1 = (bf16[192,1280]{1,0:T(8,128)(2,1)}, bf16[192,1280]{1,0:T(8,128)(2,1)S(1)}, u32[]{:S(2)}) copy-start(bf16[192,1280]{1,0:T(8,128)(2,1)S(1)} %collective-permute-done.2.refs_3_) | copy-start | bytes 1474564
  108.3 13.0 %collective-permute-start.3 = (bf16[96,1280]{1,0:T(8,128)(2,1)S(1)}, bf16[96,1280]{1,0:T(8,128)(2,1)S(1)}, u32[]{:S(2)}, u32[]{:S(2)}) collective-permute-start(bf16[96,1280]{1,0:T(8,128)(2,1)S(1)} %slice.60), channel_id=1, source_target_pairs={{0,448},{64,0},{128,64},{192,128},{256,192},{320,256},{384,320},{4... | collective-permute-start | bytes 737288 | tf_op jit(solution)/shard_map/ppermute | solution.py:46
  114.3 10.2 %copy-start.3 = (f32[128,1280]{1,0:T(8,128)S(1)}, f32[128,1280]{1,0:T(8,128)}, u32[]{:S(2)}) copy-start(f32[128,1280]{1,0:T(8,128)} %fusion.12) | copy-start | bytes 1966084
  121.9 3.8 %copy-start.2 = (bf16[192,1280]{1,0:T(8,128)(2,1)}, bf16[192,1280]{1,0:T(8,128)(2,1)S(1)}, u32[]{:S(2)}) copy-start(bf16[192,1280]{1,0:T(8,128)(2,1)S(1)} %constant_dynamic-update-slice_fusion.refs_4_) | copy-start | bytes 1474564
  192.0 20.1 %all-to-all-start.6 = ((bf16[32,16,512]{2,1,0:T(8,128)(2,1)}), bf16[32,16,512]{2,1,0:T(8,128)(2,1)S(1)}, u32[]{:S(2)}, u32[]{:S(2)}) async-start(bf16[32,16,512]{2,1,0:T(8,128)(2,1)} %broadcast_in_dim.56), calls=%async_computation.6 | async-start | bytes 1048576 | tf_op jit(solution)/shard_map/all_to_all | solution.py:26
  220.3 4.8 %copy-start.8 = (bf16[128,4096]{1,0:T(8,128)(2,1)}, bf16[128,4096]{1,0:T(8,128)(2,1)S(1)}, u32[]{:S(2)}) copy-start(bf16[128,4096]{1,0:T(8,128)(2,1)S(1)} %fusion.4) | copy-start | bytes 3145732
Sparse Core Ops, SparseCore 0:
  10.7 111.2 all-gather.2
  153.4 35.3 all-gather.4

commit v5 on v4

--- a/solution.py
+++ b/solution.py
@@ -85,29 +85,32 @@
 
 
 def terms_kernel(me_ref, grads_ref, gathered_ref, *refs):
-    pieces, (out_ref, held, kept, sems, piece_sems) = refs[:-5], refs[-5:]
-    blocks = len(pieces)
-    deep = held.shape[1]
+    pieces, (out_ref, head, sems, piece_sems) = refs[:-4], refs[-4:]
+    blocks, depth, _ = head.shape
+    deep = depth - pieces[0].shape[0]
+    piece_copies = [
+        pltpu.make_async_copy(
+            piece,
+            head.at[lax.rem(me_ref[0] + j, blocks), pl.ds(deep, depth - deep)],
+            piece_sems.at[j],
+        )
+        for j, piece in enumerate(pieces)
+    ]
     copies = [
-        pltpu.make_async_copy(gathered_ref.at[pl.ds(j * deep, deep)], held.at[j], sems.at[j])
+        pltpu.make_async_copy(
+            gathered_ref.at[pl.ds(j * deep, deep)], head.at[j, pl.ds(0, deep)], sems.at[j]
+        )
         for j in range(blocks)
     ]
-    piece_copies = [
-        pltpu.make_async_copy(piece, kept.at[j], piece_sems.at[j]) for j, piece in enumerate(pieces)
-    ]
-    for j in range(blocks):
-        copies[j].start()
-        piece_copies[j].start()
+    for copy in piece_copies + copies:
+        copy.start()
     grads = grads_ref[...]
-    contract = (((1,), (1,)), ((), ()))
-    for j in range(blocks):
-        copies[j].wait()
-        out_ref[j, :, :deep] = lax.dot_general(
-            grads, held[j], contract, preferred_element_type=jnp.float32
-        )
-        piece_copies[j].wait()
-        out_ref[lax.rem(me_ref[0] + j, blocks), :, deep:] = lax.dot_general(
-            grads, kept[j], contract, preferred_element_type=jnp.float32
+    for copy in piece_copies:
+        copy.wait()
+    for j, copy in enumerate(copies):
+        copy.wait()
+        out_ref[j] = lax.dot_general(
+            grads, head[j], (((1,), (1,)), ((), ())), preferred_element_type=jnp.float32
         )
 
 
@@ -122,8 +125,7 @@
         in_specs=[pl.BlockSpec(memory_space=pltpu.SMEM), VMEM, HBM] + [HBM] * blocks,
         out_specs=VMEM,
         scratch_shapes=[
-            pltpu.VMEM((blocks, deep, width), gathered.dtype),
-            pltpu.VMEM((blocks, rest, width), gathered.dtype),
+            pltpu.VMEM((blocks, deep + rest, width), gathered.dtype),
             pltpu.SemaphoreType.DMA((blocks,)),
             pltpu.SemaphoreType.DMA((blocks,)),
         ],
@@ -156,9 +158,7 @@
     mine = mine.reshape(many, blocks // 2 * rows // many, d)
     parts = lax.all_to_all(mine, "vocab", 0, 0, axis_index_groups=core_groups(n_v))
     total = jnp.sum(parts.astype(jnp.float32), axis=0).astype(jnp.bfloat16)
-    whole = spread(total, many, core_groups(n_v))
-    both = spread(whole, 2, pair_groups(n_v))
-    return both.reshape(blocks, rows, d)
+    return spread(total, many, core_groups(n_v))
 
 
 def body(hidden, head_weight, teacher_logprobs, lengths, seq_weights):
@@ -203,12 +203,14 @@
     everyone, grad_logits = lax.optimization_barrier((everyone, grad_logits))
     slices = everyone.transpose(1, 0, 2, 3).reshape(n_dp * tok_rows, depth)
     all_grads = lax.all_gather(grad_logits, "dp", axis=0, tiled=True)
-    summed = sum_terms(hidden_terms(me, grad_logits, gathered, pieces), n_v)
-    grad_hidden = jnp.concatenate([summed[k] for k in range(n_dp)], axis=1)
+    whole = sum_terms(hidden_terms(me, grad_logits, gathered, pieces), n_v)
     grad_head = lax.dot_general(
         slices, all_grads, (((0,), (0,)), ((), ())), preferred_element_type=jnp.float32
-    )
-    return grad_hidden, grad_head.astype(jnp.bfloat16)
+    ).astype(jnp.bfloat16)
+    whole, grad_head = lax.optimization_barrier((whole, grad_head))
+    summed = spread(whole, 2, pair_groups(n_v)).reshape(n_dp, tok_rows, depth)
+    grad_hidden = jnp.concatenate([summed[k] for k in range(n_dp)], axis=1)
+    return grad_hidden, grad_head
 
 
 def solution(mesh):

time: 233 us -> 227 us (0.974)
  waiting for transfers between devices: 52.3 us -> 47.8 us
    all_to_all x2, waiting for transfers between devices: 15.9 us -> 11.5 us  [spread(): return lax.all_to_all(copies, axis, 0, 0, axis_index_groups=groups)]
  transfers between devices with their start and end apart: 14 -> 14, of which waited for: 7 -> 7; matrix products, arithmetic and copies ran while one was open for 7% -> 9% of each run, Pallas kernels for 5% -> 4%
where the time goes in v5:
time: 227 us; the launch traced here: 226 us
  starting transfers between devices  68.9 us (30%)
  blocking collectives  53.9 us (24%)
  waiting for transfers between devices  47.8 us (21%)
  matrix products  18.7 us (8%)
  between operations  14.6 us (6%)
  local copies, waits for them, and re-layouts  10.8 us (5%)
  Pallas kernels  10.7 us (5%)
    ppermute x6, starting transfers between devices, ring_blocks(): down, up = (lax.ppermute(down, 'dp', left), lax.ppermute(up, 'dp', right))  27 us
    ppermute x6, waiting for transfers between devices, ring_blocks(): down, up = (lax.ppermute(down, 'dp', left), lax.ppermute(up, 'dp', right))  21.1 us
    all_to_all x1, blocking collectives, body(): every = lax.all_to_all(stats, 'vocab', 0, 0)  19.9 us
    all_to_all x1, blocking collectives, sum_terms(): lax.all_to_all(mine, 'vocab', 0, 0, axis_index_groups=core_groups(n_v))  19.6 us
    all_to_all x2, starting transfers between devices, spread(): return lax.all_to_all(copies, axis, 0, 0, axis_index_groups=groups)  16.7 us
    all_to_all x1, starting transfers between devices, body(): lax.all_to_all(teacher_logprobs, 'vocab', split_axis=1, concat_axis=0, ti...  14.8 us
    all_to_all x2, waiting for transfers between devices, spread(): return lax.all_to_all(copies, axis, 0, 0, axis_index_groups=groups)  11.5 us
    dot_general x8, matrix products, body(): term = jnp.dot(feats, pieces[k], preferred_element_type=jnp.float32)  10.2 us
  transfers between devices with their start and end apart: 14, of which 7 were waited for; matrix products, arithmetic and copies ran while one was open for 9% of the time, Pallas kernels for 4%

profile of v5, /device:TPU:1, one launch (start us, length us, event | category | flops | bytes accessed | tf_op | source)
XLA Modules:
  0.0 226.0 jit_solution(1147358307197510324)
XLA Ops:
  7.2 2.2 slice.45
  9.6 4.8 %collective-permute-start.4 = (bf16[192,1280]{1,0:T(8,128)(2,1)S(1)}, bf16[192,1280]{1,0:T(8,128)(2,1)}, u32[]{:S(2)}, u32[]{:S(2)}) collective-permute-start(bf16[192,1280]{1,0:T(8,128)(2,1)S(1)} %slice.46.refs_0_), channel_id=1, source_target_pairs={{0,64},{64,128},{128,192},{192,256},{256,320},{320,384},{384,448},... | collective-permute-start | bytes 1474568 | tf_op jit(solution)/shard_map/ppermute | solution.py:43
  14.4 8.6 %collective-permute-start = (bf16[192,1280]{1,0:T(8,128)(2,1)S(1)}, bf16[192,1280]{1,0:T(8,128)(2,1)}, u32[]{:S(2)}, u32[]{:S(2)}) collective-permute-start(bf16[192,1280]{1,0:T(8,128)(2,1)S(1)} %slice.46.refs_0_), channel_id=1, source_target_pairs={{0,448},{64,0},{128,64},{192,128},{256,192},{320,256},{384,320},{4... | collective-permute-start | bytes 1474568 | tf_op jit(solution)/shard_map/ppermute | solution.py:43
  23.0 0.6 constant_dynamic-slice_fusion
  23.6 3.9 %all-to-all-start = ((bf16[8,2,512]{2,1,0:T(2,128)(2,1)}), bf16[8,2,512]{2,1,0:T(2,128)(2,1)S(1)}, u32[]{:S(2)}, u32[]{:S(2)}) async-start(bf16[8,2,512]{2,1,0:T(2,128)(2,1)} %bitcast.2), calls=%async_computation | async-start | bytes 32768 | tf_op jit(solution)/shard_map/all_to_all | solution.py:173
  27.6 0.3 fusion.22
  27.9 7.7 %all-to-all-done = bf16[8,2,512]{2,1,0:T(2,128)(2,1)S(1)} async-done(((bf16[8,2,512]{2,1,0:T(2,128)(2,1)}), bf16[8,2,512]{2,1,0:T(2,128)(2,1)S(1)}, u32[]{:S(2)}, u32[]{:S(2)}) %all-to-all-start) | async-done | bytes 16416 | tf_op jit(solution)/shard_map/all_to_all | solution.py:173
  35.5 14.8 %all-to-all-start.2 = ((bf16[2,64,1280]{2,0,1:T(2,128)(2,1)}), bf16[2,64,1280]{2,0,1:T(2,128)(2,1)}, u32[]{:S(2)}, u32[]{:S(2)}) async-start(bf16[2,64,1280]{2,0,1:T(2,128)(2,1)} %bitcast.72), calls=%async_computation.2 | async-start | bytes 655360 | tf_op jit(solution)/shard_map/all_to_all | solution.py:172
  50.4 0.7 copy.14
  51.1 0.9 slice.62
  52.1 2.2 collective-permute-start.5
  54.3 4.9 %collective-permute-start.1 = (bf16[192,1280]{1,0:T(8,128)(2,1)}, bf16[192,1280]{1,0:T(8,128)(2,1)S(1)}, u32[]{:S(2)}, u32[]{:S(2)}) collective-permute-start(bf16[192,1280]{1,0:T(8,128)(2,1)} %collective-permute-done.refs_1_), channel_id=1, source_target_pairs={{0,448},{64,0},{128,64},{192,128},{256,192},{320,256},{384,320},{4... | collective-permute-start | bytes 1474568 | tf_op jit(solution)/shard_map/ppermute | solution.py:43
  59.3 1.4 convolution_add_fusion.3
  60.7 19.0 %collective-permute-done.5.refs_6_ = bf16[192,1280]{1,0:T(8,128)(2,1)} collective-permute-done((bf16[192,1280]{1,0:T(8,128)(2,1)}, bf16[192,1280]{1,0:T(8,128)(2,1)}, u32[]{:S(2)}, u32[]{:S(2)}) %collective-permute-start.5) | collective-permute-done | bytes 491552 | tf_op jit(solution)/shard_map/ppermute | solution.py:43
  79.7 1.9 collective-permute-start.6
  81.6 4.6 %collective-permute-start.2 = (bf16[192,1280]{1,0:T(8,128)(2,1)S(1)}, bf16[192,1280]{1,0:T(8,128)(2,1)S(1)}, u32[]{:S(2)}, u32[]{:S(2)}) collective-permute-start(bf16[192,1280]{1,0:T(8,128)(2,1)S(1)} %collective-permute-done.1.refs_2_), channel_id=1, source_target_pairs={{0,448},{64,0},{128,64},{192,128},{256,192},{320,256},{384,320},{4... | collective-permute-start | bytes 1474568 | tf_op jit(solution)/shard_map/ppermute | solution.py:43
  86.2 2.0 broadcast_in_dim.50
  88.2 11.5 %all-to-all-start.1 = ((bf16[64,8,2,512]{3,2,1,0:T(2,128)(2,1)}), bf16[64,8,2,512]{3,2,1,0:T(2,128)(2,1)S(1)}, u32[]{:S(2)}, u32[]{:S(2)}) async-start(bf16[64,8,2,512]{3,2,1,0:T(2,128)(2,1)} %broadcast_in_dim.50), calls=%async_computation.1 | async-start | bytes 2097152 | tf_op jit(solution)/shard_map/all_to_all | solution.py:26
  99.7 2.2 fusion.12
  101.9 1.1 all_to_all.40.teacher_ref
  103.0 1.2 convolution_add_fusion.2
  104.2 2.1 collective-permute-done.6.refs_5_
  106.3 1.9 collective-permute-start.7
  108.3 4.6 %collective-permute-start.3 = (bf16[96,1280]{1,0:T(8,128)(2,1)S(1)}, bf16[96,1280]{1,0:T(8,128)(2,1)S(1)}, u32[]{:S(2)}, u32[]{:S(2)}) collective-permute-start(bf16[96,1280]{1,0:T(8,128)(2,1)S(1)} %slice.60), channel_id=1, source_target_pairs={{0,448},{64,0},{128,64},{192,128},{256,192},{320,256},{384,320},{4... | collective-permute-start | bytes 737288 | tf_op jit(solution)/shard_map/ppermute | solution.py:46
  112.9 1.4 fusion.14
  114.3 7.0 %collective-permute-done.3 = bf16[96,1280]{1,0:T(8,128)(2,1)S(1)} collective-permute-done((bf16[96,1280]{1,0:T(8,128)(2,1)S(1)}, bf16[96,1280]{1,0:T(8,128)(2,1)S(1)}, u32[]{:S(2)}, u32[]{:S(2)}) %collective-permute-start.3) | collective-permute-done | bytes 245792 | tf_op jit(solution)/shard_map/ppermute | solution.py:46
  121.3 0.5 collective-permute-done.7
  121.9 1.3 fusion.17
  123.2 1.2 fusion.2
  124.4 1.2 fusion.1
  125.7 2.0 all-to-all-done.1
  127.6 4.1 %fusion.33 = f32[128,1280]{1,0:T(8,128)S(1)} fusion(bf16[128,2560]{0,1:T(8,128)(2,1)} %bitcast.70, bf16[2560,1280]{1,0:T(8,128)(2,1)} %all-gather.3.cloned.1.call-done.gathered_ref), kind=kOutput, calls=%fused_computation.59 | convolution fusion | flops 838860800 | bytes 7864320 | tf_op jit(solution)/shard_map/dot_general | solution.py:196
  131.9 0.4 shard_map.68
  132.3 19.9 %all_to_all.54.every_ref = f32[64,3,128]{2,1,0:T(4,128)S(1)} all-to-all(f32[64,3,128]{2,1,0:T(4,128)S(1)} %shard_map.68), channel_id=1, replica_groups=mesh['dp'=8,'vocab'=64] {'vocab'}, dimensions={0} | all-to-all | bytes 196608 | tf_op jit(solution)/shard_map/all_to_all | solution.py:198
  152.2 1.0 shard_map.69.grads_ref
  153.3 9.3 %shard_map.70 = f32[8,128,512]{2,1,0:T(8,128)} custom-call(s32[1]{0:T(128)} %bitcast.me_ref, bf16[128,1280]{1,0:T(8,128)(2,1)} %shard_map.69.grads_ref, bf16[2560,1280]{1,0:T(8,128)(2,1)} %all-gather.3.cloned.1.call-done.gathered_ref, bf16[192,1280]{1,0:T(8,128)(2,1)} %copy-done.6, bf16[192,1280]{1,0:T(8,128)(2,1)} %collective-permute-done.refs_1_, ...), custom_call_target="tpu_custom_call" | custom-call | flops 1342177280 | bytes 12582912 | tf_op jit(solution)/shard_map/pallas_call | solution.py:122
  162.6 6.6 %all_to_all.55 = f32[2,4,128,512]{3,2,1,0:T(8,128)S(1)} all-to-all(f32[2,4,128,512]{3,2,1,0:T(8,128)} %bitcast.59), channel_id=1, replica_groups={{0,1},{2,3},{4,5},{6,7},{8,9},{10,11},{12,13},{14,15},{16,17},{18,19},{..., dimensions={0} | all-to-all | bytes 4194304 | tf_op jit(solution)/shard_map/all_to_all | solution.py:154
  169.2 0.2 fusion.3
  169.4 19.6 %all_to_all.56 = bf16[32,16,512]{2,1,0:T(8,128)(2,1)S(1)} all-to-all(bf16[32,16,512]{2,1,0:T(8,128)(2,1)S(1)} %bitcast.71), channel_id=1, replica_groups={{0,2,4,6,8,10,12,14,16,18,20,22,24,26,28,30,32,34,36,38,40,42,44,46,48,..., dimensions={0} | all-to-all | bytes 1048576 | tf_op jit(solution)/shard_map/all_to_all | solution.py:159
  189.0 0.9 broadcast_in_dim.56
  189.9 5.2 %all-to-all-start.6 = ((bf16[32,16,512]{2,1,0:T(8,128)(2,1)}), bf16[32,16,512]{2,1,0:T(8,128)(2,1)S(1)}, u32[]{:S(2)}, u32[]{:S(2)}) async-start(bf16[32,16,512]{2,1,0:T(8,128)(2,1)} %broadcast_in_dim.56), calls=%async_computation.6 | async-start | bytes 1048576 | tf_op jit(solution)/shard_map/all_to_all | solution.py:26
  195.1 0.7 copy.15
  195.8 0.4 reshape.93
  196.3 4.4 %convolution_convert_fusion = bf16[512,1280]{1,0:T(8,128)(2,1)} fusion(bf16[1024,512]{1,0:T(8,128)(2,1)S(1)} %reshape.93, bf16[1024,1280]{1,0:T(8,128)(2,1)} %all-gather.5.cloned.1.call-done), kind=kOutput, calls=%fused_computation | convolution fusion | flops 1342832640 | bytes 4980736 | tf_op jit(solution)/shard_map/dot_general | solution.py:207
  200.7 9.5 %all-to-all-done.6 = bf16[32,16,512]{2,1,0:T(8,128)(2,1)S(1)} async-done(((bf16[32,16,512]{2,1,0:T(8,128)(2,1)}), bf16[32,16,512]{2,1,0:T(8,128)(2,1)S(1)}, u32[]{:S(2)}, u32[]{:S(2)}) %all-to-all-start.6) | async-done | bytes 524320 | tf_op jit(solution)/shard_map/all_to_all | solution.py:26
  210.1 0.1 broadcast_in_dim.57
  210.3 7.8 %all_to_all.57 = bf16[2,32,16,512]{3,2,1,0:T(8,128)(2,1)S(1)} all-to-all(bf16[2,32,16,512]{3,2,1,0:T(8,128)(2,1)S(1)} %broadcast_in_dim.57), channel_id=1, replica_groups={{0,1},{2,3},{4,5},{6,7},{8,9},{10,11},{12,13},{14,15},{16,17},{18,19},{..., dimensions={0} | all-to-all | bytes 2097152 | tf_op jit(solution)/shard_map/all_to_all | solution.py:26
  218.2 1.0 copy-done.8
  (51 shorter events, 0.7 us)
Async XLA Ops:
  7.2 2.3 %copy-start.4 = (bf16[512,1280]{1,0:T(8,128)(2,1)S(1)}, bf16[512,1280]{1,0:T(8,128)(2,1)}, u32[]{:S(2)}) copy-start(bf16[512,1280]{1,0:T(8,128)(2,1)} %param.6) | copy-start | bytes 3932164
  7.2 15.8 %copy-start.5 = (bf16[128,4096]{1,0:T(8,128)(2,1)S(1)}, bf16[128,4096]{1,0:T(8,128)(2,1)}, u32[]{:S(2)}) copy-start(bf16[128,4096]{1,0:T(8,128)(2,1)} %param.5) | copy-start | bytes 3145732
  7.2 43.1 %copy-start.9 = (f32[2]{0:T(128)S(1)}, f32[2]{0:T(128)}, u32[]{:S(2)}) copy-start(f32[2]{0:T(128)} %param.9) | copy-start | bytes 28
  7.2 120.4 %all-gather.3.cloned.1.call-start = ((), (), s32[]{:S(2)}) async-start(), calls=%async_computation.8 | async-start | bytes 7372800 | tf_op jit(solution)/shard_map/all_gather | solution.py:170
  9.6 42.4 %copy-start.6 = (bf16[192,1280]{1,0:T(8,128)(2,1)}, bf16[192,1280]{1,0:T(8,128)(2,1)S(1)}, u32[]{:S(2)}) copy-start(bf16[192,1280]{1,0:T(8,128)(2,1)S(1)} %slice.46.refs_0_) | copy-start | bytes 1474564
  9.6 42.5 %collective-permute-start.4 = (bf16[192,1280]{1,0:T(8,128)(2,1)S(1)}, bf16[192,1280]{1,0:T(8,128)(2,1)}, u32[]{:S(2)}, u32[]{:S(2)}) collective-permute-start(bf16[192,1280]{1,0:T(8,128)(2,1)S(1)} %slice.46.refs_0_), channel_id=1, source_target_pairs={{0,64},{64,128},{128,192},{192,256},{256,320},{320,384},{384,448},... | collective-permute-start | bytes 1474568 | tf_op jit(solution)/shard_map/ppermute | solution.py:43
  14.4 39.9 %collective-permute-start = (bf16[192,1280]{1,0:T(8,128)(2,1)S(1)}, bf16[192,1280]{1,0:T(8,128)(2,1)}, u32[]{:S(2)}, u32[]{:S(2)}) collective-permute-start(bf16[192,1280]{1,0:T(8,128)(2,1)S(1)} %slice.46.refs_0_), channel_id=1, source_target_pairs={{0,448},{64,0},{128,64},{192,128},{256,192},{320,256},{384,320},{4... | collective-permute-start | bytes 1474568 | tf_op jit(solution)/shard_map/ppermute | solution.py:43
  23.6 11.9 %all-to-all-start = ((bf16[8,2,512]{2,1,0:T(2,128)(2,1)}), bf16[8,2,512]{2,1,0:T(2,128)(2,1)S(1)}, u32[]{:S(2)}, u32[]{:S(2)}) async-start(bf16[8,2,512]{2,1,0:T(2,128)(2,1)} %bitcast.2), calls=%async_computation | async-start | bytes 32768 | tf_op jit(solution)/shard_map/all_to_all | solution.py:173
  27.6 24.4 %copy-start.10 = (s32[2]{0:T(128)S(1)}, s32[2]{0:T(128)}, u32[]{:S(2)}) copy-start(s32[2]{0:T(128)} %param.8) | copy-start | bytes 28
  35.5 50.6 %all-to-all-start.2 = ((bf16[2,64,1280]{2,0,1:T(2,128)(2,1)}), bf16[2,64,1280]{2,0,1:T(2,128)(2,1)}, u32[]{:S(2)}, u32[]{:S(2)}) async-start(bf16[2,64,1280]{2,0,1:T(2,128)(2,1)} %bitcast.72), calls=%async_computation.2 | async-start | bytes 655360 | tf_op jit(solution)/shard_map/all_to_all | solution.py:172
  52.1 27.6 %collective-permute-start.5 = (bf16[192,1280]{1,0:T(8,128)(2,1)}, bf16[192,1280]{1,0:T(8,128)(2,1)}, u32[]{:S(2)}, u32[]{:S(2)}) collective-permute-start(bf16[192,1280]{1,0:T(8,128)(2,1)} %collective-permute-done.4.refs_7_), channel_id=1, source_target_pairs={{0,64},{64,128},{128,192},{192,256},{256,320},{320,384},{384,448},... | collective-permute-start | bytes 1474568 | tf_op jit(solution)/shard_map/ppermute | solution.py:43
  54.3 27.2 %collective-permute-start.1 = (bf16[192,1280]{1,0:T(8,128)(2,1)}, bf16[192,1280]{1,0:T(8,128)(2,1)S(1)}, u32[]{:S(2)}, u32[]{:S(2)}) collective-permute-start(bf16[192,1280]{1,0:T(8,128)(2,1)} %collective-permute-done.refs_1_), channel_id=1, source_target_pairs={{0,448},{64,0},{128,64},{192,128},{256,192},{320,256},{384,320},{4... | collective-permute-start | bytes 1474568 | tf_op jit(solution)/shard_map/ppermute | solution.py:43
  79.7 26.6 %collective-permute-start.6 = (bf16[192,1280]{1,0:T(8,128)(2,1)}, bf16[192,1280]{1,0:T(8,128)(2,1)S(1)}, u32[]{:S(2)}, u32[]{:S(2)}) collective-permute-start(bf16[192,1280]{1,0:T(8,128)(2,1)} %collective-permute-done.5.refs_6_), channel_id=1, source_target_pairs={{0,64},{64,128},{128,192},{192,256},{256,320},{320,384},{384,448},... | collective-permute-start | bytes 1474568 | tf_op jit(solution)/shard_map/ppermute | solution.py:43
  81.6 22.6 %copy-start.7 = (bf16[192,1280]{1,0:T(8,128)(2,1)}, bf16[192,1280]{1,0:T(8,128)(2,1)S(1)}, u32[]{:S(2)}) copy-start(bf16[192,1280]{1,0:T(8,128)(2,1)S(1)} %collective-permute-done.1.refs_2_) | copy-start | bytes 1474564
  81.6 26.7 %collective-permute-start.2 = (bf16[192,1280]{1,0:T(8,128)(2,1)S(1)}, bf16[192,1280]{1,0:T(8,128)(2,1)S(1)}, u32[]{:S(2)}, u32[]{:S(2)}) collective-permute-start(bf16[192,1280]{1,0:T(8,128)(2,1)S(1)} %collective-permute-done.1.refs_2_), channel_id=1, source_target_pairs={{0,448},{64,0},{128,64},{192,128},{256,192},{320,256},{384,320},{4... | collective-permute-start | bytes 1474568 | tf_op jit(solution)/shard_map/ppermute | solution.py:43
  88.2 39.5 %all-to-all-start.1 = ((bf16[64,8,2,512]{3,2,1,0:T(2,128)(2,1)}), bf16[64,8,2,512]{3,2,1,0:T(2,128)(2,1)S(1)}, u32[]{:S(2)}, u32[]{:S(2)}) async-start(bf16[64,8,2,512]{3,2,1,0:T(2,128)(2,1)} %broadcast_in_dim.50), calls=%async_computation.1 | async-start | bytes 2097152 | tf_op jit(solution)/shard_map/all_to_all | solution.py:26
  99.6 96.6 %all-gather.5.cloned.1.call-start = ((), (), s32[]{:S(2)}) async-start(), calls=%async_computation.9 | async-start | bytes 2949120 | tf_op jit(solution)/shard_map/all_gather | solution.py:205
  106.3 18.1 %copy-start = (bf16[192,1280]{1,0:T(8,128)(2,1)}, bf16[192,1280]{1,0:T(8,128)(2,1)S(1)}, u32[]{:S(2)}) copy-start(bf16[192,1280]{1,0:T(8,128)(2,1)S(1)} %collective-permute-done.6.refs_5_) | copy-start | bytes 1474564
  106.3 15.5 %collective-permute-start.7 = (bf16[96,1280]{1,0:T(8,128)(2,1)S(1)}, bf16[96,1280]{1,0:T(8,128)(2,1)S(1)}, u32[]{:S(2)}, u32[]{:S(2)}) collective-permute-start(bf16[96,1280]{1,0:T(8,128)(2,1)S(1)} %slice.61), channel_id=1, source_target_pairs={{0,64},{64,128},{128,192},{192,256},{256,320},{320,384},{384,448},... | collective-permute-start | bytes 737288 | tf_op jit(solution)/shard_map/ppermute | solution.py:46
  108.3 16.2 %copy-start.1 = (bf16[192,1280]{1,0:T(8,128)(2,1)}, bf16[192,1280]{1,0:T(8,128)(2,1)S(1)}, u32[]{:S(2)}) copy-start(bf16[192,1280]{1,0:T(8,128)(2,1)S(1)} %collective-permute-done.2.refs_3_) | copy-start | bytes 1474564
  108.3 13.0 %collective-permute-start.3 = (bf16[96,1280]{1,0:T(8,128)(2,1)S(1)}, bf16[96,1280]{1,0:T(8,128)(2,1)S(1)}, u32[]{:S(2)}, u32[]{:S(2)}) collective-permute-start(bf16[96,1280]{1,0:T(8,128)(2,1)S(1)} %slice.60), channel_id=1, source_target_pairs={{0,448},{64,0},{128,64},{192,128},{256,192},{320,256},{384,320},{4... | collective-permute-start | bytes 737288 | tf_op jit(solution)/shard_map/ppermute | solution.py:46
  114.3 10.2 %copy-start.3 = (f32[128,1280]{1,0:T(8,128)S(1)}, f32[128,1280]{1,0:T(8,128)}, u32[]{:S(2)}) copy-start(f32[128,1280]{1,0:T(8,128)} %fusion.12) | copy-start | bytes 1966084
  121.9 3.8 %copy-start.2 = (bf16[192,1280]{1,0:T(8,128)(2,1)}, bf16[192,1280]{1,0:T(8,128)(2,1)S(1)}, u32[]{:S(2)}) copy-start(bf16[192,1280]{1,0:T(8,128)(2,1)S(1)} %constant_dynamic-update-slice_fusion.refs_4_) | copy-start | bytes 1474564
  189.9 20.2 %all-to-all-start.6 = ((bf16[32,16,512]{2,1,0:T(8,128)(2,1)}), bf16[32,16,512]{2,1,0:T(8,128)(2,1)S(1)}, u32[]{:S(2)}, u32[]{:S(2)}) async-start(bf16[32,16,512]{2,1,0:T(8,128)(2,1)} %broadcast_in_dim.56), calls=%async_computation.6 | async-start | bytes 1048576 | tf_op jit(solution)/shard_map/all_to_all | solution.py:26
  218.2 1.0 copy-start.8
Sparse Core Ops, SparseCore 0:
  10.7 111.2 all-gather.2
  153.4 35.1 all-gather.4

commit v6 on v5

--- a/solution.py
+++ b/solution.py
@@ -7,7 +7,7 @@
 
 SEQ_LEN = 64
 LOSS_SCALE = 32.0
-GATHERED = 10
+GATHERED = 12
 LANES = 128
 VMEM = pl.BlockSpec(memory_space=pltpu.VMEM)
 HBM = pl.BlockSpec(memory_space=pl.ANY)
@@ -88,28 +88,28 @@
     pieces, (out_ref, head, sems, piece_sems) = refs[:-4], refs[-4:]
     blocks, depth, _ = head.shape
     deep = depth - pieces[0].shape[0]
-    piece_copies = [
-        pltpu.make_async_copy(
-            piece,
-            head.at[lax.rem(me_ref[0] + j, blocks), pl.ds(deep, depth - deep)],
-            piece_sems.at[j],
+    places = [lax.rem(me_ref[0] + j, blocks) for j in range(blocks)]
+    copies = [
+        (
+            pltpu.make_async_copy(
+                piece, head.at[j, pl.ds(deep, depth - deep)], piece_sems.at[j]
+            ),
+            pltpu.make_async_copy(
+                gathered_ref.at[pl.ds(pl.multiple_of(places[j] * deep, deep), deep)],
+                head.at[j, pl.ds(0, deep)],
+                sems.at[j],
+            ),
         )
         for j, piece in enumerate(pieces)
     ]
-    copies = [
-        pltpu.make_async_copy(
-            gathered_ref.at[pl.ds(j * deep, deep)], head.at[j, pl.ds(0, deep)], sems.at[j]
-        )
-        for j in range(blocks)
-    ]
-    for copy in piece_copies + copies:
-        copy.start()
+    for pair in copies:
+        for copy in pair:
+            copy.start()
     grads = grads_ref[...]
-    for copy in piece_copies:
-        copy.wait()
-    for j, copy in enumerate(copies):
-        copy.wait()
-        out_ref[j] = lax.dot_general(
+    for j, pair in enumerate(copies):
+        for copy in pair:
+            copy.wait()
+        out_ref[places[j]] = lax.dot_general(
             grads, head[j], (((1,), (1,)), ((), ())), preferred_element_type=jnp.float32
         )
 
@@ -136,6 +136,26 @@
     )(me.reshape(1), grads, gathered, *pieces)
 
 
+def halves_kernel(core_ref, kept_ref, got_ref, out_ref):
+    some, _, depth = kept_ref.shape
+    for half, ref in ((core_ref[0], kept_ref), (1 - core_ref[0], got_ref)):
+        for i in range(some):
+            at = pl.multiple_of((half * some + i) * depth, depth)
+            out_ref[:, pl.ds(at, depth)] = ref[i]
+
+
+def both_halves(kept, got):
+    some, rows, depth = kept.shape
+    core = lax.rem(lax.axis_index("vocab"), 2)
+    return pl.pallas_call(
+        halves_kernel,
+        out_shape=jax.ShapeDtypeStruct((rows, 2 * some * depth), kept.dtype),
+        in_specs=[pl.BlockSpec(memory_space=pltpu.SMEM), VMEM, VMEM],
+        out_specs=VMEM,
+        compiler_params=pltpu.CompilerParams(vmem_limit_bytes=16 * 2**20),
+    )(core.reshape(1), kept, got)
+
+
 def row_kernel(kernel, shape, dtype, *args):
     size = args[-1].size
     return pl.pallas_call(
@@ -208,8 +228,9 @@
         slices, all_grads, (((0,), (0,)), ((), ())), preferred_element_type=jnp.float32
     ).astype(jnp.bfloat16)
     whole, grad_head = lax.optimization_barrier((whole, grad_head))
-    summed = spread(whole, 2, pair_groups(n_v)).reshape(n_dp, tok_rows, depth)
-    grad_hidden = jnp.concatenate([summed[k] for k in range(n_dp)], axis=1)
+    kept = whole.reshape(n_dp // 2, tok_rows, depth)
+    got = lax.ppermute(kept, "vocab", [(i, i ^ 1) for i in range(n_v)])
+    grad_hidden = both_halves(kept, got)
     return grad_hidden, grad_head
 
 

time: 227 us -> 226 us (level)
  waiting for transfers between devices: 47.8 us -> 59.9 us
  starting transfers between devices: 68.9 us -> 62.2 us
  blocking collectives: 53.9 us -> 47.6 us
    all_gather x1, waiting for transfers between devices: 0.01 us -> 14.4 us  [body(): gathered = lax.all_gather(head_weight[:deep], 'dp', axis=0, tiled=True)]
    ppermute x6, waiting for transfers between devices: 21.1 us -> 9.84 us  [ring_blocks(): down, up = (lax.ppermute(down, 'dp', left), lax.ppermute(up, 'dp', right))]
    all_to_all x1 -> x0, blocking collectives: 7.78 us -> none  [spread(): return lax.all_to_all(copies, axis, 0, 0, axis_index_groups=groups)]
    all_to_all x1, waiting for transfers between devices: 0.01 us -> 7.63 us  [body(): lax.all_to_all(teacher_logprobs, 'vocab', split_axis=1, concat_axis=0, ti...]
    all_to_all x2, starting transfers between devices: 16.7 us -> 10.3 us  [spread(): return lax.all_to_all(copies, axis, 0, 0, axis_index_groups=groups)]
    ppermute x1, waiting for transfers between devices: 0.53 us -> 6.15 us  [ring_blocks(): lax.ppermute(up[half:], 'dp', right)]
    ppermute x0 -> x1, starting transfers between devices: none -> 5.48 us  [body(): got = lax.ppermute(kept, 'vocab', [(i, i ^ 1) for i in range(n_v)])]
    ppermute x6, starting transfers between devices: 27 us -> 24 us  [ring_blocks(): down, up = (lax.ppermute(down, 'dp', left), lax.ppermute(up, 'dp', right))]
  transfers between devices with their start and end apart: 14 -> 15, of which waited for: 7 -> 9; matrix products, arithmetic and copies ran while one was open for 9% -> 9% of each run, Pallas kernels for 4% -> 4%
where the time goes in v6:
time: 226 us; the launch traced here: 225 us
  starting transfers between devices  62.2 us (28%)
  waiting for transfers between devices  59.9 us (27%)
  blocking collectives  47.6 us (21%)
  matrix products  17.2 us (8%)
  between operations  14.5 us (6%)
  local copies, waits for them, and re-layouts  11.9 us (5%)
  Pallas kernels  10.7 us (5%)
    ppermute x6, starting transfers between devices, ring_blocks(): down, up = (lax.ppermute(down, 'dp', left), lax.ppermute(up, 'dp', right))  24 us
    all_to_all x1, blocking collectives, body(): every = lax.all_to_all(stats, 'vocab', 0, 0)  21.4 us
    all_to_all x1, blocking collectives, sum_terms(): lax.all_to_all(mine, 'vocab', 0, 0, axis_index_groups=core_groups(n_v))  19.6 us
    all_gather x1, waiting for transfers between devices, body(): gathered = lax.all_gather(head_weight[:deep], 'dp', axis=0, tiled=True)  14.4 us
    all_to_all x1, starting transfers between devices, body(): lax.all_to_all(teacher_logprobs, 'vocab', split_axis=1, concat_axis=0, ti...  12.9 us
    all_to_all x2, starting transfers between devices, spread(): return lax.all_to_all(copies, axis, 0, 0, axis_index_groups=groups)  10.3 us
    ppermute x6, waiting for transfers between devices, ring_blocks(): down, up = (lax.ppermute(down, 'dp', left), lax.ppermute(up, 'dp', right))  9.84 us
    all_to_all x2, waiting for transfers between devices, spread(): return lax.all_to_all(copies, axis, 0, 0, axis_index_groups=groups)  9.49 us
  transfers between devices with their start and end apart: 15, of which 9 were waited for; matrix products, arithmetic and copies ran while one was open for 9% of the time, Pallas kernels for 4%

profile of v6, /device:TPU:1, one launch (start us, length us, event | category | flops | bytes accessed | tf_op | source)
XLA Modules:
  0.0 224.6 jit_solution(8820893931924898137)
XLA Ops:
  7.3 2.4 %slice.21 = bf16[384,1280]{1,0:T(8,128)(2,1)} slice(bf16[512,1280]{1,0:T(8,128)(2,1)} %param.6), slice={[0:384], [0:1280]} | slice | bytes 1966080 | tf_op jit(solution)/shard_map/slice | solution.py:190
  9.6 0.8 slice.22.refs_0_
  10.4 4.8 %collective-permute-start.4 = (bf16[128,1280]{1,0:T(8,128)(2,1)}, bf16[128,1280]{1,0:T(8,128)(2,1)}, u32[]{:S(2)}, u32[]{:S(2)}) collective-permute-start(bf16[128,1280]{1,0:T(8,128)(2,1)} %slice.22.refs_0_), channel_id=1, source_target_pairs={{0,64},{64,128},{128,192},{192,256},{256,320},{320,384},{384,448},... | collective-permute-start | bytes 983048 | tf_op jit(solution)/shard_map/ppermute | solution.py:43
  15.2 8.6 %collective-permute-start = (bf16[128,1280]{1,0:T(8,128)(2,1)}, bf16[128,1280]{1,0:T(8,128)(2,1)}, u32[]{:S(2)}, u32[]{:S(2)}) collective-permute-start(bf16[128,1280]{1,0:T(8,128)(2,1)} %slice.22.refs_0_), channel_id=1, source_target_pairs={{0,448},{64,0},{128,64},{192,128},{256,192},{320,256},{384,320},{4... | collective-permute-start | bytes 983048 | tf_op jit(solution)/shard_map/ppermute | solution.py:43
  23.9 0.6 constant_dynamic-slice_fusion
  24.5 3.9 %all-to-all-start = ((bf16[8,2,512]{2,1,0:T(2,128)(2,1)}), bf16[8,2,512]{2,1,0:T(2,128)(2,1)S(1)}, u32[]{:S(2)}, u32[]{:S(2)}) async-start(bf16[8,2,512]{2,1,0:T(2,128)(2,1)} %bitcast.3), calls=%async_computation | async-start | bytes 32768 | tf_op jit(solution)/shard_map/all_to_all | solution.py:193
  28.4 6.7 %all-to-all-done = bf16[8,2,512]{2,1,0:T(2,128)(2,1)S(1)} async-done(((bf16[8,2,512]{2,1,0:T(2,128)(2,1)}), bf16[8,2,512]{2,1,0:T(2,128)(2,1)S(1)}, u32[]{:S(2)}, u32[]{:S(2)}) %all-to-all-start) | async-done | bytes 16416 | tf_op jit(solution)/shard_map/all_to_all | solution.py:193
  35.1 12.9 %all-to-all-start.2 = ((bf16[2,64,1280]{2,0,1:T(2,128)(2,1)}), bf16[2,64,1280]{2,0,1:T(2,128)(2,1)}, u32[]{:S(2)}, u32[]{:S(2)}) async-start(bf16[2,64,1280]{2,0,1:T(2,128)(2,1)} %bitcast.4), calls=%async_computation.2 | async-start | bytes 655360 | tf_op jit(solution)/shard_map/all_to_all | solution.py:192
  48.5 2.5 %collective-permute-start.1 = (bf16[128,1280]{1,0:T(8,128)(2,1)}, bf16[128,1280]{1,0:T(8,128)(2,1)}, u32[]{:S(2)}, u32[]{:S(2)}) collective-permute-start(bf16[128,1280]{1,0:T(8,128)(2,1)} %collective-permute-done.refs_1_), channel_id=1, source_target_pairs={{0,448},{64,0},{128,64},{192,128},{256,192},{320,256},{384,320},{4... | collective-permute-start | bytes 983048 | tf_op jit(solution)/shard_map/ppermute | solution.py:43
  51.1 0.4 copy.13
  51.7 2.8 %collective-permute-start.5 = (bf16[128,1280]{1,0:T(8,128)(2,1)}, bf16[128,1280]{1,0:T(8,128)(2,1)}, u32[]{:S(2)}, u32[]{:S(2)}) collective-permute-start(bf16[128,1280]{1,0:T(8,128)(2,1)} %collective-permute-done.4.refs_7_), channel_id=1, source_target_pairs={{0,64},{64,128},{128,192},{192,256},{256,320},{320,384},{384,448},... | collective-permute-start | bytes 983048 | tf_op jit(solution)/shard_map/ppermute | solution.py:43
  54.6 7.6 %all-to-all-done.2 = bf16[2,64,1280]{2,0,1:T(2,128)(2,1)} async-done(((bf16[2,64,1280]{2,0,1:T(2,128)(2,1)}), bf16[2,64,1280]{2,0,1:T(2,128)(2,1)}, u32[]{:S(2)}, u32[]{:S(2)}) %all-to-all-start.2) | async-done | bytes 327712 | tf_op jit(solution)/shard_map/all_to_all | solution.py:192
  62.2 2.7 %broadcast_in_dim.44 = bf16[64,8,2,512]{3,2,1,0:T(2,128)(2,1)} broadcast(bf16[8,2,512]{2,1,0:T(2,128)(2,1)} %copy-done.4), dimensions={1,2,3} | broadcast | bytes 1064960 | tf_op jit(solution)/shard_map/broadcast_in_dim | solution.py:25
  64.9 5.1 %all-to-all-start.1 = ((bf16[64,8,2,512]{3,2,1,0:T(2,128)(2,1)}), bf16[64,8,2,512]{3,2,1,0:T(2,128)(2,1)S(1)}, u32[]{:S(2)}, u32[]{:S(2)}) async-start(bf16[64,8,2,512]{3,2,1,0:T(2,128)(2,1)} %broadcast_in_dim.44), calls=%async_computation.1 | async-start | bytes 2097152 | tf_op jit(solution)/shard_map/all_to_all | solution.py:26
  70.0 1.2 convolution_add_fusion.3
  71.3 2.5 %collective-permute-start.2 = (bf16[128,1280]{1,0:T(8,128)(2,1)}, bf16[128,1280]{1,0:T(8,128)(2,1)}, u32[]{:S(2)}, u32[]{:S(2)}) collective-permute-start(bf16[128,1280]{1,0:T(8,128)(2,1)} %collective-permute-done.1.refs_2_), channel_id=1, source_target_pairs={{0,448},{64,0},{128,64},{192,128},{256,192},{320,256},{384,320},{4... | collective-permute-start | bytes 983048 | tf_op jit(solution)/shard_map/ppermute | solution.py:43
  73.8 1.2 fusion.4
  75.0 1.1 all_to_all.37.teacher_ref
  76.1 2.8 %collective-permute-start.6 = (bf16[128,1280]{1,0:T(8,128)(2,1)}, bf16[128,1280]{1,0:T(8,128)(2,1)S(1)}, u32[]{:S(2)}, u32[]{:S(2)}) collective-permute-start(bf16[128,1280]{1,0:T(8,128)(2,1)} %collective-permute-done.5.refs_6_), channel_id=1, source_target_pairs={{0,64},{64,128},{128,192},{192,256},{256,320},{320,384},{384,448},... | collective-permute-start | bytes 983048 | tf_op jit(solution)/shard_map/ppermute | solution.py:43
  79.0 1.2 convolution_add_fusion.2
  80.2 9.7 %collective-permute-done.2.refs_3_ = bf16[128,1280]{1,0:T(8,128)(2,1)} collective-permute-done((bf16[128,1280]{1,0:T(8,128)(2,1)}, bf16[128,1280]{1,0:T(8,128)(2,1)}, u32[]{:S(2)}, u32[]{:S(2)}) %collective-permute-start.2) | collective-permute-done | bytes 327712 | tf_op jit(solution)/shard_map/ppermute | solution.py:43
  89.9 0.9 slice.28
  90.9 3.7 %collective-permute-start.3 = (bf16[64,1280]{1,0:T(8,128)(2,1)S(1)}, bf16[64,1280]{1,0:T(8,128)(2,1)S(1)}, u32[]{:S(2)}, u32[]{:S(2)}) collective-permute-start(bf16[64,1280]{1,0:T(8,128)(2,1)S(1)} %slice.28), channel_id=1, source_target_pairs={{0,448},{64,0},{128,64},{192,128},{256,192},{320,256},{384,320},{4... | collective-permute-start | bytes 491528 | tf_op jit(solution)/shard_map/ppermute | solution.py:46
  94.5 1.2 fusion.6
  95.9 1.9 collective-permute-start.7
  97.8 4.2 %collective-permute-done.3 = bf16[64,1280]{1,0:T(8,128)(2,1)S(1)} collective-permute-done((bf16[64,1280]{1,0:T(8,128)(2,1)S(1)}, bf16[64,1280]{1,0:T(8,128)(2,1)S(1)}, u32[]{:S(2)}, u32[]{:S(2)}) %collective-permute-start.3) | collective-permute-done | bytes 163872 | tf_op jit(solution)/shard_map/ppermute | solution.py:46
  102.0 6.1 %collective-permute-done.7 = bf16[64,1280]{1,0:T(8,128)(2,1)S(1)} collective-permute-done((bf16[64,1280]{1,0:T(8,128)(2,1)S(1)}, bf16[64,1280]{1,0:T(8,128)(2,1)S(1)}, u32[]{:S(2)}, u32[]{:S(2)}) %collective-permute-start.7) | collective-permute-done | bytes 163872 | tf_op jit(solution)/shard_map/ppermute | solution.py:46
  108.2 0.7 copy-done.1
  108.9 1.0 fusion.9
  109.9 1.2 fusion.2
  111.2 1.0 fusion.1
  112.2 14.4 %all-gather.3.cloned.1.call-done.gathered_ref = bf16[3072,1280]{1,0:T(8,128)(2,1)} async-done(((bf16[384,1280]{1,0:T(8,128)(2,1)}), bf16[3072,1280]{1,0:T(8,128)(2,1)}) %all-gather.3.cloned.1.call-update) | async-done | bytes 7864336 | tf_op jit(solution)/shard_map/all_gather | solution.py:190
  126.6 4.4 %fusion.25 = f32[128,1280]{1,0:T(8,128)S(1)} fusion(bf16[128,3072]{1,0:T(8,128)(2,1)S(1)} %bitcast.33, bf16[3072,1280]{1,0:T(8,128)(2,1)} %all-gather.3.cloned.1.call-done.gathered_ref), kind=kOutput, calls=%fused_computation.43 | convolution fusion | flops 1006632960 | bytes 9306112 | tf_op jit(solution)/shard_map/dot_general | solution.py:216
  131.1 0.4 shard_map.68
  131.5 21.4 %all_to_all.49.every_ref = f32[64,3,128]{2,1,0:T(4,128)S(1)} all-to-all(f32[64,3,128]{2,1,0:T(4,128)S(1)} %shard_map.68), channel_id=1, replica_groups=mesh['dp'=8,'vocab'=64] {'vocab'}, dimensions={0} | all-to-all | bytes 196608 | tf_op jit(solution)/shard_map/all_to_all | solution.py:218
  152.9 1.0 shard_map.69.grads_ref
  154.0 8.2 %shard_map.70 = f32[8,128,512]{2,1,0:T(8,128)} custom-call(s32[1]{0:T(128)} %bitcast.1.me_ref, bf16[128,1280]{1,0:T(8,128)(2,1)} %shard_map.69.grads_ref, bf16[3072,1280]{1,0:T(8,128)(2,1)} %all-gather.3.cloned.1.call-done.gathered_ref, bf16[128,1280]{1,0:T(8,128)(2,1)} %slice.22.refs_0_, bf16[128,1280]{1,0:T(8,128)(2,1)} %collective-permute-done.refs_1_, ...), custom_call_target="tpu_custom_call" | custom-call | flops 1342177280 | bytes 12582912 | tf_op jit(solution)/shard_map/pallas_call | solution.py:122
  162.2 6.6 %all_to_all.50 = f32[2,4,128,512]{3,2,1,0:T(8,128)S(1)} all-to-all(f32[2,4,128,512]{3,2,1,0:T(8,128)} %bitcast.32), channel_id=1, replica_groups={{0,1},{2,3},{4,5},{6,7},{8,9},{10,11},{12,13},{14,15},{16,17},{18,19},{..., dimensions={0} | all-to-all | bytes 4194304 | tf_op jit(solution)/shard_map/all_to_all | solution.py:174
  169.0 19.6 %all_to_all.51 = bf16[32,16,512]{2,1,0:T(8,128)(2,1)S(1)} all-to-all(bf16[32,16,512]{2,1,0:T(8,128)(2,1)S(1)} %bitcast.37), channel_id=1, replica_groups={{0,2,4,6,8,10,12,14,16,18,20,22,24,26,28,30,32,34,36,38,40,42,44,46,48,..., dimensions={0} | all-to-all | bytes 1048576 | tf_op jit(solution)/shard_map/all_to_all | solution.py:179
  188.6 0.9 broadcast_in_dim.50
  189.5 5.2 %all-to-all-start.6 = ((bf16[32,16,512]{2,1,0:T(8,128)(2,1)}), bf16[32,16,512]{2,1,0:T(8,128)(2,1)S(1)}, u32[]{:S(2)}, u32[]{:S(2)}) async-start(bf16[32,16,512]{2,1,0:T(8,128)(2,1)} %broadcast_in_dim.50), calls=%async_computation.6 | async-start | bytes 1048576 | tf_op jit(solution)/shard_map/all_to_all | solution.py:26
  194.7 0.7 copy.12
  195.4 0.4 reshape.96
  195.9 4.4 %convolution_convert_fusion = bf16[512,1280]{1,0:T(8,128)(2,1)} fusion(bf16[1024,512]{1,0:T(8,128)(2,1)S(1)} %reshape.96, bf16[1024,1280]{1,0:T(8,128)(2,1)} %all-gather.5.cloned.1.call-done), kind=kOutput, calls=%fused_computation | convolution fusion | flops 1342832640 | bytes 4980736 | tf_op jit(solution)/shard_map/dot_general | solution.py:227
  200.3 9.5 %all-to-all-done.6 = bf16[32,16,512]{2,1,0:T(8,128)(2,1)S(1)} async-done(((bf16[32,16,512]{2,1,0:T(8,128)(2,1)}), bf16[32,16,512]{2,1,0:T(8,128)(2,1)S(1)}, u32[]{:S(2)}, u32[]{:S(2)}) %all-to-all-start.6) | async-done | bytes 524320 | tf_op jit(solution)/shard_map/all_to_all | solution.py:26
  209.7 5.5 %collective-permute-start.8 = (bf16[4,128,512]{2,1,0:T(8,128)(2,1)S(1)}, bf16[4,128,512]{2,1,0:T(8,128)(2,1)S(1)}, u32[]{:S(2)}, u32[]{:S(2)}) collective-permute-start(bf16[4,128,512]{2,1,0:T(8,128)(2,1)S(1)} %bitcast.30), channel_id=1, source_target_pairs={{0,1},{1,0},{2,3},{3,2},{4,5},{5,4},{6,7},{7,6},{8,9},{9,8},{10,11... | collective-permute-start | bytes 1572872 | tf_op jit(solution)/shard_map/ppermute | solution.py:232
  215.2 1.5 collective-permute-done.8.got_ref
  216.7 1.0 shard_map.71
  (37 shorter events, 1.3 us)
Async XLA Ops:
  7.2 2.5 %copy-start.2 = (bf16[512,1280]{1,0:T(8,128)(2,1)S(1)}, bf16[512,1280]{1,0:T(8,128)(2,1)}, u32[]{:S(2)}) copy-start(bf16[512,1280]{1,0:T(8,128)(2,1)} %param.6) | copy-start | bytes 3932164
  7.2 16.7 %copy-start.3 = (bf16[128,4096]{1,0:T(8,128)(2,1)S(1)}, bf16[128,4096]{1,0:T(8,128)(2,1)}, u32[]{:S(2)}) copy-start(bf16[128,4096]{1,0:T(8,128)(2,1)} %param.5) | copy-start | bytes 3145732
  7.2 40.9 %copy-start.5 = (f32[2]{0:T(128)S(1)}, f32[2]{0:T(128)}, u32[]{:S(2)}) copy-start(f32[2]{0:T(128)} %param.9) | copy-start | bytes 28
  7.2 41.2 %copy-start.6 = (s32[2]{0:T(128)S(1)}, s32[2]{0:T(128)}, u32[]{:S(2)}) copy-start(s32[2]{0:T(128)} %param.8) | copy-start | bytes 28
  7.2 119.4 %all-gather.3.cloned.1.call-start = ((), (), s32[]{:S(2)}) async-start(), calls=%async_computation.7 | async-start | bytes 8847360 | tf_op jit(solution)/shard_map/all_gather | solution.py:190
  10.4 41.3 %collective-permute-start.4 = (bf16[128,1280]{1,0:T(8,128)(2,1)}, bf16[128,1280]{1,0:T(8,128)(2,1)}, u32[]{:S(2)}, u32[]{:S(2)}) collective-permute-start(bf16[128,1280]{1,0:T(8,128)(2,1)} %slice.22.refs_0_), channel_id=1, source_target_pairs={{0,64},{64,128},{128,192},{192,256},{256,320},{320,384},{384,448},... | collective-permute-start | bytes 983048 | tf_op jit(solution)/shard_map/ppermute | solution.py:43
  15.2 33.3 %collective-permute-start = (bf16[128,1280]{1,0:T(8,128)(2,1)}, bf16[128,1280]{1,0:T(8,128)(2,1)}, u32[]{:S(2)}, u32[]{:S(2)}) collective-permute-start(bf16[128,1280]{1,0:T(8,128)(2,1)} %slice.22.refs_0_), channel_id=1, source_target_pairs={{0,448},{64,0},{128,64},{192,128},{256,192},{320,256},{384,320},{4... | collective-permute-start | bytes 983048 | tf_op jit(solution)/shard_map/ppermute | solution.py:43
  24.5 10.6 %all-to-all-start = ((bf16[8,2,512]{2,1,0:T(2,128)(2,1)}), bf16[8,2,512]{2,1,0:T(2,128)(2,1)S(1)}, u32[]{:S(2)}, u32[]{:S(2)}) async-start(bf16[8,2,512]{2,1,0:T(2,128)(2,1)} %bitcast.3), calls=%async_computation | async-start | bytes 32768 | tf_op jit(solution)/shard_map/all_to_all | solution.py:193
  35.1 16.4 %copy-start.4 = (bf16[8,2,512]{2,1,0:T(2,128)(2,1)}, bf16[8,2,512]{2,1,0:T(2,128)(2,1)S(1)}, u32[]{:S(2)}) copy-start(bf16[8,2,512]{2,1,0:T(2,128)(2,1)S(1)} %all-to-all-done) | copy-start | bytes 49156
  35.1 27.1 %all-to-all-start.2 = ((bf16[2,64,1280]{2,0,1:T(2,128)(2,1)}), bf16[2,64,1280]{2,0,1:T(2,128)(2,1)}, u32[]{:S(2)}, u32[]{:S(2)}) async-start(bf16[2,64,1280]{2,0,1:T(2,128)(2,1)} %bitcast.4), calls=%async_computation.2 | async-start | bytes 655360 | tf_op jit(solution)/shard_map/all_to_all | solution.py:192
  48.5 22.8 %collective-permute-start.1 = (bf16[128,1280]{1,0:T(8,128)(2,1)}, bf16[128,1280]{1,0:T(8,128)(2,1)}, u32[]{:S(2)}, u32[]{:S(2)}) collective-permute-start(bf16[128,1280]{1,0:T(8,128)(2,1)} %collective-permute-done.refs_1_), channel_id=1, source_target_pairs={{0,448},{64,0},{128,64},{192,128},{256,192},{320,256},{384,320},{4... | collective-permute-start | bytes 983048 | tf_op jit(solution)/shard_map/ppermute | solution.py:43
  51.7 24.4 %collective-permute-start.5 = (bf16[128,1280]{1,0:T(8,128)(2,1)}, bf16[128,1280]{1,0:T(8,128)(2,1)}, u32[]{:S(2)}, u32[]{:S(2)}) collective-permute-start(bf16[128,1280]{1,0:T(8,128)(2,1)} %collective-permute-done.4.refs_7_), channel_id=1, source_target_pairs={{0,64},{64,128},{128,192},{192,256},{256,320},{320,384},{384,448},... | collective-permute-start | bytes 983048 | tf_op jit(solution)/shard_map/ppermute | solution.py:43
  64.9 47.3 %all-to-all-start.1 = ((bf16[64,8,2,512]{3,2,1,0:T(2,128)(2,1)}), bf16[64,8,2,512]{3,2,1,0:T(2,128)(2,1)S(1)}, u32[]{:S(2)}, u32[]{:S(2)}) async-start(bf16[64,8,2,512]{3,2,1,0:T(2,128)(2,1)} %broadcast_in_dim.44), calls=%async_computation.1 | async-start | bytes 2097152 | tf_op jit(solution)/shard_map/all_to_all | solution.py:26
  70.0 125.9 %all-gather.5.cloned.1.call-start = ((), (), s32[]{:S(2)}) async-start(), calls=%async_computation.8 | async-start | bytes 2949120 | tf_op jit(solution)/shard_map/all_gather | solution.py:225
  71.3 18.6 %collective-permute-start.2 = (bf16[128,1280]{1,0:T(8,128)(2,1)}, bf16[128,1280]{1,0:T(8,128)(2,1)}, u32[]{:S(2)}, u32[]{:S(2)}) collective-permute-start(bf16[128,1280]{1,0:T(8,128)(2,1)} %collective-permute-done.1.refs_2_), channel_id=1, source_target_pairs={{0,448},{64,0},{128,64},{192,128},{256,192},{320,256},{384,320},{4... | collective-permute-start | bytes 983048 | tf_op jit(solution)/shard_map/ppermute | solution.py:43
  76.1 19.7 %collective-permute-start.6 = (bf16[128,1280]{1,0:T(8,128)(2,1)}, bf16[128,1280]{1,0:T(8,128)(2,1)S(1)}, u32[]{:S(2)}, u32[]{:S(2)}) collective-permute-start(bf16[128,1280]{1,0:T(8,128)(2,1)} %collective-permute-done.5.refs_6_), channel_id=1, source_target_pairs={{0,64},{64,128},{128,192},{192,256},{256,320},{320,384},{384,448},... | collective-permute-start | bytes 983048 | tf_op jit(solution)/shard_map/ppermute | solution.py:43
  90.9 11.1 %collective-permute-start.3 = (bf16[64,1280]{1,0:T(8,128)(2,1)S(1)}, bf16[64,1280]{1,0:T(8,128)(2,1)S(1)}, u32[]{:S(2)}, u32[]{:S(2)}) collective-permute-start(bf16[64,1280]{1,0:T(8,128)(2,1)S(1)} %slice.28), channel_id=1, source_target_pairs={{0,448},{64,0},{128,64},{192,128},{256,192},{320,256},{384,320},{4... | collective-permute-start | bytes 491528 | tf_op jit(solution)/shard_map/ppermute | solution.py:46
  95.9 15.3 %copy-start = (bf16[128,1280]{1,0:T(8,128)(2,1)}, bf16[128,1280]{1,0:T(8,128)(2,1)S(1)}, u32[]{:S(2)}) copy-start(bf16[128,1280]{1,0:T(8,128)(2,1)S(1)} %collective-permute-done.6.refs_5_) | copy-start | bytes 983044
  95.9 12.3 %collective-permute-start.7 = (bf16[64,1280]{1,0:T(8,128)(2,1)S(1)}, bf16[64,1280]{1,0:T(8,128)(2,1)S(1)}, u32[]{:S(2)}, u32[]{:S(2)}) collective-permute-start(bf16[64,1280]{1,0:T(8,128)(2,1)S(1)} %slice.29), channel_id=1, source_target_pairs={{0,64},{64,128},{128,192},{192,256},{256,320},{320,384},{384,448},... | collective-permute-start | bytes 491528 | tf_op jit(solution)/shard_map/ppermute | solution.py:46
  108.1 0.8 copy-start.1
  189.5 20.2 %all-to-all-start.6 = ((bf16[32,16,512]{2,1,0:T(8,128)(2,1)}), bf16[32,16,512]{2,1,0:T(8,128)(2,1)S(1)}, u32[]{:S(2)}, u32[]{:S(2)}) async-start(bf16[32,16,512]{2,1,0:T(8,128)(2,1)} %broadcast_in_dim.50), calls=%async_computation.6 | async-start | bytes 1048576 | tf_op jit(solution)/shard_map/all_to_all | solution.py:26
  209.7 7.0 %collective-permute-start.8 = (bf16[4,128,512]{2,1,0:T(8,128)(2,1)S(1)}, bf16[4,128,512]{2,1,0:T(8,128)(2,1)S(1)}, u32[]{:S(2)}, u32[]{:S(2)}) collective-permute-start(bf16[4,128,512]{2,1,0:T(8,128)(2,1)S(1)} %bitcast.30), channel_id=1, source_target_pairs={{0,1},{1,0},{2,3},{3,2},{4,5},{5,4},{6,7},{7,6},{8,9},{9,8},{10,11... | collective-permute-start | bytes 1572872 | tf_op jit(solution)/shard_map/ppermute | solution.py:232
Sparse Core Ops, SparseCore 0:
  10.7 115.8 all-gather.2
  154.1 34.2 all-gather.4

commit v7 on v6

--- a/solution.py
+++ b/solution.py
@@ -7,7 +7,7 @@
 
 SEQ_LEN = 64
 LOSS_SCALE = 32.0
-GATHERED = 12
+GATHERED = 11
 LANES = 128
 VMEM = pl.BlockSpec(memory_space=pltpu.VMEM)
 HBM = pl.BlockSpec(memory_space=pl.ANY)
@@ -33,19 +33,21 @@
     return mine.reshape(share, n_dp, d // n_dp).transpose(1, 0, 2)
 
 
-def ring_blocks(block, n):
+def ring_blocks(block, n, beside):
     right = [(i, (i + 1) % n) for i in range(n)]
     left = [(i, (i - 1) % n) for i in range(n)]
     half = block.shape[0] // 2
     got = {0: block}
     up = down = block
     for step in range(1, n // 2):
+        if step == 3:
+            down, up, beside = lax.optimization_barrier((down, up, beside))
         down, up = lax.ppermute(down, "dp", left), lax.ppermute(up, "dp", right)
         got[step], got[n - step] = down, up
     got[n // 2] = jnp.concatenate(
         [lax.ppermute(down[:half], "dp", left), lax.ppermute(up[half:], "dp", right)]
     )
-    return [got[k] for k in range(n)]
+    return [got[k] for k in range(n)], beside
 
 
 def along_lanes(column, rows):
@@ -188,8 +190,8 @@
     tok_rows = hidden.shape[0]
     deep = depth * GATHERED // 16
     gathered = lax.all_gather(head_weight[:deep], "dp", axis=0, tiled=True)
-    pieces = ring_blocks(head_weight[deep:], n_dp)
     teacher = lax.all_to_all(teacher_logprobs, "vocab", split_axis=1, concat_axis=0, tiled=True)
+    pieces, teacher = ring_blocks(head_weight[deep:], n_dp, teacher)
     share = lax.all_to_all(hidden_share(hidden, n_dp, n_v), "dp", 0, 0)
     everyone = spread(share, n_v)
 

time: 226 us -> 224 us (level)
  waiting for transfers between devices: 59.9 us -> 47.5 us
  starting transfers between devices: 62.2 us -> 70.7 us
    all_gather x1, waiting for transfers between devices: 14.4 us -> 1.96 us  [body(): gathered = lax.all_gather(head_weight[:deep], 'dp', axis=0, tiled=True)]
    ppermute x6, waiting for transfers between devices: 9.84 us -> 15.6 us  [ring_blocks(): down, up = (lax.ppermute(down, 'dp', left), lax.ppermute(up, 'dp', right))]
    all_to_all x1, waiting for transfers between devices: 7.63 us -> 2.81 us  [body(): lax.all_to_all(teacher_logprobs, 'vocab', split_axis=1, concat_axis=0, ti...]
    ppermute x6, starting transfers between devices: 24 us -> 27.8 us  [ring_blocks(): down, up = (lax.ppermute(down, 'dp', left), lax.ppermute(up, 'dp', right))]
    all_to_all x2, starting transfers between devices: 10.3 us -> 13 us  [spread(): return lax.all_to_all(copies, axis, 0, 0, axis_index_groups=groups)]
  transfers between devices with their start and end apart: 15 -> 15, of which waited for: 9 -> 10; matrix products, arithmetic and copies ran while one was open for 9% -> 11% of each run, Pallas kernels for 4% -> 4%
where the time goes in v7:
time: 224 us; the launch traced here: 223 us
  starting transfers between devices  70.7 us (32%)
  blocking collectives  48.2 us (22%)
  waiting for transfers between devices  47.5 us (21%)
  matrix products  18.9 us (8%)
  between operations  14.5 us (6%)
  Pallas kernels  10.7 us (5%)
  local copies, waits for them, and re-layouts  10.3 us (5%)
  other arithmetic  2.34 us (1%)
    ppermute x6, starting transfers between devices, ring_blocks(): down, up = (lax.ppermute(down, 'dp', left), lax.ppermute(up, 'dp', right))  27.8 us
    all_to_all x1, blocking collectives, body(): every = lax.all_to_all(stats, 'vocab', 0, 0)  22 us
    all_to_all x1, blocking collectives, sum_terms(): lax.all_to_all(mine, 'vocab', 0, 0, axis_index_groups=core_groups(n_v))  19.6 us
    ppermute x6, waiting for transfers between devices, ring_blocks(): down, up = (lax.ppermute(down, 'dp', left), lax.ppermute(up, 'dp', right))  15.6 us
    all_to_all x1, starting transfers between devices, body(): lax.all_to_all(teacher_logprobs, 'vocab', split_axis=1, concat_axis=0, ti...  13.3 us
    all_to_all x2, starting transfers between devices, spread(): return lax.all_to_all(copies, axis, 0, 0, axis_index_groups=groups)  13 us
    dot_general x8, matrix products, body(): term = jnp.dot(feats, pieces[k], preferred_element_type=jnp.float32)  10.4 us
    all_to_all x2, waiting for transfers between devices, spread(): return lax.all_to_all(copies, axis, 0, 0, axis_index_groups=groups)  9.5 us
  transfers between devices with their start and end apart: 15, of which 10 were waited for; matrix products, arithmetic and copies ran while one was open for 11% of the time, Pallas kernels for 4%

profile of v7, /device:TPU:1, one launch (start us, length us, event | category | flops | bytes accessed | tf_op | source)
XLA Modules:
  0.0 223.2 jit_solution(964233033914273791)
XLA Ops:
  7.2 2.2 slice.21
  9.5 1.0 slice.22.refs_0_
  10.5 4.8 %collective-permute-start.2 = (bf16[160,1280]{1,0:T(8,128)(2,1)S(1)}, bf16[160,1280]{1,0:T(8,128)(2,1)}, u32[]{:S(2)}, u32[]{:S(2)}) collective-permute-start(bf16[160,1280]{1,0:T(8,128)(2,1)S(1)} %slice.22.refs_0_), channel_id=1, source_target_pairs={{0,64},{64,128},{128,192},{192,256},{256,320},{320,384},{384,448},... | collective-permute-start | bytes 1228808 | tf_op jit(solution)/shard_map/ppermute | solution.py:45
  15.4 8.6 %collective-permute-start = (bf16[160,1280]{1,0:T(8,128)(2,1)S(1)}, bf16[160,1280]{1,0:T(8,128)(2,1)}, u32[]{:S(2)}, u32[]{:S(2)}) collective-permute-start(bf16[160,1280]{1,0:T(8,128)(2,1)S(1)} %slice.22.refs_0_), channel_id=1, source_target_pairs={{0,448},{64,0},{128,64},{192,128},{256,192},{320,256},{384,320},{4... | collective-permute-start | bytes 1228808 | tf_op jit(solution)/shard_map/ppermute | solution.py:45
  24.6 3.9 %all-to-all-start = ((bf16[8,2,512]{2,1,0:T(2,128)(2,1)}), bf16[8,2,512]{2,1,0:T(2,128)(2,1)S(1)}, u32[]{:S(2)}, u32[]{:S(2)}) async-start(bf16[8,2,512]{2,1,0:T(2,128)(2,1)} %bitcast.3), calls=%async_computation | async-start | bytes 32768 | tf_op jit(solution)/shard_map/all_to_all | solution.py:195
  28.5 6.7 %all-to-all-done = bf16[8,2,512]{2,1,0:T(2,128)(2,1)S(1)} async-done(((bf16[8,2,512]{2,1,0:T(2,128)(2,1)}), bf16[8,2,512]{2,1,0:T(2,128)(2,1)S(1)}, u32[]{:S(2)}, u32[]{:S(2)}) %all-to-all-start) | async-done | bytes 16416 | tf_op jit(solution)/shard_map/all_to_all | solution.py:195
  35.2 13.3 %all-to-all-start.2 = ((bf16[2,64,1280]{2,0,1:T(2,128)(2,1)}), bf16[2,64,1280]{2,0,1:T(2,128)(2,1)S(1)}, u32[]{:S(2)}, u32[]{:S(2)}) async-start(bf16[2,64,1280]{2,0,1:T(2,128)(2,1)} %bitcast.4), calls=%async_computation.2 | async-start | bytes 655360 | tf_op jit(solution)/shard_map/all_to_all | solution.py:193
  49.1 0.7 copy.14
  49.9 0.7 select_reduce_fusion.1
  50.7 1.9 collective-permute-start.3
  52.6 5.2 %collective-permute-start.1 = (bf16[160,1280]{1,0:T(8,128)(2,1)}, bf16[160,1280]{1,0:T(8,128)(2,1)}, u32[]{:S(2)}, u32[]{:S(2)}) collective-permute-start(bf16[160,1280]{1,0:T(8,128)(2,1)} %collective-permute-done.refs_1_), channel_id=1, source_target_pairs={{0,448},{64,0},{128,64},{192,128},{256,192},{320,256},{384,320},{4... | collective-permute-start | bytes 1228808 | tf_op jit(solution)/shard_map/ppermute | solution.py:45
  57.9 0.7 compare_select_fusion.weight_ref
  58.5 1.3 fusion.16
  59.9 2.8 %all-to-all-done.2 = bf16[2,64,1280]{2,0,1:T(2,128)(2,1)S(1)} async-done(((bf16[2,64,1280]{2,0,1:T(2,128)(2,1)}), bf16[2,64,1280]{2,0,1:T(2,128)(2,1)S(1)}, u32[]{:S(2)}, u32[]{:S(2)}) %all-to-all-start.2) | async-done | bytes 327712 | tf_op jit(solution)/shard_map/all_to_all | solution.py:193
  62.7 2.7 %broadcast_in_dim.44 = bf16[64,8,2,512]{3,2,1,0:T(2,128)(2,1)} broadcast(bf16[8,2,512]{2,1,0:T(2,128)(2,1)} %copy-done.5), dimensions={1,2,3} | broadcast | bytes 1064960 | tf_op jit(solution)/shard_map/broadcast_in_dim | solution.py:25
  65.4 7.8 %all-to-all-start.1 = ((bf16[64,8,2,512]{3,2,1,0:T(2,128)(2,1)}), bf16[64,8,2,512]{3,2,1,0:T(2,128)(2,1)S(1)}, u32[]{:S(2)}, u32[]{:S(2)}) async-start(bf16[64,8,2,512]{3,2,1,0:T(2,128)(2,1)} %broadcast_in_dim.44), calls=%async_computation.1 | async-start | bytes 2097152 | tf_op jit(solution)/shard_map/all_to_all | solution.py:26
  73.4 1.4 collective-permute-done.3.refs_6_
  74.8 1.1 collective-permute-done.1.refs_2_
  75.9 5.3 %collective-permute-start.4 = (bf16[160,1280]{1,0:T(8,128)(2,1)}, bf16[160,1280]{1,0:T(8,128)(2,1)S(1)}, u32[]{:S(2)}, u32[]{:S(2)}) collective-permute-start(bf16[160,1280]{1,0:T(8,128)(2,1)} %collective-permute-done.1.refs_2_), channel_id=1, source_target_pairs={{0,448},{64,0},{128,64},{192,128},{256,192},{320,256},{384,320},{4... | collective-permute-start | bytes 1228808 | tf_op jit(solution)/shard_map/ppermute | solution.py:45
  81.2 1.9 collective-permute-start.6
  83.1 1.4 convolution_add_fusion.2
  84.5 1.3 fusion.5
  85.8 13.1 %collective-permute-done.4.refs_3_ = bf16[160,1280]{1,0:T(8,128)(2,1)S(1)} collective-permute-done((bf16[160,1280]{1,0:T(8,128)(2,1)}, bf16[160,1280]{1,0:T(8,128)(2,1)S(1)}, u32[]{:S(2)}, u32[]{:S(2)}) %collective-permute-start.4) | collective-permute-done | bytes 409632 | tf_op jit(solution)/shard_map/ppermute | solution.py:45
  99.0 5.3 %collective-permute-start.5 = (bf16[80,1280]{1,0:T(8,128)(2,1)S(1)}, bf16[80,1280]{1,0:T(8,128)(2,1)S(1)}, u32[]{:S(2)}, u32[]{:S(2)}) collective-permute-start(bf16[80,1280]{1,0:T(8,128)(2,1)S(1)} %slice.28), channel_id=1, source_target_pairs={{0,448},{64,0},{128,64},{192,128},{256,192},{320,256},{384,320},{4... | collective-permute-start | bytes 614408 | tf_op jit(solution)/shard_map/ppermute | solution.py:48
  104.3 1.9 collective-permute-start.7
  106.3 1.2 fusion.8
  107.5 1.2 fusion.12
  108.7 4.0 %collective-permute-done.5 = bf16[80,1280]{1,0:T(8,128)(2,1)S(1)} collective-permute-done((bf16[80,1280]{1,0:T(8,128)(2,1)S(1)}, bf16[80,1280]{1,0:T(8,128)(2,1)S(1)}, u32[]{:S(2)}, u32[]{:S(2)}) %collective-permute-start.5) | collective-permute-done | bytes 204832 | tf_op jit(solution)/shard_map/ppermute | solution.py:48
  112.7 5.4 %collective-permute-done.7 = bf16[80,1280]{1,0:T(8,128)(2,1)S(1)} collective-permute-done((bf16[80,1280]{1,0:T(8,128)(2,1)S(1)}, bf16[80,1280]{1,0:T(8,128)(2,1)S(1)}, u32[]{:S(2)}, u32[]{:S(2)}) %collective-permute-start.7) | collective-permute-done | bytes 204832 | tf_op jit(solution)/shard_map/ppermute | solution.py:48
  118.1 0.8 copy-done.2
  118.9 1.2 fusion.10
  120.1 1.4 fusion.3
  121.5 1.4 fusion
  122.8 2.0 all-gather.3.cloned.1.call-done.gathered_ref
  124.8 4.2 %fusion.27 = f32[128,1280]{1,0:T(8,128)S(1)} fusion(bf16[128,2816]{0,1:T(8,128)(2,1)S(1)} %bitcast.31, bf16[2816,1280]{1,0:T(8,128)(2,1)} %all-gather.3.cloned.1.call-done.gathered_ref), kind=kOutput, calls=%fused_computation.44 | convolution fusion | flops 922746880 | bytes 8585216 | tf_op jit(solution)/shard_map/dot_general | solution.py:218
  129.5 22.0 %all_to_all.49.every_ref = f32[64,3,128]{2,1,0:T(4,128)S(1)} all-to-all(f32[64,3,128]{2,1,0:T(4,128)S(1)} %shard_map.68), channel_id=1, replica_groups=mesh['dp'=8,'vocab'=64] {'vocab'}, dimensions={0} | all-to-all | bytes 196608 | tf_op jit(solution)/shard_map/all_to_all | solution.py:220
  151.5 1.0 shard_map.69.grads_ref
  152.6 8.2 %shard_map.70 = f32[8,128,512]{2,1,0:T(8,128)} custom-call(s32[1]{0:T(128)} %bitcast.1.me_ref, bf16[128,1280]{1,0:T(8,128)(2,1)} %shard_map.69.grads_ref, bf16[2816,1280]{1,0:T(8,128)(2,1)} %all-gather.3.cloned.1.call-done.gathered_ref, bf16[160,1280]{1,0:T(8,128)(2,1)} %copy-done.4, bf16[160,1280]{1,0:T(8,128)(2,1)} %collective-permute-done.refs_1_, ...), custom_call_target="tpu_custom_call" | custom-call | flops 1342177280 | bytes 12582912 | tf_op jit(solution)/shard_map/pallas_call | solution.py:124
  160.8 6.6 %all_to_all.50 = f32[2,4,128,512]{3,2,1,0:T(8,128)S(1)} all-to-all(f32[2,4,128,512]{3,2,1,0:T(8,128)} %bitcast.30), channel_id=1, replica_groups={{0,1},{2,3},{4,5},{6,7},{8,9},{10,11},{12,13},{14,15},{16,17},{18,19},{..., dimensions={0} | all-to-all | bytes 4194304 | tf_op jit(solution)/shard_map/all_to_all | solution.py:176
  167.6 19.6 %all_to_all.51 = bf16[32,16,512]{2,1,0:T(8,128)(2,1)S(1)} all-to-all(bf16[32,16,512]{2,1,0:T(8,128)(2,1)S(1)} %bitcast.34), channel_id=1, replica_groups={{0,2,4,6,8,10,12,14,16,18,20,22,24,26,28,30,32,34,36,38,40,42,44,46,48,..., dimensions={0} | all-to-all | bytes 1048576 | tf_op jit(solution)/shard_map/all_to_all | solution.py:181
  187.2 0.9 broadcast_in_dim.50
  188.1 5.2 %all-to-all-start.6 = ((bf16[32,16,512]{2,1,0:T(8,128)(2,1)}), bf16[32,16,512]{2,1,0:T(8,128)(2,1)S(1)}, u32[]{:S(2)}, u32[]{:S(2)}) async-start(bf16[32,16,512]{2,1,0:T(8,128)(2,1)} %broadcast_in_dim.50), calls=%async_computation.6 | async-start | bytes 1048576 | tf_op jit(solution)/shard_map/all_to_all | solution.py:26
  193.3 0.7 copy.15
  194.5 4.4 %convolution_convert_fusion = bf16[512,1280]{1,0:T(8,128)(2,1)} fusion(bf16[1024,512]{1,0:T(8,128)(2,1)S(1)} %reshape.96, bf16[1024,1280]{1,0:T(8,128)(2,1)} %all-gather.5.cloned.1.call-done), kind=kOutput, calls=%fused_computation | convolution fusion | flops 1342832640 | bytes 4980736 | tf_op jit(solution)/shard_map/dot_general | solution.py:229
  198.8 9.5 %all-to-all-done.6 = bf16[32,16,512]{2,1,0:T(8,128)(2,1)S(1)} async-done(((bf16[32,16,512]{2,1,0:T(8,128)(2,1)}), bf16[32,16,512]{2,1,0:T(8,128)(2,1)S(1)}, u32[]{:S(2)}, u32[]{:S(2)}) %all-to-all-start.6) | async-done | bytes 524320 | tf_op jit(solution)/shard_map/all_to_all | solution.py:26
  208.3 5.5 %collective-permute-start.8 = (bf16[4,128,512]{2,1,0:T(8,128)(2,1)S(1)}, bf16[4,128,512]{2,1,0:T(8,128)(2,1)S(1)}, u32[]{:S(2)}, u32[]{:S(2)}) collective-permute-start(bf16[4,128,512]{2,1,0:T(8,128)(2,1)S(1)} %bitcast.28), channel_id=1, source_target_pairs={{0,1},{1,0},{2,3},{3,2},{4,5},{5,4},{6,7},{7,6},{8,9},{9,8},{10,11... | collective-permute-start | bytes 1572872 | tf_op jit(solution)/shard_map/ppermute | solution.py:234
  213.8 1.5 collective-permute-done.8.got_ref
  215.3 1.0 shard_map.71
  (38 shorter events, 2.8 us)
Async XLA Ops:
  7.2 16.8 %copy-start.3 = (bf16[128,4096]{1,0:T(8,128)(2,1)S(1)}, bf16[128,4096]{1,0:T(8,128)(2,1)}, u32[]{:S(2)}) copy-start(bf16[128,4096]{1,0:T(8,128)(2,1)} %param.5) | copy-start | bytes 3145732
  7.2 41.3 %copy-start.6 = (f32[2]{0:T(128)S(1)}, f32[2]{0:T(128)}, u32[]{:S(2)}) copy-start(f32[2]{0:T(128)} %param.9) | copy-start | bytes 28
  7.2 117.6 %all-gather.3.cloned.1.call-start = ((), (), s32[]{:S(2)}) async-start(), calls=%async_computation.7 | async-start | bytes 8110080 | tf_op jit(solution)/shard_map/all_gather | solution.py:192
  10.5 49.4 %copy-start.4 = (bf16[160,1280]{1,0:T(8,128)(2,1)}, bf16[160,1280]{1,0:T(8,128)(2,1)S(1)}, u32[]{:S(2)}) copy-start(bf16[160,1280]{1,0:T(8,128)(2,1)S(1)} %slice.22.refs_0_) | copy-start | bytes 1228804
  10.5 40.2 %collective-permute-start.2 = (bf16[160,1280]{1,0:T(8,128)(2,1)S(1)}, bf16[160,1280]{1,0:T(8,128)(2,1)}, u32[]{:S(2)}, u32[]{:S(2)}) collective-permute-start(bf16[160,1280]{1,0:T(8,128)(2,1)S(1)} %slice.22.refs_0_), channel_id=1, source_target_pairs={{0,64},{64,128},{128,192},{192,256},{256,320},{320,384},{384,448},... | collective-permute-start | bytes 1228808 | tf_op jit(solution)/shard_map/ppermute | solution.py:45
  15.4 37.2 %collective-permute-start = (bf16[160,1280]{1,0:T(8,128)(2,1)S(1)}, bf16[160,1280]{1,0:T(8,128)(2,1)}, u32[]{:S(2)}, u32[]{:S(2)}) collective-permute-start(bf16[160,1280]{1,0:T(8,128)(2,1)S(1)} %slice.22.refs_0_), channel_id=1, source_target_pairs={{0,448},{64,0},{128,64},{192,128},{256,192},{320,256},{384,320},{4... | collective-permute-start | bytes 1228808 | tf_op jit(solution)/shard_map/ppermute | solution.py:45
  24.6 10.6 %all-to-all-start = ((bf16[8,2,512]{2,1,0:T(2,128)(2,1)}), bf16[8,2,512]{2,1,0:T(2,128)(2,1)S(1)}, u32[]{:S(2)}, u32[]{:S(2)}) async-start(bf16[8,2,512]{2,1,0:T(2,128)(2,1)} %bitcast.3), calls=%async_computation | async-start | bytes 32768 | tf_op jit(solution)/shard_map/all_to_all | solution.py:195
  28.5 21.3 %copy-start.7 = (s32[128]{0:T(128)}, s32[128]{0:T(128)S(1)}, u32[]{:S(2)}) copy-start(s32[128]{0:T(128)S(1)} %and_select_fusion) | copy-start | bytes 1540
  35.2 14.6 %copy-start.5 = (bf16[8,2,512]{2,1,0:T(2,128)(2,1)}, bf16[8,2,512]{2,1,0:T(2,128)(2,1)S(1)}, u32[]{:S(2)}) copy-start(bf16[8,2,512]{2,1,0:T(2,128)(2,1)S(1)} %all-to-all-done) | copy-start | bytes 49156
  35.2 27.4 %all-to-all-start.2 = ((bf16[2,64,1280]{2,0,1:T(2,128)(2,1)}), bf16[2,64,1280]{2,0,1:T(2,128)(2,1)S(1)}, u32[]{:S(2)}, u32[]{:S(2)}) async-start(bf16[2,64,1280]{2,0,1:T(2,128)(2,1)} %bitcast.4), calls=%async_computation.2 | async-start | bytes 655360 | tf_op jit(solution)/shard_map/all_to_all | solution.py:193
  50.7 24.1 %collective-permute-start.3 = (bf16[160,1280]{1,0:T(8,128)(2,1)}, bf16[160,1280]{1,0:T(8,128)(2,1)}, u32[]{:S(2)}, u32[]{:S(2)}) collective-permute-start(bf16[160,1280]{1,0:T(8,128)(2,1)} %collective-permute-done.2.refs_7_), channel_id=1, source_target_pairs={{0,64},{64,128},{128,192},{192,256},{256,320},{320,384},{384,448},... | collective-permute-start | bytes 1228808 | tf_op jit(solution)/shard_map/ppermute | solution.py:45
  52.6 23.3 %collective-permute-start.1 = (bf16[160,1280]{1,0:T(8,128)(2,1)}, bf16[160,1280]{1,0:T(8,128)(2,1)}, u32[]{:S(2)}, u32[]{:S(2)}) collective-permute-start(bf16[160,1280]{1,0:T(8,128)(2,1)} %collective-permute-done.refs_1_), channel_id=1, source_target_pairs={{0,448},{64,0},{128,64},{192,128},{256,192},{320,256},{384,320},{4... | collective-permute-start | bytes 1228808 | tf_op jit(solution)/shard_map/ppermute | solution.py:45
  65.4 57.4 %all-to-all-start.1 = ((bf16[64,8,2,512]{3,2,1,0:T(2,128)(2,1)}), bf16[64,8,2,512]{3,2,1,0:T(2,128)(2,1)S(1)}, u32[]{:S(2)}, u32[]{:S(2)}) async-start(bf16[64,8,2,512]{3,2,1,0:T(2,128)(2,1)} %broadcast_in_dim.44), calls=%async_computation.1 | async-start | bytes 2097152 | tf_op jit(solution)/shard_map/all_to_all | solution.py:26
  73.2 121.3 %all-gather.5.cloned.1.call-start = ((), (), s32[]{:S(2)}) async-start(), calls=%async_computation.8 | async-start | bytes 2949120 | tf_op jit(solution)/shard_map/all_gather | solution.py:227
  75.9 23.1 %collective-permute-start.4 = (bf16[160,1280]{1,0:T(8,128)(2,1)}, bf16[160,1280]{1,0:T(8,128)(2,1)S(1)}, u32[]{:S(2)}, u32[]{:S(2)}) collective-permute-start(bf16[160,1280]{1,0:T(8,128)(2,1)} %collective-permute-done.1.refs_2_), channel_id=1, source_target_pairs={{0,448},{64,0},{128,64},{192,128},{256,192},{320,256},{384,320},{4... | collective-permute-start | bytes 1228808 | tf_op jit(solution)/shard_map/ppermute | solution.py:45
  81.2 23.1 %collective-permute-start.6 = (bf16[160,1280]{1,0:T(8,128)(2,1)}, bf16[160,1280]{1,0:T(8,128)(2,1)S(1)}, u32[]{:S(2)}, u32[]{:S(2)}) collective-permute-start(bf16[160,1280]{1,0:T(8,128)(2,1)} %collective-permute-done.3.refs_6_), channel_id=1, source_target_pairs={{0,64},{64,128},{128,192},{192,256},{256,320},{320,384},{384,448},... | collective-permute-start | bytes 1228808 | tf_op jit(solution)/shard_map/ppermute | solution.py:45
  98.9 22.5 %copy-start = (bf16[160,1280]{1,0:T(8,128)(2,1)}, bf16[160,1280]{1,0:T(8,128)(2,1)S(1)}, u32[]{:S(2)}) copy-start(bf16[160,1280]{1,0:T(8,128)(2,1)S(1)} %collective-permute-done.4.refs_3_) | copy-start | bytes 1228804
  99.0 13.7 %collective-permute-start.5 = (bf16[80,1280]{1,0:T(8,128)(2,1)S(1)}, bf16[80,1280]{1,0:T(8,128)(2,1)S(1)}, u32[]{:S(2)}, u32[]{:S(2)}) collective-permute-start(bf16[80,1280]{1,0:T(8,128)(2,1)S(1)} %slice.28), channel_id=1, source_target_pairs={{0,448},{64,0},{128,64},{192,128},{256,192},{320,256},{384,320},{4... | collective-permute-start | bytes 614408 | tf_op jit(solution)/shard_map/ppermute | solution.py:48
  104.3 13.8 %copy-start.1 = (bf16[160,1280]{1,0:T(8,128)(2,1)}, bf16[160,1280]{1,0:T(8,128)(2,1)S(1)}, u32[]{:S(2)}) copy-start(bf16[160,1280]{1,0:T(8,128)(2,1)S(1)} %collective-permute-done.6.refs_5_) | copy-start | bytes 1228804
  104.3 13.7 %collective-permute-start.7 = (bf16[80,1280]{1,0:T(8,128)(2,1)S(1)}, bf16[80,1280]{1,0:T(8,128)(2,1)S(1)}, u32[]{:S(2)}, u32[]{:S(2)}) collective-permute-start(bf16[80,1280]{1,0:T(8,128)(2,1)S(1)} %slice.29), channel_id=1, source_target_pairs={{0,64},{64,128},{128,192},{192,256},{256,320},{320,384},{384,448},... | collective-permute-start | bytes 614408 | tf_op jit(solution)/shard_map/ppermute | solution.py:48
  118.1 0.8 copy-start.2
  188.1 20.3 %all-to-all-start.6 = ((bf16[32,16,512]{2,1,0:T(8,128)(2,1)}), bf16[32,16,512]{2,1,0:T(8,128)(2,1)S(1)}, u32[]{:S(2)}, u32[]{:S(2)}) async-start(bf16[32,16,512]{2,1,0:T(8,128)(2,1)} %broadcast_in_dim.50), calls=%async_computation.6 | async-start | bytes 1048576 | tf_op jit(solution)/shard_map/all_to_all | solution.py:26
  208.3 7.0 %collective-permute-start.8 = (bf16[4,128,512]{2,1,0:T(8,128)(2,1)S(1)}, bf16[4,128,512]{2,1,0:T(8,128)(2,1)S(1)}, u32[]{:S(2)}, u32[]{:S(2)}) collective-permute-start(bf16[4,128,512]{2,1,0:T(8,128)(2,1)S(1)} %bitcast.28), channel_id=1, source_target_pairs={{0,1},{1,0},{2,3},{3,2},{4,5},{5,4},{6,7},{7,6},{8,9},{9,8},{10,11... | collective-permute-start | bytes 1572872 | tf_op jit(solution)/shard_map/ppermute | solution.py:234
Sparse Core Ops, SparseCore 0:
  10.7 114.0 all-gather.2
  152.7 34.7 all-gather.4

commit v8 on v7

--- a/solution.py
+++ b/solution.py
@@ -11,10 +11,6 @@
 LANES = 128
 VMEM = pl.BlockSpec(memory_space=pltpu.VMEM)
 HBM = pl.BlockSpec(memory_space=pl.ANY)
-
-
-def pair_groups(n):
-    return [[2 * i, 2 * i + 1] for i in range(n // 2)]
 
 
 def core_groups(n):
@@ -86,11 +82,12 @@
         out_ref[:, cols] = (factor * jnp.exp(shifted) * gap).astype(jnp.bfloat16)
 
 
-def terms_kernel(me_ref, grads_ref, gathered_ref, *refs):
-    pieces, (out_ref, head, sems, piece_sems) = refs[:-4], refs[-4:]
+def terms_kernel(place_ref, grads_ref, gathered_ref, *refs):
+    pieces, (kept_ref, sent_ref, head, sems, piece_sems) = refs[:-5], refs[-5:]
     blocks, depth, _ = head.shape
     deep = depth - pieces[0].shape[0]
-    places = [lax.rem(me_ref[0] + j, blocks) for j in range(blocks)]
+    places = [lax.rem(place_ref[0] + j, blocks) for j in range(blocks)]
+    some = blocks // 2
     copies = [
         (
             pltpu.make_async_copy(
@@ -111,21 +108,31 @@
     for j, pair in enumerate(copies):
         for copy in pair:
             copy.wait()
-        out_ref[places[j]] = lax.dot_general(
+        term = lax.dot_general(
             grads, head[j], (((1,), (1,)), ((), ())), preferred_element_type=jnp.float32
         )
-
-
-def hidden_terms(me, grads, gathered, pieces):
+        place = lax.rem(places[j], some)
+        mine = (places[j] >= some) == (place_ref[1] == 1)
+
+        @pl.when(mine)
+        def _():
+            kept_ref[place] = term
+
+        @pl.when(jnp.logical_not(mine))
+        def _():
+            sent_ref[place] = term
+
+
+def hidden_terms(me, core, grads, gathered, pieces):
     rows, width = grads.shape
     blocks = len(pieces)
     deep, rest = gathered.shape[0] // blocks, pieces[0].shape[0]
     d = blocks * (deep + rest)
     return pl.pallas_call(
         terms_kernel,
-        out_shape=jax.ShapeDtypeStruct((blocks, rows, deep + rest), jnp.float32),
+        out_shape=(jax.ShapeDtypeStruct((blocks // 2, rows, deep + rest), jnp.float32),) * 2,
         in_specs=[pl.BlockSpec(memory_space=pltpu.SMEM), VMEM, HBM] + [HBM] * blocks,
-        out_specs=VMEM,
+        out_specs=(VMEM, VMEM),
         scratch_shapes=[
             pltpu.VMEM((blocks, deep + rest, width), gathered.dtype),
             pltpu.SemaphoreType.DMA((blocks,)),
@@ -135,7 +142,7 @@
         cost_estimate=pl.CostEstimate(
             flops=2 * rows * d * width, bytes_accessed=2 * d * width + 4 * rows * d, transcendentals=0
         ),
-    )(me.reshape(1), grads, gathered, *pieces)
+    )(jnp.stack([me, core]), grads, gathered, *pieces)
 
 
 def halves_kernel(core_ref, kept_ref, got_ref, out_ref):
@@ -170,14 +177,11 @@
     )(*args)
 
 
-def sum_terms(terms, n_v):
-    blocks, rows, d = terms.shape
+def sum_terms(kept, sent, n_v):
+    blocks, rows, d = kept.shape
     many = n_v // 2
-    swapped = lax.all_to_all(
-        terms.reshape(2, blocks // 2, rows, d), "vocab", 0, 0, axis_index_groups=pair_groups(n_v)
-    )
-    mine = (swapped[0] + swapped[1]).astype(jnp.bfloat16)
-    mine = mine.reshape(many, blocks // 2 * rows // many, d)
+    got = lax.ppermute(sent, "vocab", [(i, i ^ 1) for i in range(n_v)])
+    mine = (kept + got).astype(jnp.bfloat16).reshape(many, blocks * rows // many, d)
     parts = lax.all_to_all(mine, "vocab", 0, 0, axis_index_groups=core_groups(n_v))
     total = jnp.sum(parts.astype(jnp.float32), axis=0).astype(jnp.bfloat16)
     return spread(total, many, core_groups(n_v))
@@ -225,7 +229,9 @@
     everyone, grad_logits = lax.optimization_barrier((everyone, grad_logits))
     slices = everyone.transpose(1, 0, 2, 3).reshape(n_dp * tok_rows, depth)
     all_grads = lax.all_gather(grad_logits, "dp", axis=0, tiled=True)
-    whole = sum_terms(hidden_terms(me, grad_logits, gathered, pieces), n_v)
+    core = lax.rem(lax.axis_index("vocab"), 2)
+    kept, sent = hidden_terms(me, core, grad_logits, gathered, pieces)
+    whole = sum_terms(kept, sent, n_v)
     grad_head = lax.dot_general(
         slices, all_grads, (((0,), (0,)), ((), ())), preferred_element_type=jnp.float32
     ).astype(jnp.bfloat16)

time: 224 us -> 225 us (level)
  blocking collectives: 48.2 us -> 41.6 us
  waiting for transfers between devices: 47.5 us -> 50.1 us
    all_to_all x1 -> x0, blocking collectives: 6.64 us -> none  [sum_terms(): lax.all_to_all(terms.reshape(2, blocks // 2, rows, d), 'vocab', 0, 0, axi...]
    ppermute x0 -> x1, waiting for transfers between devices: none -> 2.48 us  [sum_terms(): got = lax.ppermute(sent, 'vocab', [(i, i ^ 1) for i in range(n_v)])]
    ppermute x0 -> x1, starting transfers between devices: none -> 2.3 us  [sum_terms(): got = lax.ppermute(sent, 'vocab', [(i, i ^ 1) for i in range(n_v)])]
  transfers between devices with their start and end apart: 15 -> 16, of which waited for: 10 -> 11; matrix products, arithmetic and copies ran while one was open for 11% -> 12% of each run, Pallas kernels for 4% -> 4%
where the time goes in v8:
time: 225 us; the launch traced here: 223 us
  starting transfers between devices  72.9 us (32%)
  waiting for transfers between devices  50.1 us (22%)
  blocking collectives  41.6 us (18%)
  matrix products  18.9 us (8%)
  between operations  14.5 us (6%)
  Pallas kernels  10.8 us (5%)
  local copies, waits for them, and re-layouts  10.3 us (5%)
  other arithmetic  4.27 us (2%)
    ppermute x6, starting transfers between devices, ring_blocks(): down, up = (lax.ppermute(down, 'dp', left), lax.ppermute(up, 'dp', right))  27.8 us
    all_to_all x1, blocking collectives, body(): every = lax.all_to_all(stats, 'vocab', 0, 0)  22 us
    all_to_all x1, blocking collectives, sum_terms(): lax.all_to_all(mine, 'vocab', 0, 0, axis_index_groups=core_groups(n_v))  19.6 us
    ppermute x6, waiting for transfers between devices, ring_blocks(): down, up = (lax.ppermute(down, 'dp', left), lax.ppermute(up, 'dp', right))  15.6 us
    all_to_all x1, starting transfers between devices, body(): lax.all_to_all(teacher_logprobs, 'vocab', split_axis=1, concat_axis=0, ti...  13.3 us
    all_to_all x2, starting transfers between devices, spread(): return lax.all_to_all(copies, axis, 0, 0, axis_index_groups=groups)  12.8 us
    dot_general x8, matrix products, body(): term = jnp.dot(feats, pieces[k], preferred_element_type=jnp.float32)  10.4 us
    all_to_all x2, waiting for transfers between devices, spread(): return lax.all_to_all(copies, axis, 0, 0, axis_index_groups=groups)  9.63 us
  transfers between devices with their start and end apart: 16, of which 11 were waited for; matrix products, arithmetic and copies ran while one was open for 12% of the time, Pallas kernels for 4%

profile of v8, /device:TPU:1, one launch (start us, length us, event | category | flops | bytes accessed | tf_op | source)
XLA Modules:
  0.0 223.3 jit_solution(13996683040996236172)
XLA Ops:
  7.2 2.2 slice.15
  9.5 1.0 slice.16.refs_0_
  10.5 4.8 %collective-permute-start.2 = (bf16[160,1280]{1,0:T(8,128)(2,1)S(1)}, bf16[160,1280]{1,0:T(8,128)(2,1)}, u32[]{:S(2)}, u32[]{:S(2)}) collective-permute-start(bf16[160,1280]{1,0:T(8,128)(2,1)S(1)} %slice.16.refs_0_), channel_id=1, source_target_pairs={{0,64},{64,128},{128,192},{192,256},{256,320},{320,384},{384,448},... | collective-permute-start | bytes 1228808 | tf_op jit(solution)/shard_map/ppermute | solution.py:41
  15.4 8.6 %collective-permute-start = (bf16[160,1280]{1,0:T(8,128)(2,1)S(1)}, bf16[160,1280]{1,0:T(8,128)(2,1)}, u32[]{:S(2)}, u32[]{:S(2)}) collective-permute-start(bf16[160,1280]{1,0:T(8,128)(2,1)S(1)} %slice.16.refs_0_), channel_id=1, source_target_pairs={{0,448},{64,0},{128,64},{192,128},{256,192},{320,256},{384,320},{4... | collective-permute-start | bytes 1228808 | tf_op jit(solution)/shard_map/ppermute | solution.py:41
  24.6 3.9 %all-to-all-start = ((bf16[8,2,512]{2,1,0:T(2,128)(2,1)}), bf16[8,2,512]{2,1,0:T(2,128)(2,1)S(1)}, u32[]{:S(2)}, u32[]{:S(2)}) async-start(bf16[8,2,512]{2,1,0:T(2,128)(2,1)} %bitcast.3), calls=%async_computation | async-start | bytes 32768 | tf_op jit(solution)/shard_map/all_to_all | solution.py:199
  28.5 6.7 %all-to-all-done = bf16[8,2,512]{2,1,0:T(2,128)(2,1)S(1)} async-done(((bf16[8,2,512]{2,1,0:T(2,128)(2,1)}), bf16[8,2,512]{2,1,0:T(2,128)(2,1)S(1)}, u32[]{:S(2)}, u32[]{:S(2)}) %all-to-all-start) | async-done | bytes 16416 | tf_op jit(solution)/shard_map/all_to_all | solution.py:199
  35.2 13.3 %all-to-all-start.2 = ((bf16[2,64,1280]{2,0,1:T(2,128)(2,1)}), bf16[2,64,1280]{2,0,1:T(2,128)(2,1)S(1)}, u32[]{:S(2)}, u32[]{:S(2)}) async-start(bf16[2,64,1280]{2,0,1:T(2,128)(2,1)} %bitcast.4), calls=%async_computation.2 | async-start | bytes 655360 | tf_op jit(solution)/shard_map/all_to_all | solution.py:197
  49.9 0.8 select_reduce_fusion.1
  50.7 1.9 collective-permute-start.3
  52.6 5.2 %collective-permute-start.1 = (bf16[160,1280]{1,0:T(8,128)(2,1)}, bf16[160,1280]{1,0:T(8,128)(2,1)}, u32[]{:S(2)}, u32[]{:S(2)}) collective-permute-start(bf16[160,1280]{1,0:T(8,128)(2,1)} %collective-permute-done.refs_1_), channel_id=1, source_target_pairs={{0,448},{64,0},{128,64},{192,128},{256,192},{320,256},{384,320},{4... | collective-permute-start | bytes 1228808 | tf_op jit(solution)/shard_map/ppermute | solution.py:41
  58.5 1.3 fusion.15
  59.9 2.8 %all-to-all-done.2 = bf16[2,64,1280]{2,0,1:T(2,128)(2,1)S(1)} async-done(((bf16[2,64,1280]{2,0,1:T(2,128)(2,1)}), bf16[2,64,1280]{2,0,1:T(2,128)(2,1)S(1)}, u32[]{:S(2)}, u32[]{:S(2)}) %all-to-all-start.2) | async-done | bytes 327712 | tf_op jit(solution)/shard_map/all_to_all | solution.py:197
  62.7 2.7 %broadcast_in_dim.44 = bf16[64,8,2,512]{3,2,1,0:T(2,128)(2,1)} broadcast(bf16[8,2,512]{2,1,0:T(2,128)(2,1)} %copy-done.5), dimensions={1,2,3} | broadcast | bytes 1064960 | tf_op jit(solution)/shard_map/broadcast_in_dim | solution.py:21
  65.4 7.8 %all-to-all-start.1 = ((bf16[64,8,2,512]{3,2,1,0:T(2,128)(2,1)}), bf16[64,8,2,512]{3,2,1,0:T(2,128)(2,1)S(1)}, u32[]{:S(2)}, u32[]{:S(2)}) async-start(bf16[64,8,2,512]{3,2,1,0:T(2,128)(2,1)} %broadcast_in_dim.44), calls=%async_computation.1 | async-start | bytes 2097152 | tf_op jit(solution)/shard_map/all_to_all | solution.py:22
  73.4 1.4 collective-permute-done.3.refs_6_
  74.8 1.1 collective-permute-done.1.refs_2_
  75.9 5.3 %collective-permute-start.4 = (bf16[160,1280]{1,0:T(8,128)(2,1)}, bf16[160,1280]{1,0:T(8,128)(2,1)S(1)}, u32[]{:S(2)}, u32[]{:S(2)}) collective-permute-start(bf16[160,1280]{1,0:T(8,128)(2,1)} %collective-permute-done.1.refs_2_), channel_id=1, source_target_pairs={{0,448},{64,0},{128,64},{192,128},{256,192},{320,256},{384,320},{4... | collective-permute-start | bytes 1228808 | tf_op jit(solution)/shard_map/ppermute | solution.py:41
  81.2 1.9 collective-permute-start.6
  83.2 1.4 convolution_add_fusion.2
  84.5 1.3 fusion.4
  85.9 13.1 %collective-permute-done.4.refs_3_ = bf16[160,1280]{1,0:T(8,128)(2,1)S(1)} collective-permute-done((bf16[160,1280]{1,0:T(8,128)(2,1)}, bf16[160,1280]{1,0:T(8,128)(2,1)S(1)}, u32[]{:S(2)}, u32[]{:S(2)}) %collective-permute-start.4) | collective-permute-done | bytes 409632 | tf_op jit(solution)/shard_map/ppermute | solution.py:41
  99.0 5.3 %collective-permute-start.5 = (bf16[80,1280]{1,0:T(8,128)(2,1)S(1)}, bf16[80,1280]{1,0:T(8,128)(2,1)S(1)}, u32[]{:S(2)}, u32[]{:S(2)}) collective-permute-start(bf16[80,1280]{1,0:T(8,128)(2,1)S(1)} %slice.20), channel_id=1, source_target_pairs={{0,448},{64,0},{128,64},{192,128},{256,192},{320,256},{384,320},{4... | collective-permute-start | bytes 614408 | tf_op jit(solution)/shard_map/ppermute | solution.py:44
  104.4 1.9 collective-permute-start.7
  106.3 1.2 fusion.7
  107.5 1.2 fusion.11
  108.7 4.0 %collective-permute-done.5 = bf16[80,1280]{1,0:T(8,128)(2,1)S(1)} collective-permute-done((bf16[80,1280]{1,0:T(8,128)(2,1)S(1)}, bf16[80,1280]{1,0:T(8,128)(2,1)S(1)}, u32[]{:S(2)}, u32[]{:S(2)}) %collective-permute-start.5) | collective-permute-done | bytes 204832 | tf_op jit(solution)/shard_map/ppermute | solution.py:44
  112.7 5.4 %collective-permute-done.7 = bf16[80,1280]{1,0:T(8,128)(2,1)S(1)} collective-permute-done((bf16[80,1280]{1,0:T(8,128)(2,1)S(1)}, bf16[80,1280]{1,0:T(8,128)(2,1)S(1)}, u32[]{:S(2)}, u32[]{:S(2)}) %collective-permute-start.7) | collective-permute-done | bytes 204832 | tf_op jit(solution)/shard_map/ppermute | solution.py:44
  118.1 0.8 copy-done.2
  118.9 1.2 fusion.9
  120.1 1.4 fusion.3
  121.5 1.4 fusion
  122.8 1.9 all-gather.3.cloned.1.call-done.gathered_ref
  124.8 4.2 %fusion.26 = f32[128,1280]{1,0:T(8,128)S(1)} fusion(bf16[128,2816]{0,1:T(8,128)(2,1)S(1)} %bitcast.29, bf16[2816,1280]{1,0:T(8,128)(2,1)} %all-gather.3.cloned.1.call-done.gathered_ref), kind=kOutput, calls=%fused_computation.44 | convolution fusion | flops 922746880 | bytes 8585216 | tf_op jit(solution)/shard_map/dot_general | solution.py:222
  129.5 22.0 %all_to_all.44.every_ref = f32[64,3,128]{2,1,0:T(4,128)S(1)} all-to-all(f32[64,3,128]{2,1,0:T(4,128)S(1)} %shard_map.68), channel_id=1, replica_groups=mesh['dp'=8,'vocab'=64] {'vocab'}, dimensions={0} | all-to-all | bytes 196608 | tf_op jit(solution)/shard_map/all_to_all | solution.py:224
  151.5 1.1 shard_map.69.grads_ref
  153.3 8.3 %shard_map.70 = (f32[4,128,512]{2,1,0:T(8,128)}, f32[4,128,512]{2,1,0:T(8,128)}) custom-call(s32[2]{0:T(128)} %pad_add_fusion.place_ref, bf16[128,1280]{1,0:T(8,128)(2,1)} %shard_map.69.grads_ref, bf16[2816,1280]{1,0:T(8,128)(2,1)} %all-gather.3.cloned.1.call-done.gathered_ref, bf16[160,1280]{1,0:T(8,128)(2,1)} %copy-done.4, ...), custom_call_target="tpu_custom_call" | custom-call | flops 1342177280 | bytes 12582912 | tf_op jit(solution)/shard_map/pallas_call | solution.py:131
  161.5 2.3 %collective-permute-start.8 = (f32[4,128,512]{2,1,0:T(8,128)}, f32[4,128,512]{2,1,0:T(8,128)S(1)}, u32[]{:S(2)}, u32[]{:S(2)}) collective-permute-start(f32[4,128,512]{2,1,0:T(8,128)} %get-tuple-element.28), channel_id=1, source_target_pairs={{0,1},{1,0},{2,3},{3,2},{4,5},{5,4},{6,7},{7,6},{8,9},{9,8},{10,11... | collective-permute-start | bytes 3145736 | tf_op jit(solution)/shard_map/ppermute | solution.py:183
  163.9 2.5 %collective-permute-done.8 = f32[4,128,512]{2,1,0:T(8,128)S(1)} collective-permute-done((f32[4,128,512]{2,1,0:T(8,128)}, f32[4,128,512]{2,1,0:T(8,128)S(1)}, u32[]{:S(2)}, u32[]{:S(2)}) %collective-permute-start.8) | collective-permute-done | bytes 1048608 | tf_op jit(solution)/shard_map/ppermute | solution.py:183
  166.3 1.4 add_convert_fusion
  167.7 19.6 %all_to_all.45 = bf16[32,16,512]{2,1,0:T(8,128)(2,1)S(1)} all-to-all(bf16[32,16,512]{2,1,0:T(8,128)(2,1)S(1)} %bitcast.32), channel_id=1, replica_groups={{0,2,4,6,8,10,12,14,16,18,20,22,24,26,28,30,32,34,36,38,40,42,44,46,48,..., dimensions={0} | all-to-all | bytes 1048576 | tf_op jit(solution)/shard_map/all_to_all | solution.py:185
  187.4 0.9 broadcast_in_dim.50
  188.2 5.0 %all-to-all-start.5 = ((bf16[32,16,512]{2,1,0:T(8,128)(2,1)}), bf16[32,16,512]{2,1,0:T(8,128)(2,1)S(1)}, u32[]{:S(2)}, u32[]{:S(2)}) async-start(bf16[32,16,512]{2,1,0:T(8,128)(2,1)} %broadcast_in_dim.50), calls=%async_computation.5 | async-start | bytes 1048576 | tf_op jit(solution)/shard_map/all_to_all | solution.py:22
  193.2 0.7 copy.15
  194.4 4.4 %convolution_convert_fusion = bf16[512,1280]{1,0:T(8,128)(2,1)} fusion(bf16[1024,512]{1,0:T(8,128)(2,1)S(1)} %reshape.87, bf16[1024,1280]{1,0:T(8,128)(2,1)} %all-gather.5.cloned.1.call-done), kind=kOutput, calls=%fused_computation | convolution fusion | flops 1342832640 | bytes 4980736 | tf_op jit(solution)/shard_map/dot_general | solution.py:235
  198.8 9.6 %all-to-all-done.5 = bf16[32,16,512]{2,1,0:T(8,128)(2,1)S(1)} async-done(((bf16[32,16,512]{2,1,0:T(8,128)(2,1)}), bf16[32,16,512]{2,1,0:T(8,128)(2,1)S(1)}, u32[]{:S(2)}, u32[]{:S(2)}) %all-to-all-start.5) | async-done | bytes 524320 | tf_op jit(solution)/shard_map/all_to_all | solution.py:22
  208.4 5.5 %collective-permute-start.9 = (bf16[4,128,512]{2,1,0:T(8,128)(2,1)S(1)}, bf16[4,128,512]{2,1,0:T(8,128)(2,1)S(1)}, u32[]{:S(2)}, u32[]{:S(2)}) collective-permute-start(bf16[4,128,512]{2,1,0:T(8,128)(2,1)S(1)} %bitcast.27), channel_id=1, source_target_pairs={{0,1},{1,0},{2,3},{3,2},{4,5},{5,4},{6,7},{7,6},{8,9},{9,8},{10,11... | collective-permute-start | bytes 1572872 | tf_op jit(solution)/shard_map/ppermute | solution.py:240
  214.0 1.5 collective-permute-done.9.got_ref
  215.5 1.0 shard_map.71
  (40 shorter events, 4.6 us)
Async XLA Ops:
  7.2 16.8 %copy-start.3 = (bf16[128,4096]{1,0:T(8,128)(2,1)S(1)}, bf16[128,4096]{1,0:T(8,128)(2,1)}, u32[]{:S(2)}) copy-start(bf16[128,4096]{1,0:T(8,128)(2,1)} %param.5) | copy-start | bytes 3145732
  7.2 41.3 %copy-start.6 = (f32[2]{0:T(128)S(1)}, f32[2]{0:T(128)}, u32[]{:S(2)}) copy-start(f32[2]{0:T(128)} %param.9) | copy-start | bytes 28
  7.2 117.6 %all-gather.3.cloned.1.call-start = ((), (), s32[]{:S(2)}) async-start(), calls=%async_computation.6 | async-start | bytes 8110080 | tf_op jit(solution)/shard_map/all_gather | solution.py:196
  10.5 49.4 %copy-start.4 = (bf16[160,1280]{1,0:T(8,128)(2,1)}, bf16[160,1280]{1,0:T(8,128)(2,1)S(1)}, u32[]{:S(2)}) copy-start(bf16[160,1280]{1,0:T(8,128)(2,1)S(1)} %slice.16.refs_0_) | copy-start | bytes 1228804
  10.5 40.2 %collective-permute-start.2 = (bf16[160,1280]{1,0:T(8,128)(2,1)S(1)}, bf16[160,1280]{1,0:T(8,128)(2,1)}, u32[]{:S(2)}, u32[]{:S(2)}) collective-permute-start(bf16[160,1280]{1,0:T(8,128)(2,1)S(1)} %slice.16.refs_0_), channel_id=1, source_target_pairs={{0,64},{64,128},{128,192},{192,256},{256,320},{320,384},{384,448},... | collective-permute-start | bytes 1228808 | tf_op jit(solution)/shard_map/ppermute | solution.py:41
  15.4 37.3 %collective-permute-start = (bf16[160,1280]{1,0:T(8,128)(2,1)S(1)}, bf16[160,1280]{1,0:T(8,128)(2,1)}, u32[]{:S(2)}, u32[]{:S(2)}) collective-permute-start(bf16[160,1280]{1,0:T(8,128)(2,1)S(1)} %slice.16.refs_0_), channel_id=1, source_target_pairs={{0,448},{64,0},{128,64},{192,128},{256,192},{320,256},{384,320},{4... | collective-permute-start | bytes 1228808 | tf_op jit(solution)/shard_map/ppermute | solution.py:41
  24.6 10.6 %all-to-all-start = ((bf16[8,2,512]{2,1,0:T(2,128)(2,1)}), bf16[8,2,512]{2,1,0:T(2,128)(2,1)S(1)}, u32[]{:S(2)}, u32[]{:S(2)}) async-start(bf16[8,2,512]{2,1,0:T(2,128)(2,1)} %bitcast.3), calls=%async_computation | async-start | bytes 32768 | tf_op jit(solution)/shard_map/all_to_all | solution.py:199
  28.5 21.3 %copy-start.7 = (s32[128]{0:T(128)}, s32[128]{0:T(128)S(1)}, u32[]{:S(2)}) copy-start(s32[128]{0:T(128)S(1)} %and_select_fusion) | copy-start | bytes 1540
  35.2 14.6 %copy-start.5 = (bf16[8,2,512]{2,1,0:T(2,128)(2,1)}, bf16[8,2,512]{2,1,0:T(2,128)(2,1)S(1)}, u32[]{:S(2)}) copy-start(bf16[8,2,512]{2,1,0:T(2,128)(2,1)S(1)} %all-to-all-done) | copy-start | bytes 49156
  35.2 27.4 %all-to-all-start.2 = ((bf16[2,64,1280]{2,0,1:T(2,128)(2,1)}), bf16[2,64,1280]{2,0,1:T(2,128)(2,1)S(1)}, u32[]{:S(2)}, u32[]{:S(2)}) async-start(bf16[2,64,1280]{2,0,1:T(2,128)(2,1)} %bitcast.4), calls=%async_computation.2 | async-start | bytes 655360 | tf_op jit(solution)/shard_map/all_to_all | solution.py:197
  50.7 24.1 %collective-permute-start.3 = (bf16[160,1280]{1,0:T(8,128)(2,1)}, bf16[160,1280]{1,0:T(8,128)(2,1)}, u32[]{:S(2)}, u32[]{:S(2)}) collective-permute-start(bf16[160,1280]{1,0:T(8,128)(2,1)} %collective-permute-done.2.refs_7_), channel_id=1, source_target_pairs={{0,64},{64,128},{128,192},{192,256},{256,320},{320,384},{384,448},... | collective-permute-start | bytes 1228808 | tf_op jit(solution)/shard_map/ppermute | solution.py:41
  52.6 23.3 %collective-permute-start.1 = (bf16[160,1280]{1,0:T(8,128)(2,1)}, bf16[160,1280]{1,0:T(8,128)(2,1)}, u32[]{:S(2)}, u32[]{:S(2)}) collective-permute-start(bf16[160,1280]{1,0:T(8,128)(2,1)} %collective-permute-done.refs_1_), channel_id=1, source_target_pairs={{0,448},{64,0},{128,64},{192,128},{256,192},{320,256},{384,320},{4... | collective-permute-start | bytes 1228808 | tf_op jit(solution)/shard_map/ppermute | solution.py:41
  65.4 57.5 %all-to-all-start.1 = ((bf16[64,8,2,512]{3,2,1,0:T(2,128)(2,1)}), bf16[64,8,2,512]{3,2,1,0:T(2,128)(2,1)S(1)}, u32[]{:S(2)}, u32[]{:S(2)}) async-start(bf16[64,8,2,512]{3,2,1,0:T(2,128)(2,1)} %broadcast_in_dim.44), calls=%async_computation.1 | async-start | bytes 2097152 | tf_op jit(solution)/shard_map/all_to_all | solution.py:22
  73.2 121.2 %all-gather.5.cloned.1.call-start = ((), (), s32[]{:S(2)}) async-start(), calls=%async_computation.7 | async-start | bytes 2949120 | tf_op jit(solution)/shard_map/all_gather | solution.py:231
  75.9 23.1 %collective-permute-start.4 = (bf16[160,1280]{1,0:T(8,128)(2,1)}, bf16[160,1280]{1,0:T(8,128)(2,1)S(1)}, u32[]{:S(2)}, u32[]{:S(2)}) collective-permute-start(bf16[160,1280]{1,0:T(8,128)(2,1)} %collective-permute-done.1.refs_2_), channel_id=1, source_target_pairs={{0,448},{64,0},{128,64},{192,128},{256,192},{320,256},{384,320},{4... | collective-permute-start | bytes 1228808 | tf_op jit(solution)/shard_map/ppermute | solution.py:41
  81.2 23.1 %collective-permute-start.6 = (bf16[160,1280]{1,0:T(8,128)(2,1)}, bf16[160,1280]{1,0:T(8,128)(2,1)S(1)}, u32[]{:S(2)}, u32[]{:S(2)}) collective-permute-start(bf16[160,1280]{1,0:T(8,128)(2,1)} %collective-permute-done.3.refs_6_), channel_id=1, source_target_pairs={{0,64},{64,128},{128,192},{192,256},{256,320},{320,384},{384,448},... | collective-permute-start | bytes 1228808 | tf_op jit(solution)/shard_map/ppermute | solution.py:41
  99.0 22.5 %copy-start = (bf16[160,1280]{1,0:T(8,128)(2,1)}, bf16[160,1280]{1,0:T(8,128)(2,1)S(1)}, u32[]{:S(2)}) copy-start(bf16[160,1280]{1,0:T(8,128)(2,1)S(1)} %collective-permute-done.4.refs_3_) | copy-start | bytes 1228804
  99.0 13.7 %collective-permute-start.5 = (bf16[80,1280]{1,0:T(8,128)(2,1)S(1)}, bf16[80,1280]{1,0:T(8,128)(2,1)S(1)}, u32[]{:S(2)}, u32[]{:S(2)}) collective-permute-start(bf16[80,1280]{1,0:T(8,128)(2,1)S(1)} %slice.20), channel_id=1, source_target_pairs={{0,448},{64,0},{128,64},{192,128},{256,192},{320,256},{384,320},{4... | collective-permute-start | bytes 614408 | tf_op jit(solution)/shard_map/ppermute | solution.py:44
  104.3 13.8 %copy-start.1 = (bf16[160,1280]{1,0:T(8,128)(2,1)}, bf16[160,1280]{1,0:T(8,128)(2,1)S(1)}, u32[]{:S(2)}) copy-start(bf16[160,1280]{1,0:T(8,128)(2,1)S(1)} %collective-permute-done.6.refs_5_) | copy-start | bytes 1228804
  104.4 13.7 %collective-permute-start.7 = (bf16[80,1280]{1,0:T(8,128)(2,1)S(1)}, bf16[80,1280]{1,0:T(8,128)(2,1)S(1)}, u32[]{:S(2)}, u32[]{:S(2)}) collective-permute-start(bf16[80,1280]{1,0:T(8,128)(2,1)S(1)} %slice.21), channel_id=1, source_target_pairs={{0,64},{64,128},{128,192},{192,256},{256,320},{320,384},{384,448},... | collective-permute-start | bytes 614408 | tf_op jit(solution)/shard_map/ppermute | solution.py:44
  118.1 0.8 copy-start.2
  161.5 4.8 %collective-permute-start.8 = (f32[4,128,512]{2,1,0:T(8,128)}, f32[4,128,512]{2,1,0:T(8,128)S(1)}, u32[]{:S(2)}, u32[]{:S(2)}) collective-permute-start(f32[4,128,512]{2,1,0:T(8,128)} %get-tuple-element.28), channel_id=1, source_target_pairs={{0,1},{1,0},{2,3},{3,2},{4,5},{5,4},{6,7},{7,6},{8,9},{9,8},{10,11... | collective-permute-start | bytes 3145736 | tf_op jit(solution)/shard_map/ppermute | solution.py:183
  188.2 20.2 %all-to-all-start.5 = ((bf16[32,16,512]{2,1,0:T(8,128)(2,1)}), bf16[32,16,512]{2,1,0:T(8,128)(2,1)S(1)}, u32[]{:S(2)}, u32[]{:S(2)}) async-start(bf16[32,16,512]{2,1,0:T(8,128)(2,1)} %broadcast_in_dim.50), calls=%async_computation.5 | async-start | bytes 1048576 | tf_op jit(solution)/shard_map/all_to_all | solution.py:22
  208.4 7.0 %collective-permute-start.9 = (bf16[4,128,512]{2,1,0:T(8,128)(2,1)S(1)}, bf16[4,128,512]{2,1,0:T(8,128)(2,1)S(1)}, u32[]{:S(2)}, u32[]{:S(2)}) collective-permute-start(bf16[4,128,512]{2,1,0:T(8,128)(2,1)S(1)} %bitcast.27), channel_id=1, source_target_pairs={{0,1},{1,0},{2,3},{3,2},{4,5},{5,4},{6,7},{7,6},{8,9},{9,8},{10,11... | collective-permute-start | bytes 1572872 | tf_op jit(solution)/shard_map/ppermute | solution.py:240
Sparse Core Ops, SparseCore 0:
  10.7 114.0 all-gather.2
  152.7 34.9 all-gather.4
